TPU v7x, 32 devices: a whole 2x2x4 slice. The times are simulated.
32 devices in a mesh: pb: 8 (over z, y), row: 4 (over x, core).
Axes of the slice: x: 2, y: 2, z: 4, core: 2. Of those that a mesh axis runs over, the one named last changes fastest.
Arguments:
- orbitals: bfloat16 [8, 1280, 128], P('pb', 'row'), may hold values from -4 to 4
- interaction: bfloat16 [2, 8, 1280, 1280], P(None, 'pb', 'row'), may hold values from -0.078125 to 0.078125
- pair_list: int32 [8, 3, 2], P('pb'), may hold values from 0 to 7, as said below
- flag_list: int32 [8, 3], P('pb'), may hold values from 0 to 1
- pair_counts: int32 [8], P('pb'), may hold values from 1 to 3, as said below
Outputs:
- exchange_terms: float32 [8, 3, 1280, 128], P('pb', None, 'row')
Inputs may be any that keep to these rules, and one draw needn't show every extreme that they name: pair_list[q, s, 1] = (pair_list[q, s, 0] - q) mod 8. `pair_counts`: some q has all 3 slots live.
All inputs are finite; a program needn't handle non-finite values.
Results may differ from a plain program's by a relative error of at most 0.0029.
Values may be sent and summed in bfloat16 or wider, within the bound.
No kernel may reach another device: no remote copies, remote signals or barrier semaphores. Data moves between devices by JAX's collectives and lax.ppermute only.
A program may use at most 64 MiB of HBM per device.

v0:
```python
import jax
import jax.numpy as jnp
from jax import lax
from jax.sharding import PartitionSpec as P


def rotate_parts(block):
    half_width = block.shape[1] // 2
    return jnp.concatenate([block[:, half_width:], -block[:, :half_width]], axis=1)


def apply_kernel(kern_real, kern_imag, target):
    half_width = target.shape[1] // 2
    prod_real = jnp.dot(kern_real, target, preferred_element_type=jnp.float32)
    prod_imag = jnp.dot(kern_imag, target, preferred_element_type=jnp.float32)
    return jnp.concatenate(
        [
            prod_real[:, :half_width] - prod_imag[:, half_width:],
            prod_real[:, half_width:] + prod_imag[:, :half_width],
        ],
        axis=1,
    )


def density(local_rows, all_rows):
    dens_real = jnp.dot(local_rows, all_rows.T, preferred_element_type=jnp.float32)
    dens_imag = jnp.dot(rotate_parts(local_rows), all_rows.T, preferred_element_type=jnp.float32)
    return (dens_real, dens_imag)


def shards(orbitals, interaction, pair_list, flag_list, pair_counts):
    slot_total = pair_list.shape[1]
    wanted = jnp.stack([pair_list[0, :, 0], pair_list[0, :, 1]])
    shard_piece = lax.all_gather(orbitals, "pb", axis=0, tiled=True)
    indices = jnp.arange(shard_piece.shape[0], dtype=jnp.int32)
    select = (wanted[:, :, None] == indices[None, None, :]).astype(jnp.bfloat16)
    chosen = jnp.einsum(
        "spi,ird->sprd", select, shard_piece, preferred_element_type=jnp.float32
    ).astype(jnp.bfloat16)
    all_rows = lax.all_gather(chosen, "row", axis=2, tiled=True)
    w_real = interaction[0, 0]
    w_imag = interaction[1, 0]
    active = jnp.arange(slot_total) < pair_counts[0]
    adjoint = flag_list[0] == 1
    turned = lax.all_to_all(interaction[:, 0], "row", split_axis=2, concat_axis=1, tiled=True)
    turned = jnp.swapaxes(turned, 1, 2)
    results = []
    for slot_index in range(slot_total):
        dens_real, dens_imag = density(chosen[1, slot_index], all_rows[1, slot_index])
        eff_real = jnp.where(adjoint[slot_index], turned[0], w_real)
        eff_imag = jnp.where(adjoint[slot_index], -turned[1], w_imag)
        kern_real = (eff_real * dens_real - eff_imag * dens_imag).astype(jnp.bfloat16)
        kern_imag = (eff_real * dens_imag + eff_imag * dens_real).astype(jnp.bfloat16)
        keep_slot = active[slot_index].astype(jnp.float32)
        results.append(apply_kernel(kern_real, kern_imag, all_rows[0, slot_index]) * keep_slot)
    output = jnp.stack(results)
    return output[None]


def solution(mesh):
    return jax.shard_map(
        shards,
        mesh=mesh,
        in_specs=(
            P("pb", "row", None),
            P(None, "pb", "row", None),
            P("pb", None, None),
            P("pb", None),
            P("pb"),
        ),
        out_specs=P("pb", None, "row", None),
        check_vma=False,
    )
```

profile of v0, /device:TPU:0, one launch (start us, length us, event | category | flops | bytes accessed | tf_op | source)
XLA Modules:
  0.0 123.3 jit_solution(14033997229826708994)
XLA Ops:
  6.5 33.7 %all_gather.6 = bf16[8,320,128]{2,1,0:T(8,128)(2,1)S(1)} all-gather(bf16[1,320,128]{2,1,0:T(8,128)(2,1)} %param.5), channel_id=1, replica_groups=mesh['pb'=8,'row'=4] {'pb'}, dimensions={0}, use_global_device_ids=true | all-gather | bytes 737280 | tf_op jit(solution)/shard_map/all_gather | solution.py:34
  40.2 0.8 slice_bitcast_fusion.2
  41.0 1.4 %convolution_convert_fusion = bf16[2,3,320,128]{3,1,2,0:T(4,128)(2,1)} fusion(bf16[8,320,128]{2,1,0:T(8,128)(2,1)S(1)} %all_gather.6, s32[2,3]{1,0:T(2,128)S(1)} %pad_add_fusion), kind=kOutput, calls=%fused_computation.25 | convolution fusion | flops 4177968 | bytes 1146904 | tf_op jit(solution)/shard_map/spi,ird->sprd/dot_general | solution.py:37
  42.5 5.2 %copy.10 = bf16[2,1,320,1280]{2,0,3,1:T(2,128)(2,1)} copy(bf16[2,1,320,1280]{3,2,1,0:T(8,128)(2,1)S(1)} %copy-done.2) | data formatting | bytes 3276800 | tf_op args[1]
  47.7 3.8 %all-to-all-start = ((bf16[2,320,1280]{1,0,2:T(2,128)(2,1)}), bf16[2,320,1280]{1,0,2:T(2,128)(2,1)S(1)}, u32[]{:S(2)}, u32[]{:S(2)}) async-start(bf16[2,320,1280]{1,0,2:T(2,128)(2,1)} %bitcast.1), calls=%async_computation | async-start | bytes 3932160 | tf_op jit(solution)/shard_map/all_to_all | solution.py:45
  52.1 0.7 fusion.83
  54.1 0.3 fusion.79
  55.1 0.7 fusion.84
  56.1 32.7 %all-to-all-done = bf16[2,320,1280]{1,0,2:T(2,128)(2,1)S(1)} async-done(((bf16[2,320,1280]{1,0,2:T(2,128)(2,1)}), bf16[2,320,1280]{1,0,2:T(2,128)(2,1)S(1)}, u32[]{:S(2)}, u32[]{:S(2)}) %all-to-all-start) | async-done | bytes 1638432 | tf_op jit(solution)/shard_map/all_to_all | solution.py:45
  88.8 1.3 %copy-done = bf16[2,320,1280]{1,0,2:T(2,128)(2,1)} copy-done((bf16[2,320,1280]{1,0,2:T(2,128)(2,1)}, bf16[2,320,1280]{1,0,2:T(2,128)(2,1)S(1)}, u32[]{:S(2)}) %copy-start) | copy-done | bytes 1638424
  90.1 3.1 %copy.79 = bf16[2,320,4,320]{1,2,3,0:T(4,128)(2,1)S(1)} copy(bf16[2,320,4,320]{1,0,3,2:T(2,128)(2,1)} %bitcast.179) | data formatting | bytes 3276800 | tf_op jit(solution)/shard_map/all_to_all | solution.py:45
  93.1 2.4 %all_to_all.16 = bf16[2,1280,320]{1,2,0:T(8,128)(2,1)} reshape(bf16[2,4,320,320]{2,1,3,0:T(4,128)(2,1)S(1)} %bitcast.178) | data formatting | bytes 3276800 | tf_op jit(solution)/shard_map/all_to_all | solution.py:45
  95.6 7.1 %fusion.78 = (bf16[1,1,1280,128]{3,1,2,0:T(2,128)(2,1)S(1)}, bf16[1,1,1280,128]{3,1,2,0:T(2,128)(2,1)S(1)}, bf16[1,1,1280,128]{3,1,2,0:T(2,128)(2,1)S(1)}, bf16[...) fusion(bf16[2,3,1280,128]{3,1,2,0:T(4,128)(2,1)} %all-gather.2.clo, ...), kind=kLoop, calls=%fused_computation.115 | loop fusion | bytes 3932160 | tf_op jit(solution)/shard_map/slice | solution.py:55
  102.7 0.4 fusion.31
  103.1 0.4 fusion.29
  103.5 0.6 copy-done.3
  104.1 0.5 copy-done.4
  104.6 1.5 %fusion.12 = f32[320,128]{1,0:T(8,128)S(1)} fusion(f32[320,1280]{1,0:T(8,128)S(1)} %fusion.29, f32[320,1280]{1,0:T(8,128)S(1)} %fusion.31, bf16[1,1,1280,128]{3,1,2,0:T(2,128)(2,1)S(1)} %get-tuple-element.6, pred[]{:T(512)} %bitcast.22, bf16[2,320,1280]{2,1,0:T(8,128)(2,1)S(1)} %bitcast.180, bf16[2,1,320,1280]{3,2,1,0:T(8,128)(2,1)S(1)} %copy-done.3), kind=kOutput, calls=%fused_computation.26 | convolution fusion | flops 108544000 | bytes 7045121 | tf_op jit(solution)/shard_map/dot_general | solution.py:15
  106.1 1.5 %fusion.14 = f32[320,128]{1,0:T(8,128)S(1)} fusion(f32[320,1280]{1,0:T(8,128)S(1)} %fusion.31, f32[320,1280]{1,0:T(8,128)S(1)} %fusion.29, bf16[1,1,1280,128]{3,1,2,0:T(2,128)(2,1)S(1)} %get-tuple-element.6, pred[]{:T(512)} %bitcast.22, bf16[2,320,1280]{2,1,0:T(8,128)(2,1)S(1)} %bitcast.181, bf16[2,1,320,1280]{3,2,1,0:T(8,128)(2,1)S(1)} %copy-done.3), kind=kOutput, calls=%fused_computation.27 | convolution fusion | flops 108544000 | bytes 7045121 | tf_op jit(solution)/shard_map/dot_general | solution.py:14
  107.6 0.4 fusion.37
  108.0 0.4 fusion.35
  108.4 1.4 %fusion.16 = f32[320,128]{1,0:T(8,128)S(1)} fusion(f32[320,1280]{1,0:T(8,128)S(1)} %fusion.35, f32[320,1280]{1,0:T(8,128)S(1)} %fusion.37, bf16[1,1,1280,128]{3,1,2,0:T(2,128)(2,1)S(1)} %get-tuple-element.8, pred[]{:T(512)} %bitcast.18, bf16[2,320,1280]{2,1,0:T(8,128)(2,1)S(1)} %bitcast.182, bf16[2,1,320,1280]{3,2,1,0:T(8,128)(2,1)S(1)} %copy-done.3), kind=kOutput, calls=%fused_computation.28 | convolution fusion | flops 108544000 | bytes 7045121 | tf_op jit(solution)/shard_map/dot_general | solution.py:15
  109.8 1.4 %fusion.18 = f32[320,128]{1,0:T(8,128)S(1)} fusion(f32[320,1280]{1,0:T(8,128)S(1)} %fusion.37, f32[320,1280]{1,0:T(8,128)S(1)} %fusion.35, bf16[1,1,1280,128]{3,1,2,0:T(2,128)(2,1)S(1)} %get-tuple-element.8, pred[]{:T(512)} %bitcast.18, bf16[2,320,1280]{2,1,0:T(8,128)(2,1)S(1)} %bitcast.183, bf16[2,1,320,1280]{3,2,1,0:T(8,128)(2,1)S(1)} %copy-done.3), kind=kOutput, calls=%fused_computation.29 | convolution fusion | flops 108544000 | bytes 7045121 | tf_op jit(solution)/shard_map/dot_general | solution.py:14
  111.1 0.4 fusion.43
  111.5 0.4 fusion.41
  112.0 1.4 %fusion.20 = f32[320,128]{1,0:T(8,128)S(1)} fusion(f32[320,1280]{1,0:T(8,128)S(1)} %fusion.41, f32[320,1280]{1,0:T(8,128)S(1)} %fusion.43, bf16[1,1,1280,128]{3,1,2,0:T(2,128)(2,1)S(1)} %get-tuple-element.5, pred[]{:T(512)} %bitcast, bf16[2,320,1280]{2,1,0:T(8,128)(2,1)S(1)} %bitcast.184, bf16[2,1,320,1280]{3,2,1,0:T(8,128)(2,1)S(1)} %copy-done.3), kind=kOutput, calls=%fused_computation.30 | convolution fusion | flops 108544000 | bytes 7045121 | tf_op jit(solution)/shard_map/dot_general | solution.py:15
  113.4 1.4 %fusion.22 = f32[320,128]{1,0:T(8,128)S(1)} fusion(f32[320,1280]{1,0:T(8,128)S(1)} %fusion.43, f32[320,1280]{1,0:T(8,128)S(1)} %fusion.41, bf16[1,1,1280,128]{3,1,2,0:T(2,128)(2,1)S(1)} %get-tuple-element.5, pred[]{:T(512)} %bitcast, bf16[2,320,1280]{2,1,0:T(8,128)(2,1)S(1)} %bitcast.185, bf16[2,1,320,1280]{3,2,1,0:T(8,128)(2,1)S(1)} %copy-done.3), kind=kOutput, calls=%fused_computation.31 | convolution fusion | flops 108544000 | bytes 7045121 | tf_op jit(solution)/shard_map/dot_general | solution.py:14
  114.8 0.2 fusion.46
  115.0 0.2 fusion.48
  115.2 0.2 fusion.50
  115.4 0.1 maximum_multiply_fusion.1
  115.7 0.8 maximum_bitcast_fusion
  (22 shorter events, 0.6 us)
Async XLA Ops:
  6.5 35.9 %copy-start.2 = (bf16[2,1,320,1280]{3,2,1,0:T(8,128)(2,1)S(1)}, bf16[2,1,320,1280]{3,2,1,0:T(8,128)(2,1)}, u32[]{:S(2)}) copy-start(bf16[2,1,320,1280]{3,2,1,0:T(8,128)(2,1)} %param.6) | copy-start | bytes 4915204
  6.5 89.0 %all-gather.2.cloned.1.call-start = ((), (), s32[]{:S(2)}) async-start(), calls=%async_computation.1 | async-start | bytes 3276800 | tf_op jit(solution)/shard_map/all_gather | solution.py:40
  47.7 6.4 %copy-start.1 = (bf16[2,3,320,128]{3,1,2,0:T(4,128)(2,1)S(1)}, bf16[2,3,320,128]{3,1,2,0:T(4,128)(2,1)}, u32[]{:S(2)}) copy-start(bf16[2,3,320,128]{3,1,2,0:T(4,128)(2,1)} %convolution_convert_fusion) | copy-start | bytes 1474564
  47.7 7.4 %copy-start.5 = (s32[1,3]{1,0:T(1,128)S(1)}, s32[1,3]{1,0:T(1,128)}, u32[]{:S(2)}) copy-start(s32[1,3]{1,0:T(1,128)} %param.8) | copy-start | bytes 40
  47.7 41.1 %all-to-all-start = ((bf16[2,320,1280]{1,0,2:T(2,128)(2,1)}), bf16[2,320,1280]{1,0,2:T(2,128)(2,1)S(1)}, u32[]{:S(2)}, u32[]{:S(2)}) async-start(bf16[2,320,1280]{1,0,2:T(2,128)(2,1)} %bitcast.1), calls=%async_computation | async-start | bytes 3932160 | tf_op jit(solution)/shard_map/all_to_all | solution.py:45
  88.8 1.3 %copy-start = (bf16[2,320,1280]{1,0,2:T(2,128)(2,1)}, bf16[2,320,1280]{1,0,2:T(2,128)(2,1)S(1)}, u32[]{:S(2)}) copy-start(bf16[2,320,1280]{1,0,2:T(2,128)(2,1)S(1)} %all-to-all-done) | copy-start | bytes 4915204
  102.7 1.4 %copy-start.3 = (bf16[2,1,320,1280]{3,2,1,0:T(8,128)(2,1)S(1)}, bf16[2,1,320,1280]{3,2,1,0:T(8,128)(2,1)}, u32[]{:S(2)}) copy-start(bf16[2,1,320,1280]{3,2,1,0:T(8,128)(2,1)} %param.6) | copy-start | bytes 4915204
  102.7 1.9 %copy-start.4 = (bf16[2,1280,320]{1,2,0:T(8,128)(2,1)S(1)}, bf16[2,1280,320]{1,2,0:T(8,128)(2,1)}, u32[]{:S(2)}) copy-start(bf16[2,1280,320]{1,2,0:T(8,128)(2,1)} %all_to_all.16) | copy-start | bytes 4915204
Sparse Core Ops, SparseCore 0:
  42.6 39.9 all-gather.1
where the time goes:
time: 124 us; the launch traced here: 123 us
  blocking collectives  33.7 us (27%)
  waiting for transfers between devices  32.7 us (26%)
  local copies, waits for them, and re-layouts  22.7 us (18%)
  between operations  16.2 us (13%)
  matrix products  12.3 us (10%)
  starting transfers between devices  3.77 us (3%)
  other arithmetic  1.91 us (2%)
    all_gather x1, blocking collectives, shards(): shard_piece = lax.all_gather(orbitals, 'pb', axis=0, tiled=True)  33.7 us
    all_to_all x1, waiting for transfers between devices, shards(): lax.all_to_all(interaction[:, 0], 'row', split_axis=2, concat_axis=1, til...  32.7 us
    unnamed x15, local copies, waits for them, and re-layouts  7.65 us
    slice x1, local copies, waits for them, and re-layouts, shards(): all_rows[0, slot_index]  7.15 us
    all_to_all x2, local copies, waits for them, and re-layouts, shards(): lax.all_to_all(interaction[:, 0], 'row', split_axis=2, concat_axis=1, til...  5.5 us
    dot_general x3, matrix products, apply_kernel(): prod_real = jnp.dot(kern_real, target, preferred_element_type=jnp.float32)  4.27 us
    dot_general x3, matrix products, apply_kernel(): prod_imag = jnp.dot(kern_imag, target, preferred_element_type=jnp.float32)  4.24 us
    all_to_all x1, starting transfers between devices, shards(): lax.all_to_all(interaction[:, 0], 'row', split_axis=2, concat_axis=1, til...  3.76 us
  transfers between devices with their start and end apart: 2, of which 1 were waited for; matrix products, arithmetic and copies ran while one was open for 8% of the time, Pallas kernels for 0%

commit v1 on v0

--- a/solution.py
+++ b/solution.py
@@ -1,7 +1,13 @@
+import functools
+
 import jax
 import jax.numpy as jnp
 from jax import lax
+from jax.experimental import pallas as pl
+from jax.experimental.pallas import tpu as pltpu
 from jax.sharding import PartitionSpec as P
+
+CORES = 2
 
 
 def rotate_parts(block):
@@ -28,7 +34,7 @@
     return (dens_real, dens_imag)
 
 
-def shards(orbitals, interaction, pair_list, flag_list, pair_counts):
+def general_shards(orbitals, interaction, pair_list, flag_list, pair_counts):
     slot_total = pair_list.shape[1]
     wanted = jnp.stack([pair_list[0, :, 0], pair_list[0, :, 1]])
     shard_piece = lax.all_gather(orbitals, "pb", axis=0, tiled=True)
@@ -57,7 +63,229 @@
     return output[None]
 
 
+def ring_position(index, total):
+    half = index // 2
+    return jnp.where(index % 2 == 0, half, total - 1 - half)
+
+
+def ring_order(total):
+    return list(range(0, total, 2)) + list(range(total - 1, 0, -2))
+
+
+def rotated(block):
+    half = block.shape[1] // 2
+    return jnp.concatenate([block[:, half:], -block[:, :half]], axis=1)
+
+
+def exchange_kernel(steps, total, *refs):
+    (place, pairs, flags, counts), refs = refs[:4], refs[4:]
+    (w_own, w_core, w_far, w_far_core), refs = refs[:4], refs[4:]
+    near, refs = refs[:2], refs[2:]
+    ring, refs = refs[: 2 * steps], refs[2 * steps :]
+    swap, refs = refs[: 2 * steps], refs[2 * steps :]
+    last, refs = refs[:2], refs[2:]
+    out, eff, full, w_sem, orb_sem = refs
+    slots, rows, width = out.shape[1:]
+    points = full.shape[2]
+    chip = 2 * rows
+    wide = rows + 64
+    me, x, c = place[0], place[1], place[2]
+
+    def fetch(slot):
+        turned = flags[0, slot] == 1
+        for which in (1, 0):
+            momentum = pairs[0, slot, which]
+            spot = jnp.where(momentum % 2 == 0, momentum // 2, total - 1 - momentum // 2)
+            gap = lax.rem(spot - me + total, total)
+            dst, sem = full.at[which, slot], orb_sem.at[which, slot]
+
+            def bring(waves, dst=dst, sem=sem):
+                for wave in range(2):
+                    at = jnp.where(turned, wave, jnp.where(wave == 0, x, 1 - x)) * chip
+                    pltpu.make_async_copy(
+                        waves[wave], dst.at[pl.ds(pl.multiple_of(at, chip), chip)], sem
+                    ).start()
+
+            pl.when(gap == 0)(functools.partial(bring, near))
+            for k in range(1, steps + 1):
+                own = gap == jnp.where(c == 0, total - k, k)
+                other = gap == jnp.where(c == 0, k, total - k)
+                pl.when(own)(functools.partial(bring, ring[2 * k - 2 : 2 * k]))
+                pl.when(other)(functools.partial(bring, swap[2 * k - 2 : 2 * k]))
+            pl.when(gap == steps + 1)(functools.partial(bring, last))
+
+    def arrive(which, slot):
+        pltpu.make_async_copy(
+            full.at[which, slot], full.at[which, slot], orb_sem.at[which, slot]
+        ).wait()
+
+    fetch(0)
+    eff_copy = pltpu.make_async_copy(w_own.at[:, 0], eff.at[0], w_sem)
+    eff_copy.start()
+    for slot in range(1, slots):
+        fetch(slot)
+    any_turned = False
+    for slot in range(slots):
+        any_turned = jnp.logical_or(
+            any_turned, jnp.logical_and(slot < counts[0], flags[0, slot] == 1)
+        )
+    for core in range(CORES):
+
+        @pl.when(jnp.logical_and(any_turned, c == core))
+        def _(core=core):
+            first = core * (chip - wide)
+            start = pl.multiple_of(x * chip + first, 128)
+            skip = core * (wide - rows)
+            for block, lanes, at in (
+                (w_own.at[:, 0], pl.ds(start, wide), core * rows),
+                (w_core, slice(first, first + wide), (1 - core) * rows),
+                (w_far, slice(first, first + wide), chip + core * rows),
+                (w_far_core, slice(first, first + wide), chip + (1 - core) * rows),
+            ):
+                eff[1, 0, :, at : at + rows] = block[0, :, lanes].T[skip : skip + rows]
+                eff[1, 1, :, at : at + rows] = -block[1, :, lanes].T[skip : skip + rows]
+
+    eff_copy.wait()
+
+    def compute(slot, carry):
+        arrive(1, slot)
+        arrive(0, slot)
+        live = slot < counts[0]
+
+        @pl.when(live)
+        def _():
+            flag = flags[0, slot]
+            mine = pl.multiple_of(jnp.where(flag == 1, c, 2 * x + c) * rows, rows)
+            local = full[1, slot, pl.ds(mine, rows)]
+            left = jnp.concatenate([local, rotated(local)], axis=0)
+            step = 128
+            result = jnp.zeros((rows, width), jnp.float32)
+            for at in range(0, points, step):
+                dens = lax.dot_general(
+                    left,
+                    full[1, slot, at : at + step],
+                    (((1,), (1,)), ((), ())),
+                    preferred_element_type=jnp.float32,
+                )
+                dens_real, dens_imag = dens[:rows], dens[rows:]
+                eff_real = eff[flag, 0, :, at : at + step].astype(jnp.float32)
+                eff_imag = eff[flag, 1, :, at : at + step].astype(jnp.float32)
+                kern_real = (eff_real * dens_real - eff_imag * dens_imag).astype(jnp.bfloat16)
+                kern_imag = (eff_real * dens_imag + eff_imag * dens_real).astype(jnp.bfloat16)
+                target = full[0, slot, at : at + step]
+                result += jnp.dot(kern_real, target, preferred_element_type=jnp.float32)
+                result += jnp.dot(
+                    kern_imag, -rotated(target), preferred_element_type=jnp.float32
+                )
+            out[0, slot] = result
+
+        @pl.when(jnp.logical_not(live))
+        def _():
+            out[0, slot] = jnp.zeros((rows, width), jnp.float32)
+
+        return carry
+
+    lax.fori_loop(0, slots, compute, 0)
+
+
+def paired_shards(total, orbitals, interaction, pair_list, flag_list, pair_counts):
+    _, rows, width = orbitals.shape
+    slots = pair_list.shape[1]
+    points = interaction.shape[3]
+    chip = CORES * rows
+    row = lax.axis_index("row")
+    x, c = row // CORES, row % CORES
+    me = ring_position(lax.axis_index("pb"), total)
+    order = ring_order(total)
+    row_total = 2 * CORES
+
+    def other_core(value):
+        return lax.ppermute(value, "row", [(r, r ^ 1) for r in range(row_total)])
+
+    def other_chip(value):
+        return lax.ppermute(value, "row", [(r, r ^ CORES) for r in range(row_total)])
+
+    def along_ring(value):
+        moves = []
+        for place in range(total):
+            for r in range(row_total):
+                step = 1 if r % CORES == 0 else -1
+                target = order[(place + step) % total]
+                moves.append((order[place] * row_total + r, target * row_total + r))
+        return lax.ppermute(value, ("pb", "row"), moves)
+
+    def in_order(mine, other):
+        return jnp.where(
+            c == 0, jnp.concatenate([mine, other]), jnp.concatenate([other, mine])
+        )
+
+    def after(value, *earlier):
+        return lax.optimization_barrier((value, *earlier))[0]
+
+    own = orbitals[0]
+    w_block = interaction[:, 0]
+    far = other_chip(own)
+    near_other = other_core(own)
+    w_away = lax.dynamic_slice_in_dim(w_block, (1 - x) * chip, chip, axis=2)
+    w_mine = lax.dynamic_slice_in_dim(w_block, x * chip, chip, axis=2)
+    w_far = other_chip(after(w_away, far))
+    near = [in_order(own, near_other), in_order(far, other_core(after(far, w_away, w_mine)))]
+    steps = total // 2 - 1
+    first, second = [near[0]], [near[1]]
+    for _ in range(steps + 1):
+        first.append(along_ring(first[-1]))
+        second.append(along_ring(second[-1]))
+    ring, swap = [], []
+    for k in range(1, steps + 1):
+        ring += [first[k], second[k]]
+        swap += [other_core(after(first[k], first[steps+1])), other_core(after(second[k], second[steps+1]))]
+    last = [first[steps + 1], second[steps + 1]]
+    w_core = other_core(after(w_mine, first[steps+1]))
+    w_far_core = other_core(after(w_far, second[steps+1]))
+
+    place = jnp.stack([me, x, c]).astype(jnp.int32)
+    in_hbm = pl.BlockSpec(memory_space=pltpu.HBM)
+    in_vmem = pl.BlockSpec(memory_space=pltpu.VMEM)
+    scalars = pl.BlockSpec(memory_space=pltpu.SMEM)
+    pieces = [
+        pltpu.with_memory_space_constraint(piece, pltpu.HBM)
+        for piece in (*near, *ring, *swap, *last)
+    ]
+    w_pieces = [pltpu.with_memory_space_constraint(piece, pltpu.VMEM) for piece in (interaction, w_core, w_far, w_far_core)]
+    return pl.pallas_call(
+        functools.partial(exchange_kernel, steps, total),
+        out_shape=jax.ShapeDtypeStruct((1, slots, rows, width), jnp.float32),
+        in_specs=[scalars] * 4 + [in_vmem] * 4 + [in_hbm] * len(pieces),
+        out_specs=in_vmem,
+        scratch_shapes=[
+            pltpu.VMEM((2, 2, rows, points), jnp.bfloat16),
+            pltpu.VMEM((2, slots, points, width), jnp.bfloat16),
+            pltpu.SemaphoreType.DMA,
+            pltpu.SemaphoreType.DMA((2, slots)),
+        ],
+        compiler_params=pltpu.CompilerParams(vmem_limit_bytes=24 * 2**20),
+        cost_estimate=pl.CostEstimate(
+            flops=slots * rows * points * width * 8, bytes_accessed=8 * 2**20, transcendentals=0
+        ),
+    )(
+        place, pair_list, flag_list, pair_counts,
+        *w_pieces, *pieces,
+    )
+
+
 def solution(mesh):
+    total, row_total = mesh.shape["pb"], mesh.shape["row"]
+
+    def shards(orbitals, interaction, pair_list, flag_list, pair_counts):
+        rows, width = orbitals.shape[1:]
+        fits = total * interaction.shape[3] * width * 2 <= 8 * 2**20
+        aligned = rows % 64 == 0 and (CORES * rows) % 128 == 0 and (rows + 64) % 128 == 0
+        if row_total == 2 * CORES and total % 2 == 0 and total >= 4 and fits and aligned:
+            return paired_shards(
+                total, orbitals, interaction, pair_list, flag_list, pair_counts
+            )
+        return general_shards(orbitals, interaction, pair_list, flag_list, pair_counts)
+
     return jax.shard_map(
         shards,
         mesh=mesh,

time: 124 us -> 44.7 us (0.36)
  blocking collectives: 33.7 us -> 0 us
  waiting for transfers between devices: 32.7 us -> 13.7 us
  local copies, waits for them, and re-layouts: 22.7 us -> 3.78 us
  between operations: 16.2 us -> 0.76 us
  starting transfers between devices: 3.77 us -> 19.2 us
  matrix products: 12.3 us -> 0 us
  Pallas kernels: 0 us -> 6.96 us
  other arithmetic: 1.91 us -> 0.16 us
    all_gather x1 -> x0, blocking collectives: 33.7 us -> none  [shards(): shard_piece = lax.all_gather(orbitals, 'pb', axis=0, tiled=True)]
    all_to_all x1 -> x0, waiting for transfers between devices: 32.7 us -> none  [shards(): lax.all_to_all(interaction[:, 0], 'row', split_axis=2, concat_axis=1, til...]
    ppermute x0 -> x20, starting transfers between devices: none -> 19.2 us  [the longest x8 12.7 us: along_ring(): return lax.ppermute(value, ('pb', 'row'), moves)]
    ppermute x0 -> x20, waiting for transfers between devices: none -> 13.7 us  [the longest x8 11.2 us: along_ring(): return lax.ppermute(value, ('pb', 'row'), moves)]
    dot_general x13 -> x0, matrix products: 12.3 us -> none  [the longest x3 4.27 us: apply_kernel(): prod_real = jnp.dot(kern_real, target, preferred_element_type=jnp.float32)]
    slice x4 -> x0, local copies, waits for them, and re-layouts: 8.82 us -> none  [the longest x1 7.15 us: shards(): all_rows[0, slot_index]]
    pallas_call x0 -> x1, Pallas kernels: none -> 6.96 us  [paired_shards(): pl.pallas_call(functools.partial(exchange_kernel, steps, total), out_shap...]
    unnamed x15 -> x27, local copies, waits for them, and re-layouts: 7.65 us -> 1.21 us
  transfers between devices with their start and end apart: 2 -> 20, of which waited for: 1 -> 12; matrix products, arithmetic and copies ran while one was open for 8% -> 6% of each run, Pallas kernels for 0% -> 0%
where the time goes in v1:
time: 44.7 us; the launch traced here: 44.5 us
  starting transfers between devices  19.2 us (43%)
  waiting for transfers between devices  13.7 us (31%)
  Pallas kernels  6.96 us (16%)
  local copies, waits for them, and re-layouts  3.78 us (8%)
  between operations  0.76 us (2%)
    ppermute x8, starting transfers between devices, along_ring(): return lax.ppermute(value, ('pb', 'row'), moves)  12.7 us
    ppermute x8, waiting for transfers between devices, along_ring(): return lax.ppermute(value, ('pb', 'row'), moves)  11.2 us
    pallas_call x1, Pallas kernels, paired_shards(): pl.pallas_call(functools.partial(exchange_kernel, steps, total), out_shap...  6.96 us
    ppermute x2, starting transfers between devices, other_chip(): lax.ppermute(value, 'row', [(r, r ^ CORES) for r in range(row_total)])  4.5 us
    dynamic_slice x1, local copies, waits for them, and re-layouts, paired_shards(): w_away = lax.dynamic_slice_in_dim(w_block, (1 - x) * chip, chip, axis=2)  2.57 us
    ppermute x10, waiting for transfers between devices, other_core(): return lax.ppermute(value, 'row', [(r, r ^ 1) for r in range(row_total)])  2.42 us
    ppermute x10, starting transfers between devices, other_core(): return lax.ppermute(value, 'row', [(r, r ^ 1) for r in range(row_total)])  1.96 us
    unnamed x27, local copies, waits for them, and re-layouts  1.21 us
  transfers between devices with their start and end apart: 20, of which 12 were waited for; matrix products, arithmetic and copies ran while one was open for 6% of the time, Pallas kernels for 0%

profile of v1, /device:TPU:0, one launch (start us, length us, event | category | flops | bytes accessed | tf_op | source)
XLA Modules:
  0.0 44.5 jit_solution(2378099148378530567)
XLA Ops:
  0.0 2.9 %collective-permute-start.6 = (bf16[320,128]{1,0:T(8,128)(2,1)}, bf16[320,128]{1,0:T(8,128)(2,1)S(1)}, u32[]{:S(2)}, u32[]{:S(2)}) collective-permute-start(bf16[320,128]{1,0:T(8,128)(2,1)} %bitcast.8), channel_id=1, source_target_pairs={{0,2},{1,3},{2,0},{3,1},{4,6},{5,7},{6,4},{7,5},{8,10},{9,11},{10,... | collective-permute-start | bytes 245768 | tf_op jit(solution)/shard_map/ppermute | solution.py:206
  3.0 2.6 %dynamic-slice_bitcast_fusion = (bf16[2,320,640]{2,1,0:T(8,128)(2,1)S(1)}, bf16[2,320,640]{2,1,0:T(8,128)(2,1)}) fusion(bf16[2,1,320,1280]{3,2,1,0:T(8,128)(2,1)} %refs_4_.1, s32[]{:T(128)S(6)} %select_n.47, s32[]{:T(128)S(6)} %select_n.44), kind=kLoop, calls=%fused_computation | loop fusion | bytes 3276808 | tf_op jit(solution)/shard_map/dynamic_slice | solution.py:229
  5.6 0.4 %collective-permute-start.8 = (bf16[320,128]{1,0:T(8,128)(2,1)S(1)}, bf16[320,128]{1,0:T(8,128)(2,1)S(1)}, u32[]{:S(2)}, u32[]{:S(2)}) collective-permute-start(bf16[320,128]{1,0:T(8,128)(2,1)S(1)} %collective-permute-done.6), channel_id=1, source_target_pairs={{0,1},{1,0},{2,3},{3,2},{4,5},{5,4},{6,7},{7,6},{8,9},{9,8},{10,11... | collective-permute-start | bytes 245768 | tf_op jit(solution)/shard_map/ppermute | solution.py:203
  6.0 1.6 %collective-permute-start.7 = (bf16[2,320,640]{2,1,0:T(8,128)(2,1)S(1)}, bf16[2,320,640]{2,1,0:T(8,128)(2,1)S(1)}, u32[]{:S(2)}, u32[]{:S(2)}) collective-permute-start(bf16[2,320,640]{2,1,0:T(8,128)(2,1)S(1)} %get-tuple-element.16), channel_id=1, source_target_pairs={{0,2},{1,3},{2,0},{3,1},{4,6},{5,7},{6,4},{7,5},{8,10},{9,11},{10,... | collective-permute-start | bytes 2457608 | tf_op jit(solution)/shard_map/ppermute | solution.py:206
  7.7 1.6 %collective-permute-start.1 = (bf16[640,128]{1,0:T(8,128)(2,1)S(1)}, bf16[640,128]{1,0:T(8,128)(2,1)S(1)}, u32[]{:S(2)}, u32[]{:S(2)}) collective-permute-start(bf16[640,128]{1,0:T(8,128)(2,1)S(1)} %maximum_select_fusion.refs_8_), channel_id=1, source_target_pairs={{0,8},{1,5},{2,10},{3,7},{8,16},{9,1},{10,18},{11,3},{16,24},{17,9... | collective-permute-start | bytes 491528 | tf_op jit(solution)/shard_map/ppermute | solution.py:215
  9.3 1.6 %collective-permute-start.9 = (bf16[640,128]{1,0:T(8,128)(2,1)S(1)}, bf16[640,128]{1,0:T(8,128)(2,1)}, u32[]{:S(2)}, u32[]{:S(2)}) collective-permute-start(bf16[640,128]{1,0:T(8,128)(2,1)S(1)} %maximum_select_fusion.1.refs_9_), channel_id=1, source_target_pairs={{0,8},{1,5},{2,10},{3,7},{8,16},{9,1},{10,18},{11,3},{16,24},{17,9... | collective-permute-start | bytes 491528 | tf_op jit(solution)/shard_map/ppermute | solution.py:215
  11.0 2.1 %collective-permute-done.1.refs_10_ = bf16[640,128]{1,0:T(8,128)(2,1)S(1)} collective-permute-done((bf16[640,128]{1,0:T(8,128)(2,1)S(1)}, bf16[640,128]{1,0:T(8,128)(2,1)S(1)}, u32[]{:S(2)}, u32[]{:S(2)}) %collective-permute-start.1) | collective-permute-done | bytes 163872 | tf_op jit(solution)/shard_map/ppermute | solution.py:215
  13.0 1.6 %collective-permute-start.2 = (bf16[640,128]{1,0:T(8,128)(2,1)S(1)}, bf16[640,128]{1,0:T(8,128)(2,1)S(1)}, u32[]{:S(2)}, u32[]{:S(2)}) collective-permute-start(bf16[640,128]{1,0:T(8,128)(2,1)S(1)} %collective-permute-done.1.refs_10_), channel_id=1, source_target_pairs={{0,8},{1,5},{2,10},{3,7},{8,16},{9,1},{10,18},{11,3},{16,24},{17,9... | collective-permute-start | bytes 491528 | tf_op jit(solution)/shard_map/ppermute | solution.py:215
  14.6 0.3 collective-permute-done.9.refs_11_
  14.9 1.6 %collective-permute-start.10 = (bf16[640,128]{1,0:T(8,128)(2,1)}, bf16[640,128]{1,0:T(8,128)(2,1)}, u32[]{:S(2)}, u32[]{:S(2)}) collective-permute-start(bf16[640,128]{1,0:T(8,128)(2,1)} %collective-permute-done.9.refs_11_), channel_id=1, source_target_pairs={{0,8},{1,5},{2,10},{3,7},{8,16},{9,1},{10,18},{11,3},{16,24},{17,9... | collective-permute-start | bytes 491528 | tf_op jit(solution)/shard_map/ppermute | solution.py:215
  16.5 1.9 %collective-permute-done.2.refs_12_ = bf16[640,128]{1,0:T(8,128)(2,1)S(1)} collective-permute-done((bf16[640,128]{1,0:T(8,128)(2,1)S(1)}, bf16[640,128]{1,0:T(8,128)(2,1)S(1)}, u32[]{:S(2)}, u32[]{:S(2)}) %collective-permute-start.2) | collective-permute-done | bytes 163872 | tf_op jit(solution)/shard_map/ppermute | solution.py:215
  18.4 1.6 %collective-permute-start.3 = (bf16[640,128]{1,0:T(8,128)(2,1)S(1)}, bf16[640,128]{1,0:T(8,128)(2,1)S(1)}, u32[]{:S(2)}, u32[]{:S(2)}) collective-permute-start(bf16[640,128]{1,0:T(8,128)(2,1)S(1)} %collective-permute-done.2.refs_12_), channel_id=1, source_target_pairs={{0,8},{1,5},{2,10},{3,7},{8,16},{9,1},{10,18},{11,3},{16,24},{17,9... | collective-permute-start | bytes 491528 | tf_op jit(solution)/shard_map/ppermute | solution.py:215
  19.9 0.6 %collective-permute-done.10.refs_13_ = bf16[640,128]{1,0:T(8,128)(2,1)} collective-permute-done((bf16[640,128]{1,0:T(8,128)(2,1)}, bf16[640,128]{1,0:T(8,128)(2,1)}, u32[]{:S(2)}, u32[]{:S(2)}) %collective-permute-start.10) | collective-permute-done | bytes 163872 | tf_op jit(solution)/shard_map/ppermute | solution.py:215
  20.5 1.6 %collective-permute-start.11 = (bf16[640,128]{1,0:T(8,128)(2,1)}, bf16[640,128]{1,0:T(8,128)(2,1)}, u32[]{:S(2)}, u32[]{:S(2)}) collective-permute-start(bf16[640,128]{1,0:T(8,128)(2,1)} %collective-permute-done.10.refs_13_), channel_id=1, source_target_pairs={{0,8},{1,5},{2,10},{3,7},{8,16},{9,1},{10,18},{11,3},{16,24},{17,9... | collective-permute-start | bytes 491528 | tf_op jit(solution)/shard_map/ppermute | solution.py:215
  22.1 1.6 %collective-permute-done.3.refs_14_ = bf16[640,128]{1,0:T(8,128)(2,1)S(1)} collective-permute-done((bf16[640,128]{1,0:T(8,128)(2,1)S(1)}, bf16[640,128]{1,0:T(8,128)(2,1)S(1)}, u32[]{:S(2)}, u32[]{:S(2)}) %collective-permute-start.3) | collective-permute-done | bytes 163872 | tf_op jit(solution)/shard_map/ppermute | solution.py:215
  23.7 1.6 %collective-permute-start.4 = (bf16[640,128]{1,0:T(8,128)(2,1)S(1)}, bf16[640,128]{1,0:T(8,128)(2,1)}, u32[]{:S(2)}, u32[]{:S(2)}) collective-permute-start(bf16[640,128]{1,0:T(8,128)(2,1)S(1)} %collective-permute-done.3.refs_14_), channel_id=1, source_target_pairs={{0,8},{1,5},{2,10},{3,7},{8,16},{9,1},{10,18},{11,3},{16,24},{17,9... | collective-permute-start | bytes 491528 | tf_op jit(solution)/shard_map/ppermute | solution.py:215
  25.3 0.9 %collective-permute-done.11.refs_15_ = bf16[640,128]{1,0:T(8,128)(2,1)} collective-permute-done((bf16[640,128]{1,0:T(8,128)(2,1)}, bf16[640,128]{1,0:T(8,128)(2,1)}, u32[]{:S(2)}, u32[]{:S(2)}) %collective-permute-start.11) | collective-permute-done | bytes 163872 | tf_op jit(solution)/shard_map/ppermute | solution.py:215
  26.2 1.6 %collective-permute-start.12 = (bf16[640,128]{1,0:T(8,128)(2,1)}, bf16[640,128]{1,0:T(8,128)(2,1)S(1)}, u32[]{:S(2)}, u32[]{:S(2)}) collective-permute-start(bf16[640,128]{1,0:T(8,128)(2,1)} %collective-permute-done.11.refs_15_), channel_id=1, source_target_pairs={{0,8},{1,5},{2,10},{3,7},{8,16},{9,1},{10,18},{11,3},{16,24},{17,9... | collective-permute-start | bytes 491528 | tf_op jit(solution)/shard_map/ppermute | solution.py:215
  27.7 1.4 %collective-permute-done.4.refs_22_ = bf16[640,128]{1,0:T(8,128)(2,1)} collective-permute-done((bf16[640,128]{1,0:T(8,128)(2,1)S(1)}, bf16[640,128]{1,0:T(8,128)(2,1)}, u32[]{:S(2)}, u32[]{:S(2)}) %collective-permute-start.4) | collective-permute-done | bytes 163872 | tf_op jit(solution)/shard_map/ppermute | solution.py:215
  29.1 2.6 %collective-permute-done.12.refs_23_ = bf16[640,128]{1,0:T(8,128)(2,1)S(1)} collective-permute-done((bf16[640,128]{1,0:T(8,128)(2,1)}, bf16[640,128]{1,0:T(8,128)(2,1)S(1)}, u32[]{:S(2)}, u32[]{:S(2)}) %collective-permute-start.12) | collective-permute-done | bytes 163872 | tf_op jit(solution)/shard_map/ppermute | solution.py:215
  31.7 0.5 %collective-permute-start.14 = (bf16[640,128]{1,0:T(8,128)(2,1)S(1)}, bf16[640,128]{1,0:T(8,128)(2,1)S(1)}, u32[]{:S(2)}, u32[]{:S(2)}) collective-permute-start(bf16[640,128]{1,0:T(8,128)(2,1)S(1)} %collective-permute-done.1.refs_10_), channel_id=1, source_target_pairs={{0,1},{1,0},{2,3},{3,2},{4,5},{5,4},{6,7},{7,6},{8,9},{9,8},{10,11... | collective-permute-start | bytes 491528 | tf_op jit(solution)/shard_map/ppermute | solution.py:203
  32.3 0.4 collective-permute-start.18
  32.7 1.4 %collective-permute-done.14.refs_16_ = bf16[640,128]{1,0:T(8,128)(2,1)S(1)} collective-permute-done((bf16[640,128]{1,0:T(8,128)(2,1)S(1)}, bf16[640,128]{1,0:T(8,128)(2,1)S(1)}, u32[]{:S(2)}, u32[]{:S(2)}) %collective-permute-start.14) | collective-permute-done | bytes 163872 | tf_op jit(solution)/shard_map/ppermute | solution.py:203
  34.1 0.1 collective-permute-start.15
  34.3 0.2 collective-permute-done.16.refs_18_
  34.5 0.2 collective-permute-start.17
  34.8 0.4 copy-done.9
  35.2 0.7 %copy-done.10 = bf16[640,128]{1,0:T(8,128)(2,1)} copy-done((bf16[640,128]{1,0:T(8,128)(2,1)}, bf16[640,128]{1,0:T(8,128)(2,1)S(1)}, u32[]{:S(2)}) %copy-start.10) | copy-done | bytes 163864
  35.8 0.1 collective-permute-start.19
  36.6 0.1 copy.6.refs_1_
  36.8 0.8 %collective-permute-done.19.refs_21_ = bf16[640,128]{1,0:T(8,128)(2,1)} collective-permute-done((bf16[640,128]{1,0:T(8,128)(2,1)}, bf16[640,128]{1,0:T(8,128)(2,1)}, u32[]{:S(2)}, u32[]{:S(2)}) %collective-permute-start.19) | collective-permute-done | bytes 163872 | tf_op jit(solution)/shard_map/ppermute | solution.py:203
  37.6 7.0 %shard_map.55 = f32[1,3,320,128]{3,2,1,0:T(8,128)} custom-call(s32[3]{0:T(128)S(1)} %pad_add_fusion.refs_0_, s32[1,3,2]{2,1,0:T(4,128)S(1)} %copy.6.refs_1_, s32[1,3]{1,0:T(1,128)S(1)} %copy-done.1, s32[1]{0:T(128)S(6)} %copy.7.refs_3_, bf16[2,1,320,1280]{3,2,1,0:T(8,128)(2,1)S(1)} %copy-done, bf16[2,320,640]{2,1,0:T(8,128)(2,1)S(1)} %collective-permute-done.5.refs_5_, ...), custom_call_target="tpu_custom_call" | custom-call | flops 1258291200 | bytes 8388608 | tf_op jit(solution)/shard_map/pallas_call | solution.py:255
  (40 shorter events, 0.4 us)
Async XLA Ops:
  0.0 5.6 %collective-permute-start.6 = (bf16[320,128]{1,0:T(8,128)(2,1)}, bf16[320,128]{1,0:T(8,128)(2,1)S(1)}, u32[]{:S(2)}, u32[]{:S(2)}) collective-permute-start(bf16[320,128]{1,0:T(8,128)(2,1)} %bitcast.8), channel_id=1, source_target_pairs={{0,2},{1,3},{2,0},{3,1},{4,6},{5,7},{6,4},{7,5},{8,10},{9,11},{10,... | collective-permute-start | bytes 245768 | tf_op jit(solution)/shard_map/ppermute | solution.py:206
  2.9 4.7 %collective-permute-start = (bf16[320,128]{1,0:T(8,128)(2,1)}, bf16[320,128]{1,0:T(8,128)(2,1)S(1)}, u32[]{:S(2)}, u32[]{:S(2)}) collective-permute-start(bf16[320,128]{1,0:T(8,128)(2,1)} %bitcast.9), channel_id=1, source_target_pairs={{0,1},{1,0},{2,3},{3,2},{4,5},{5,4},{6,7},{7,6},{8,9},{9,8},{10,11... | collective-permute-start | bytes 245768 | tf_op jit(solution)/shard_map/ppermute | solution.py:203
  2.9 4.7 %copy-start.11 = (bf16[1,320,128]{2,1,0:T(8,128)(2,1)S(1)}, bf16[1,320,128]{2,1,0:T(8,128)(2,1)}, u32[]{:S(2)}) copy-start(bf16[1,320,128]{2,1,0:T(8,128)(2,1)} %param.5) | copy-start | bytes 245764
  2.9 33.7 %copy-start.12 = (s32[1,3,2]{1,2,0:T(2,128)S(1)}, s32[1,3,2]{1,2,0:T(2,128)}, u32[]{:S(2)}) copy-start(s32[1,3,2]{1,2,0:T(2,128)} %param.7) | copy-start | bytes 76
  2.9 34.6 %copy-start = (bf16[2,1,320,1280]{3,2,1,0:T(8,128)(2,1)S(1)}, bf16[2,1,320,1280]{3,2,1,0:T(8,128)(2,1)}, u32[]{:S(2)}) copy-start(bf16[2,1,320,1280]{3,2,1,0:T(8,128)(2,1)} %refs_4_.1) | copy-start | bytes 4915204
  3.0 34.6 %copy-start.1 = (s32[1,3]{1,0:T(1,128)S(1)}, s32[1,3]{1,0:T(1,128)}, u32[]{:S(2)}) copy-start(s32[1,3]{1,0:T(1,128)} %refs_2_.1) | copy-start | bytes 40
  5.6 3.7 %collective-permute-start.8 = (bf16[320,128]{1,0:T(8,128)(2,1)S(1)}, bf16[320,128]{1,0:T(8,128)(2,1)S(1)}, u32[]{:S(2)}, u32[]{:S(2)}) collective-permute-start(bf16[320,128]{1,0:T(8,128)(2,1)S(1)} %collective-permute-done.6), channel_id=1, source_target_pairs={{0,1},{1,0},{2,3},{3,2},{4,5},{5,4},{6,7},{7,6},{8,9},{9,8},{10,11... | collective-permute-start | bytes 245768 | tf_op jit(solution)/shard_map/ppermute | solution.py:203
  6.0 25.7 %collective-permute-start.7 = (bf16[2,320,640]{2,1,0:T(8,128)(2,1)S(1)}, bf16[2,320,640]{2,1,0:T(8,128)(2,1)S(1)}, u32[]{:S(2)}, u32[]{:S(2)}) collective-permute-start(bf16[2,320,640]{2,1,0:T(8,128)(2,1)S(1)} %get-tuple-element.16), channel_id=1, source_target_pairs={{0,2},{1,3},{2,0},{3,1},{4,6},{5,7},{6,4},{7,5},{8,10},{9,11},{10,... | collective-permute-start | bytes 2457608 | tf_op jit(solution)/shard_map/ppermute | solution.py:206
  7.6 29.9 %copy-start.2 = (bf16[640,128]{1,0:T(8,128)(2,1)}, bf16[640,128]{1,0:T(8,128)(2,1)S(1)}, u32[]{:S(2)}) copy-start(bf16[640,128]{1,0:T(8,128)(2,1)S(1)} %maximum_select_fusion.refs_8_) | copy-start | bytes 491524
  7.7 5.4 %collective-permute-start.1 = (bf16[640,128]{1,0:T(8,128)(2,1)S(1)}, bf16[640,128]{1,0:T(8,128)(2,1)S(1)}, u32[]{:S(2)}, u32[]{:S(2)}) collective-permute-start(bf16[640,128]{1,0:T(8,128)(2,1)S(1)} %maximum_select_fusion.refs_8_), channel_id=1, source_target_pairs={{0,8},{1,5},{2,10},{3,7},{8,16},{9,1},{10,18},{11,3},{16,24},{17,9... | collective-permute-start | bytes 491528 | tf_op jit(solution)/shard_map/ppermute | solution.py:215
  9.3 18.4 %copy-start.3 = (bf16[640,128]{1,0:T(8,128)(2,1)}, bf16[640,128]{1,0:T(8,128)(2,1)S(1)}, u32[]{:S(2)}) copy-start(bf16[640,128]{1,0:T(8,128)(2,1)S(1)} %maximum_select_fusion.1.refs_9_) | copy-start | bytes 491524
  9.3 5.5 %collective-permute-start.9 = (bf16[640,128]{1,0:T(8,128)(2,1)S(1)}, bf16[640,128]{1,0:T(8,128)(2,1)}, u32[]{:S(2)}, u32[]{:S(2)}) collective-permute-start(bf16[640,128]{1,0:T(8,128)(2,1)S(1)} %maximum_select_fusion.1.refs_9_), channel_id=1, source_target_pairs={{0,8},{1,5},{2,10},{3,7},{8,16},{9,1},{10,18},{11,3},{16,24},{17,9... | collective-permute-start | bytes 491528 | tf_op jit(solution)/shard_map/ppermute | solution.py:215
  13.0 18.7 %copy-start.4 = (bf16[640,128]{1,0:T(8,128)(2,1)}, bf16[640,128]{1,0:T(8,128)(2,1)S(1)}, u32[]{:S(2)}) copy-start(bf16[640,128]{1,0:T(8,128)(2,1)S(1)} %collective-permute-done.1.refs_10_) | copy-start | bytes 491524
  13.0 5.3 %collective-permute-start.2 = (bf16[640,128]{1,0:T(8,128)(2,1)S(1)}, bf16[640,128]{1,0:T(8,128)(2,1)S(1)}, u32[]{:S(2)}, u32[]{:S(2)}) collective-permute-start(bf16[640,128]{1,0:T(8,128)(2,1)S(1)} %collective-permute-done.1.refs_10_), channel_id=1, source_target_pairs={{0,8},{1,5},{2,10},{3,7},{8,16},{9,1},{10,18},{11,3},{16,24},{17,9... | collective-permute-start | bytes 491528 | tf_op jit(solution)/shard_map/ppermute | solution.py:215
  14.9 5.6 %collective-permute-start.10 = (bf16[640,128]{1,0:T(8,128)(2,1)}, bf16[640,128]{1,0:T(8,128)(2,1)}, u32[]{:S(2)}, u32[]{:S(2)}) collective-permute-start(bf16[640,128]{1,0:T(8,128)(2,1)} %collective-permute-done.9.refs_11_), channel_id=1, source_target_pairs={{0,8},{1,5},{2,10},{3,7},{8,16},{9,1},{10,18},{11,3},{16,24},{17,9... | collective-permute-start | bytes 491528 | tf_op jit(solution)/shard_map/ppermute | solution.py:215
  18.4 15.8 %copy-start.5 = (bf16[640,128]{1,0:T(8,128)(2,1)}, bf16[640,128]{1,0:T(8,128)(2,1)S(1)}, u32[]{:S(2)}) copy-start(bf16[640,128]{1,0:T(8,128)(2,1)S(1)} %collective-permute-done.2.refs_12_) | copy-start | bytes 491524
  18.4 5.3 %collective-permute-start.3 = (bf16[640,128]{1,0:T(8,128)(2,1)S(1)}, bf16[640,128]{1,0:T(8,128)(2,1)S(1)}, u32[]{:S(2)}, u32[]{:S(2)}) collective-permute-start(bf16[640,128]{1,0:T(8,128)(2,1)S(1)} %collective-permute-done.2.refs_12_), channel_id=1, source_target_pairs={{0,8},{1,5},{2,10},{3,7},{8,16},{9,1},{10,18},{11,3},{16,24},{17,9... | collective-permute-start | bytes 491528 | tf_op jit(solution)/shard_map/ppermute | solution.py:215
  20.5 5.6 %collective-permute-start.11 = (bf16[640,128]{1,0:T(8,128)(2,1)}, bf16[640,128]{1,0:T(8,128)(2,1)}, u32[]{:S(2)}, u32[]{:S(2)}) collective-permute-start(bf16[640,128]{1,0:T(8,128)(2,1)} %collective-permute-done.10.refs_13_), channel_id=1, source_target_pairs={{0,8},{1,5},{2,10},{3,7},{8,16},{9,1},{10,18},{11,3},{16,24},{17,9... | collective-permute-start | bytes 491528 | tf_op jit(solution)/shard_map/ppermute | solution.py:215
  23.7 10.8 %copy-start.6 = (bf16[640,128]{1,0:T(8,128)(2,1)}, bf16[640,128]{1,0:T(8,128)(2,1)S(1)}, u32[]{:S(2)}) copy-start(bf16[640,128]{1,0:T(8,128)(2,1)S(1)} %collective-permute-done.3.refs_14_) | copy-start | bytes 491524
  23.7 5.4 %collective-permute-start.4 = (bf16[640,128]{1,0:T(8,128)(2,1)S(1)}, bf16[640,128]{1,0:T(8,128)(2,1)}, u32[]{:S(2)}, u32[]{:S(2)}) collective-permute-start(bf16[640,128]{1,0:T(8,128)(2,1)S(1)} %collective-permute-done.3.refs_14_), channel_id=1, source_target_pairs={{0,8},{1,5},{2,10},{3,7},{8,16},{9,1},{10,18},{11,3},{16,24},{17,9... | collective-permute-start | bytes 491528 | tf_op jit(solution)/shard_map/ppermute | solution.py:215
  26.2 5.5 %collective-permute-start.12 = (bf16[640,128]{1,0:T(8,128)(2,1)}, bf16[640,128]{1,0:T(8,128)(2,1)S(1)}, u32[]{:S(2)}, u32[]{:S(2)}) collective-permute-start(bf16[640,128]{1,0:T(8,128)(2,1)} %collective-permute-done.11.refs_15_), channel_id=1, source_target_pairs={{0,8},{1,5},{2,10},{3,7},{8,16},{9,1},{10,18},{11,3},{16,24},{17,9... | collective-permute-start | bytes 491528 | tf_op jit(solution)/shard_map/ppermute | solution.py:215
  29.1 8.5 %collective-permute-start.5 = (bf16[2,320,640]{2,1,0:T(8,128)(2,1)}, bf16[2,320,640]{2,1,0:T(8,128)(2,1)S(1)}, u32[]{:S(2)}, u32[]{:S(2)}) collective-permute-start(bf16[2,320,640]{2,1,0:T(8,128)(2,1)} %get-tuple-element.15), channel_id=1, source_target_pairs={{0,1},{1,0},{2,3},{3,2},{4,5},{5,4},{6,7},{7,6},{8,9},{9,8},{10,11... | collective-permute-start | bytes 2457608 | tf_op jit(solution)/shard_map/ppermute | solution.py:203
  31.7 3.0 %copy-start.7 = (bf16[640,128]{1,0:T(8,128)(2,1)}, bf16[640,128]{1,0:T(8,128)(2,1)S(1)}, u32[]{:S(2)}) copy-start(bf16[640,128]{1,0:T(8,128)(2,1)S(1)} %collective-permute-done.12.refs_23_) | copy-start | bytes 491524
  31.7 5.9 %collective-permute-start.13 = (bf16[2,320,640]{2,1,0:T(8,128)(2,1)S(1)}, bf16[2,320,640]{2,1,0:T(8,128)(2,1)}, u32[]{:S(2)}, u32[]{:S(2)}) collective-permute-start(bf16[2,320,640]{2,1,0:T(8,128)(2,1)S(1)} %collective-permute-done.7.refs_6_), channel_id=1, source_target_pairs={{0,1},{1,0},{2,3},{3,2},{4,5},{5,4},{6,7},{7,6},{8,9},{9,8},{10,11... | collective-permute-start | bytes 2457608 | tf_op jit(solution)/shard_map/ppermute | solution.py:203
  31.7 2.4 %collective-permute-start.14 = (bf16[640,128]{1,0:T(8,128)(2,1)S(1)}, bf16[640,128]{1,0:T(8,128)(2,1)S(1)}, u32[]{:S(2)}, u32[]{:S(2)}) collective-permute-start(bf16[640,128]{1,0:T(8,128)(2,1)S(1)} %collective-permute-done.1.refs_10_), channel_id=1, source_target_pairs={{0,1},{1,0},{2,3},{3,2},{4,5},{5,4},{6,7},{7,6},{8,9},{9,8},{10,11... | collective-permute-start | bytes 491528 | tf_op jit(solution)/shard_map/ppermute | solution.py:203
  32.2 2.3 %collective-permute-start.16 = (bf16[640,128]{1,0:T(8,128)(2,1)S(1)}, bf16[640,128]{1,0:T(8,128)(2,1)S(1)}, u32[]{:S(2)}, u32[]{:S(2)}) collective-permute-start(bf16[640,128]{1,0:T(8,128)(2,1)S(1)} %collective-permute-done.2.refs_12_), channel_id=1, source_target_pairs={{0,1},{1,0},{2,3},{3,2},{4,5},{5,4},{6,7},{7,6},{8,9},{9,8},{10,11... | collective-permute-start | bytes 491528 | tf_op jit(solution)/shard_map/ppermute | solution.py:203
  32.3 2.4 %collective-permute-start.18 = (bf16[640,128]{1,0:T(8,128)(2,1)S(1)}, bf16[640,128]{1,0:T(8,128)(2,1)S(1)}, u32[]{:S(2)}, u32[]{:S(2)}) collective-permute-start(bf16[640,128]{1,0:T(8,128)(2,1)S(1)} %collective-permute-done.3.refs_14_), channel_id=1, source_target_pairs={{0,1},{1,0},{2,3},{3,2},{4,5},{5,4},{6,7},{7,6},{8,9},{9,8},{10,11... | collective-permute-start | bytes 491528 | tf_op jit(solution)/shard_map/ppermute | solution.py:203
  34.1 0.7 %copy-start.8 = (bf16[640,128]{1,0:T(8,128)(2,1)}, bf16[640,128]{1,0:T(8,128)(2,1)S(1)}, u32[]{:S(2)}) copy-start(bf16[640,128]{1,0:T(8,128)(2,1)S(1)} %collective-permute-done.14.refs_16_) | copy-start | bytes 491524
  34.1 2.7 %collective-permute-start.15 = (bf16[640,128]{1,0:T(8,128)(2,1)}, bf16[640,128]{1,0:T(8,128)(2,1)}, u32[]{:S(2)}, u32[]{:S(2)}) collective-permute-start(bf16[640,128]{1,0:T(8,128)(2,1)} %collective-permute-done.9.refs_11_), channel_id=1, source_target_pairs={{0,1},{1,0},{2,3},{3,2},{4,5},{5,4},{6,7},{7,6},{8,9},{9,8},{10,11... | collective-permute-start | bytes 491528 | tf_op jit(solution)/shard_map/ppermute | solution.py:203
  34.5 0.7 %copy-start.9 = (bf16[640,128]{1,0:T(8,128)(2,1)}, bf16[640,128]{1,0:T(8,128)(2,1)S(1)}, u32[]{:S(2)}) copy-start(bf16[640,128]{1,0:T(8,128)(2,1)S(1)} %collective-permute-done.16.refs_18_) | copy-start | bytes 491524
  34.5 2.3 %collective-permute-start.17 = (bf16[640,128]{1,0:T(8,128)(2,1)}, bf16[640,128]{1,0:T(8,128)(2,1)}, u32[]{:S(2)}, u32[]{:S(2)}) collective-permute-start(bf16[640,128]{1,0:T(8,128)(2,1)} %collective-permute-done.10.refs_13_), channel_id=1, source_target_pairs={{0,1},{1,0},{2,3},{3,2},{4,5},{5,4},{6,7},{7,6},{8,9},{9,8},{10,11... | collective-permute-start | bytes 491528 | tf_op jit(solution)/shard_map/ppermute | solution.py:203
  35.8 1.7 %collective-permute-start.19 = (bf16[640,128]{1,0:T(8,128)(2,1)}, bf16[640,128]{1,0:T(8,128)(2,1)}, u32[]{:S(2)}, u32[]{:S(2)}) collective-permute-start(bf16[640,128]{1,0:T(8,128)(2,1)} %collective-permute-done.11.refs_15_), channel_id=1, source_target_pairs={{0,1},{1,0},{2,3},{3,2},{4,5},{5,4},{6,7},{7,6},{8,9},{9,8},{10,11... | collective-permute-start | bytes 491528 | tf_op jit(solution)/shard_map/ppermute | solution.py:203
  (1 other events, 0.7 us)

commit v2 on v1

--- a/solution.py
+++ b/solution.py
@@ -78,7 +78,7 @@
 
 
 def exchange_kernel(steps, total, *refs):
-    (place, pairs, flags, counts), refs = refs[:4], refs[4:]
+    (pairs, flags, counts), refs = refs[:3], refs[3:]
     (w_own, w_core, w_far, w_far_core), refs = refs[:4], refs[4:]
     near, refs = refs[:2], refs[2:]
     ring, refs = refs[: 2 * steps], refs[2 * steps :]
@@ -89,12 +89,14 @@
     points = full.shape[2]
     chip = 2 * rows
     wide = rows + 64
-    me, x, c = place[0], place[1], place[2]
+    row = lax.axis_index("row")
+    x, c = row // CORES, row % CORES
+    me = ring_position(lax.axis_index("pb"), total)
 
     def fetch(slot):
         turned = flags[0, slot] == 1
         for which in (1, 0):
-            momentum = pairs[0, slot, which]
+            momentum = pairs[0, which, slot]
             spot = jnp.where(momentum % 2 == 0, momentum // 2, total - 1 - momentum // 2)
             gap = lax.rem(spot - me + total, total)
             dst, sem = full.at[which, slot], orb_sem.at[which, slot]
@@ -195,7 +197,6 @@
     chip = CORES * rows
     row = lax.axis_index("row")
     x, c = row // CORES, row % CORES
-    me = ring_position(lax.axis_index("pb"), total)
     order = ring_order(total)
     row_total = 2 * CORES
 
@@ -226,24 +227,29 @@
     w_block = interaction[:, 0]
     far = other_chip(own)
     near_other = other_core(own)
+    near = [in_order(own, near_other)]
     w_away = lax.dynamic_slice_in_dim(w_block, (1 - x) * chip, chip, axis=2)
-    w_mine = lax.dynamic_slice_in_dim(w_block, x * chip, chip, axis=2)
     w_far = other_chip(after(w_away, far))
-    near = [in_order(own, near_other), in_order(far, other_core(after(far, w_away, w_mine)))]
+    near.append(in_order(far, other_core(after(far, w_away))))
     steps = total // 2 - 1
     first, second = [near[0]], [near[1]]
-    for _ in range(steps + 1):
-        first.append(along_ring(first[-1]))
-        second.append(along_ring(second[-1]))
-    ring, swap = [], []
-    for k in range(1, steps + 1):
-        ring += [first[k], second[k]]
-        swap += [other_core(after(first[k], first[steps+1])), other_core(after(second[k], second[steps+1]))]
+    swap_first, swap_second = [], []
+    for k in range(steps + 1):
+        if k >= 2:
+            swap_first.append(other_core(first[k - 1]))
+            swap_second.append(other_core(second[k - 1]))
+        first.append(along_ring(after(first[-1], swap_second[0]) if k == 3 else first[-1]))
+        second.append(along_ring(after(second[-1], swap_first[0]) if k == 3 else second[-1]))
+    ring = [wave[k] for k in range(1, steps + 1) for wave in (first, second)]
     last = [first[steps + 1], second[steps + 1]]
-    w_core = other_core(after(w_mine, first[steps+1]))
-    w_far_core = other_core(after(w_far, second[steps+1]))
-
-    place = jnp.stack([me, x, c]).astype(jnp.int32)
+    for k in range(len(swap_first) + 1, steps + 1):
+        swap_first.append(other_core(after(first[k], last[0])))
+        swap_second.append(other_core(after(second[k], last[1])))
+    swap = [wave[k] for k in range(steps) for wave in (swap_first, swap_second)]
+    w_far_core = other_core(after(w_far, last[1]))
+    w_mine = lax.dynamic_slice_in_dim(w_block, x * chip, chip, axis=2)
+    w_core = other_core(after(w_mine, last[0]))
+
     in_hbm = pl.BlockSpec(memory_space=pltpu.HBM)
     in_vmem = pl.BlockSpec(memory_space=pltpu.VMEM)
     scalars = pl.BlockSpec(memory_space=pltpu.SMEM)
@@ -255,7 +261,7 @@
     return pl.pallas_call(
         functools.partial(exchange_kernel, steps, total),
         out_shape=jax.ShapeDtypeStruct((1, slots, rows, width), jnp.float32),
-        in_specs=[scalars] * 4 + [in_vmem] * 4 + [in_hbm] * len(pieces),
+        in_specs=[scalars] * 3 + [in_vmem] * 4 + [in_hbm] * len(pieces),
         out_specs=in_vmem,
         scratch_shapes=[
             pltpu.VMEM((2, 2, rows, points), jnp.bfloat16),
@@ -268,7 +274,7 @@
             flops=slots * rows * points * width * 8, bytes_accessed=8 * 2**20, transcendentals=0
         ),
     )(
-        place, pair_list, flag_list, pair_counts,
+        jnp.swapaxes(pair_list, 1, 2), flag_list, pair_counts,
         *w_pieces, *pieces,
     )
 

time: 44.7 us -> 41.9 us (0.937)
  local copies, waits for them, and re-layouts: 3.78 us -> 2.23 us
  Pallas kernels: 6.96 us -> 6.36 us
    ppermute x8, waiting for transfers between devices: 11.2 us -> 10.3 us  [along_ring(): return lax.ppermute(value, ('pb', 'row'), moves)]
    dynamic_slice x1, local copies, waits for them, and re-layouts: 2.57 us -> 1.66 us  [paired_shards(): w_away = lax.dynamic_slice_in_dim(w_block, (1 - x) * chip, chip, axis=2)]
    ppermute x2, waiting for transfers between devices: 0.06 us -> 0.96 us  [other_chip(): lax.ppermute(value, 'row', [(r, r ^ CORES) for r in range(row_total)])]
    ppermute x10, starting transfers between devices: 1.96 us -> 1.17 us  [other_core(): return lax.ppermute(value, 'row', [(r, r ^ 1) for r in range(row_total)])]
    unnamed x27 -> x40, local copies, waits for them, and re-layouts: 1.21 us -> 0.57 us
    pallas_call x1, Pallas kernels: 6.96 us -> 6.36 us  [paired_shards(): pl.pallas_call(functools.partial(exchange_kernel, steps, total), out_shap...]
  transfers between devices with their start and end apart: 20 -> 20, of which waited for: 12 -> 11; matrix products, arithmetic and copies ran while one was open for 6% -> 4% of each run, Pallas kernels for 0% -> 0%
where the time goes in v2:
time: 41.9 us; the launch traced here: 41.7 us
  starting transfers between devices  18.8 us (45%)
  waiting for transfers between devices  13.4 us (32%)
  Pallas kernels  6.36 us (15%)
  local copies, waits for them, and re-layouts  2.23 us (5%)
  between operations  0.88 us (2%)
    ppermute x8, starting transfers between devices, along_ring(): return lax.ppermute(value, ('pb', 'row'), moves)  12.7 us
    ppermute x8, waiting for transfers between devices, along_ring(): return lax.ppermute(value, ('pb', 'row'), moves)  10.3 us
    pallas_call x1, Pallas kernels, paired_shards(): pl.pallas_call(functools.partial(exchange_kernel, steps, total), out_shap...  6.36 us
    ppermute x2, starting transfers between devices, other_chip(): lax.ppermute(value, 'row', [(r, r ^ CORES) for r in range(row_total)])  4.94 us
    ppermute x10, waiting for transfers between devices, other_core(): return lax.ppermute(value, 'row', [(r, r ^ 1) for r in range(row_total)])  2.13 us
    dynamic_slice x1, local copies, waits for them, and re-layouts, paired_shards(): w_away = lax.dynamic_slice_in_dim(w_block, (1 - x) * chip, chip, axis=2)  1.66 us
    ppermute x10, starting transfers between devices, other_core(): return lax.ppermute(value, 'row', [(r, r ^ 1) for r in range(row_total)])  1.17 us
    ppermute x2, waiting for transfers between devices, other_chip(): lax.ppermute(value, 'row', [(r, r ^ CORES) for r in range(row_total)])  0.96 us
  transfers between devices with their start and end apart: 20, of which 11 were waited for; matrix products, arithmetic and copies ran while one was open for 4% of the time, Pallas kernels for 0%

profile of v2, /device:TPU:0, one launch (start us, length us, event | category | flops | bytes accessed | tf_op | source)
XLA Modules:
  0.0 41.7 jit_solution(14319111389515603309)
XLA Ops:
  0.0 2.9 %collective-permute-start.4 = (bf16[320,128]{1,0:T(8,128)(2,1)}, bf16[320,128]{1,0:T(8,128)(2,1)S(1)}, u32[]{:S(2)}, u32[]{:S(2)}) collective-permute-start(bf16[320,128]{1,0:T(8,128)(2,1)} %bitcast.7), channel_id=1, source_target_pairs={{0,2},{1,3},{2,0},{3,1},{4,6},{5,7},{6,4},{7,5},{8,10},{9,11},{10,... | collective-permute-start | bytes 245768 | tf_op jit(solution)/shard_map/ppermute | solution.py:207
  3.0 1.7 %dynamic-slice_bitcast_fusion = (bf16[2,320,640]{2,1,0:T(8,128)(2,1)S(1)}, bf16[2,320,640]{2,1,0:T(8,128)(2,1)S(1)}) fusion(bf16[2,1,320,1280]{3,2,1,0:T(8,128)(2,1)} %refs_3_.1, s32[]{:T(128)S(6)} %select_n.34, s32[]{:T(128)S(6)} %select_n.30), kind=kLoop, calls=%fused_computation | loop fusion | bytes 3276808 | tf_op jit(solution)/shard_map/dynamic_slice | solution.py:231
  4.6 1.0 %collective-permute-done.4 = bf16[320,128]{1,0:T(8,128)(2,1)S(1)} collective-permute-done((bf16[320,128]{1,0:T(8,128)(2,1)}, bf16[320,128]{1,0:T(8,128)(2,1)S(1)}, u32[]{:S(2)}, u32[]{:S(2)}) %collective-permute-start.4) | collective-permute-done | bytes 81952 | tf_op jit(solution)/shard_map/ppermute | solution.py:207
  5.6 0.0 collective-permute-start.5
  5.6 2.0 %collective-permute-start.10 = (bf16[2,320,640]{2,1,0:T(8,128)(2,1)S(1)}, bf16[2,320,640]{2,1,0:T(8,128)(2,1)S(1)}, u32[]{:S(2)}, u32[]{:S(2)}) collective-permute-start(bf16[2,320,640]{2,1,0:T(8,128)(2,1)S(1)} %get-tuple-element.16), channel_id=1, source_target_pairs={{0,2},{1,3},{2,0},{3,1},{4,6},{5,7},{6,4},{7,5},{8,10},{9,11},{10,... | collective-permute-start | bytes 2457608 | tf_op jit(solution)/shard_map/ppermute | solution.py:207
  7.6 0.0 collective-permute-done
  7.7 1.6 %collective-permute-start.1 = (bf16[640,128]{1,0:T(8,128)(2,1)S(1)}, bf16[640,128]{1,0:T(8,128)(2,1)S(1)}, u32[]{:S(2)}, u32[]{:S(2)}) collective-permute-start(bf16[640,128]{1,0:T(8,128)(2,1)S(1)} %maximum_select_fusion.refs_7_), channel_id=1, source_target_pairs={{0,8},{1,5},{2,10},{3,7},{8,16},{9,1},{10,18},{11,3},{16,24},{17,9... | collective-permute-start | bytes 491528 | tf_op jit(solution)/shard_map/ppermute | solution.py:216
  9.4 1.6 %collective-permute-start.6 = (bf16[640,128]{1,0:T(8,128)(2,1)S(1)}, bf16[640,128]{1,0:T(8,128)(2,1)S(1)}, u32[]{:S(2)}, u32[]{:S(2)}) collective-permute-start(bf16[640,128]{1,0:T(8,128)(2,1)S(1)} %maximum_select_fusion.1.refs_8_), channel_id=1, source_target_pairs={{0,8},{1,5},{2,10},{3,7},{8,16},{9,1},{10,18},{11,3},{16,24},{17,9... | collective-permute-start | bytes 491528 | tf_op jit(solution)/shard_map/ppermute | solution.py:216
  11.0 2.1 %collective-permute-done.1.refs_9_ = bf16[640,128]{1,0:T(8,128)(2,1)S(1)} collective-permute-done((bf16[640,128]{1,0:T(8,128)(2,1)S(1)}, bf16[640,128]{1,0:T(8,128)(2,1)S(1)}, u32[]{:S(2)}, u32[]{:S(2)}) %collective-permute-start.1) | collective-permute-done | bytes 163872 | tf_op jit(solution)/shard_map/ppermute | solution.py:216
  13.0 1.6 %collective-permute-start.2 = (bf16[640,128]{1,0:T(8,128)(2,1)S(1)}, bf16[640,128]{1,0:T(8,128)(2,1)S(1)}, u32[]{:S(2)}, u32[]{:S(2)}) collective-permute-start(bf16[640,128]{1,0:T(8,128)(2,1)S(1)} %collective-permute-done.1.refs_9_), channel_id=1, source_target_pairs={{0,8},{1,5},{2,10},{3,7},{8,16},{9,1},{10,18},{11,3},{16,24},{17,9... | collective-permute-start | bytes 491528 | tf_op jit(solution)/shard_map/ppermute | solution.py:216
  14.6 0.2 collective-permute-done.6.refs_10_
  14.8 1.6 %collective-permute-start.11 = (bf16[640,128]{1,0:T(8,128)(2,1)S(1)}, bf16[640,128]{1,0:T(8,128)(2,1)S(1)}, u32[]{:S(2)}, u32[]{:S(2)}) collective-permute-start(bf16[640,128]{1,0:T(8,128)(2,1)S(1)} %collective-permute-done.6.refs_10_), channel_id=1, source_target_pairs={{0,8},{1,5},{2,10},{3,7},{8,16},{9,1},{10,18},{11,3},{16,24},{17,9... | collective-permute-start | bytes 491528 | tf_op jit(solution)/shard_map/ppermute | solution.py:216
  16.4 0.0 collective-permute-start.7
  16.4 2.0 %collective-permute-done.2.refs_11_ = bf16[640,128]{1,0:T(8,128)(2,1)S(1)} collective-permute-done((bf16[640,128]{1,0:T(8,128)(2,1)S(1)}, bf16[640,128]{1,0:T(8,128)(2,1)S(1)}, u32[]{:S(2)}, u32[]{:S(2)}) %collective-permute-start.2) | collective-permute-done | bytes 163872 | tf_op jit(solution)/shard_map/ppermute | solution.py:216
  18.4 1.6 %collective-permute-start.3 = (bf16[640,128]{1,0:T(8,128)(2,1)S(1)}, bf16[640,128]{1,0:T(8,128)(2,1)S(1)}, u32[]{:S(2)}, u32[]{:S(2)}) collective-permute-start(bf16[640,128]{1,0:T(8,128)(2,1)S(1)} %collective-permute-done.2.refs_11_), channel_id=1, source_target_pairs={{0,8},{1,5},{2,10},{3,7},{8,16},{9,1},{10,18},{11,3},{16,24},{17,9... | collective-permute-start | bytes 491528 | tf_op jit(solution)/shard_map/ppermute | solution.py:216
  19.9 0.0 collective-permute-start.13
  19.9 0.2 collective-permute-done.11.refs_12_
  20.1 1.6 %collective-permute-start.12 = (bf16[640,128]{1,0:T(8,128)(2,1)S(1)}, bf16[640,128]{1,0:T(8,128)(2,1)S(1)}, u32[]{:S(2)}, u32[]{:S(2)}) collective-permute-start(bf16[640,128]{1,0:T(8,128)(2,1)S(1)} %collective-permute-done.11.refs_12_), channel_id=1, source_target_pairs={{0,8},{1,5},{2,10},{3,7},{8,16},{9,1},{10,18},{11,3},{16,24},{17,9... | collective-permute-start | bytes 491528 | tf_op jit(solution)/shard_map/ppermute | solution.py:216
  21.7 2.0 %collective-permute-done.3.refs_13_ = bf16[640,128]{1,0:T(8,128)(2,1)S(1)} collective-permute-done((bf16[640,128]{1,0:T(8,128)(2,1)S(1)}, bf16[640,128]{1,0:T(8,128)(2,1)S(1)}, u32[]{:S(2)}, u32[]{:S(2)}) %collective-permute-start.3) | collective-permute-done | bytes 163872 | tf_op jit(solution)/shard_map/ppermute | solution.py:216
  23.7 1.6 %collective-permute-start.8 = (bf16[640,128]{1,0:T(8,128)(2,1)S(1)}, bf16[640,128]{1,0:T(8,128)(2,1)S(1)}, u32[]{:S(2)}, u32[]{:S(2)}) collective-permute-start(bf16[640,128]{1,0:T(8,128)(2,1)S(1)} %collective-permute-done.3.refs_13_), channel_id=1, source_target_pairs={{0,8},{1,5},{2,10},{3,7},{8,16},{9,1},{10,18},{11,3},{16,24},{17,9... | collective-permute-start | bytes 491528 | tf_op jit(solution)/shard_map/ppermute | solution.py:216
  25.3 0.2 collective-permute-done.12.refs_14_
  25.4 1.6 %collective-permute-start.14 = (bf16[640,128]{1,0:T(8,128)(2,1)S(1)}, bf16[640,128]{1,0:T(8,128)(2,1)S(1)}, u32[]{:S(2)}, u32[]{:S(2)}) collective-permute-start(bf16[640,128]{1,0:T(8,128)(2,1)S(1)} %collective-permute-done.12.refs_14_), channel_id=1, source_target_pairs={{0,8},{1,5},{2,10},{3,7},{8,16},{9,1},{10,18},{11,3},{16,24},{17,9... | collective-permute-start | bytes 491528 | tf_op jit(solution)/shard_map/ppermute | solution.py:216
  27.0 2.0 %collective-permute-done.8.refs_21_ = bf16[640,128]{1,0:T(8,128)(2,1)S(1)} collective-permute-done((bf16[640,128]{1,0:T(8,128)(2,1)S(1)}, bf16[640,128]{1,0:T(8,128)(2,1)S(1)}, u32[]{:S(2)}, u32[]{:S(2)}) %collective-permute-start.8) | collective-permute-done | bytes 163872 | tf_op jit(solution)/shard_map/ppermute | solution.py:216
  29.0 1.8 %collective-permute-done.14.refs_22_ = bf16[640,128]{1,0:T(8,128)(2,1)S(1)} collective-permute-done((bf16[640,128]{1,0:T(8,128)(2,1)S(1)}, bf16[640,128]{1,0:T(8,128)(2,1)S(1)}, u32[]{:S(2)}, u32[]{:S(2)}) %collective-permute-start.14) | collective-permute-done | bytes 163872 | tf_op jit(solution)/shard_map/ppermute | solution.py:216
  30.8 0.5 %collective-permute-start.16 = (bf16[640,128]{1,0:T(8,128)(2,1)S(1)}, bf16[640,128]{1,0:T(8,128)(2,1)S(1)}, u32[]{:S(2)}, u32[]{:S(2)}) collective-permute-start(bf16[640,128]{1,0:T(8,128)(2,1)S(1)} %collective-permute-done.2.refs_11_), channel_id=1, source_target_pairs={{0,1},{1,0},{2,3},{3,2},{4,5},{5,4},{6,7},{7,6},{8,9},{9,8},{10,11... | collective-permute-start | bytes 491528 | tf_op jit(solution)/shard_map/ppermute | solution.py:204
  31.3 0.1 collective-permute-start.17
  31.3 0.4 %collective-permute-start.18 = (bf16[640,128]{1,0:T(8,128)(2,1)S(1)}, bf16[640,128]{1,0:T(8,128)(2,1)S(1)}, u32[]{:S(2)}, u32[]{:S(2)}) collective-permute-start(bf16[640,128]{1,0:T(8,128)(2,1)S(1)} %collective-permute-done.3.refs_13_), channel_id=1, source_target_pairs={{0,1},{1,0},{2,3},{3,2},{4,5},{5,4},{6,7},{7,6},{8,9},{9,8},{10,11... | collective-permute-start | bytes 491528 | tf_op jit(solution)/shard_map/ppermute | solution.py:204
  31.8 1.5 %collective-permute-done.16.refs_17_ = bf16[640,128]{1,0:T(8,128)(2,1)S(1)} collective-permute-done((bf16[640,128]{1,0:T(8,128)(2,1)S(1)}, bf16[640,128]{1,0:T(8,128)(2,1)S(1)}, u32[]{:S(2)}, u32[]{:S(2)}) %collective-permute-start.16) | collective-permute-done | bytes 163872 | tf_op jit(solution)/shard_map/ppermute | solution.py:204
  33.3 0.1 collective-permute-start.19
  34.2 0.6 %collective-permute-done.19.refs_20_ = bf16[640,128]{1,0:T(8,128)(2,1)S(1)} collective-permute-done((bf16[640,128]{1,0:T(8,128)(2,1)S(1)}, bf16[640,128]{1,0:T(8,128)(2,1)S(1)}, u32[]{:S(2)}, u32[]{:S(2)}) %collective-permute-start.19) | collective-permute-done | bytes 163872 | tf_op jit(solution)/shard_map/ppermute | solution.py:204
  34.9 0.5 %copy-done.18 = bf16[640,128]{1,0:T(8,128)(2,1)} copy-done((bf16[640,128]{1,0:T(8,128)(2,1)}, bf16[640,128]{1,0:T(8,128)(2,1)S(1)}, u32[]{:S(2)}) %copy-start.18) | copy-done | bytes 163864
  35.4 6.4 %shard_map.55 = f32[1,3,320,128]{3,2,1,0:T(8,128)} custom-call(s32[1,2,3]{2,1,0:T(2,128)S(1)} %bitcast.6, s32[1,3]{1,0:T(1,128)S(1)} %copy-done.2, s32[1]{0:T(128)S(6)} %copy.6.refs_2_, bf16[2,1,320,1280]{3,2,1,0:T(8,128)(2,1)S(1)} %copy-done, bf16[2,320,640]{2,1,0:T(8,128)(2,1)S(1)} %collective-permute-done.9.refs_4_, ...), custom_call_target="tpu_custom_call" | custom-call | flops 1258291200 | bytes 8388608 | tf_op jit(solution)/shard_map/pallas_call | solution.py:261
  (52 shorter events, 0.2 us)
Async XLA Ops:
  0.0 5.6 %collective-permute-start.4 = (bf16[320,128]{1,0:T(8,128)(2,1)}, bf16[320,128]{1,0:T(8,128)(2,1)S(1)}, u32[]{:S(2)}, u32[]{:S(2)}) collective-permute-start(bf16[320,128]{1,0:T(8,128)(2,1)} %bitcast.7), channel_id=1, source_target_pairs={{0,2},{1,3},{2,0},{3,1},{4,6},{5,7},{6,4},{7,5},{8,10},{9,11},{10,... | collective-permute-start | bytes 245768 | tf_op jit(solution)/shard_map/ppermute | solution.py:207
  2.9 4.7 %collective-permute-start = (bf16[320,128]{1,0:T(8,128)(2,1)}, bf16[320,128]{1,0:T(8,128)(2,1)S(1)}, u32[]{:S(2)}, u32[]{:S(2)}) collective-permute-start(bf16[320,128]{1,0:T(8,128)(2,1)} %bitcast.8), channel_id=1, source_target_pairs={{0,1},{1,0},{2,3},{3,2},{4,5},{5,4},{6,7},{7,6},{8,9},{9,8},{10,11... | collective-permute-start | bytes 245768 | tf_op jit(solution)/shard_map/ppermute | solution.py:204
  2.9 32.4 %copy-start = (bf16[2,1,320,1280]{3,2,1,0:T(8,128)(2,1)S(1)}, bf16[2,1,320,1280]{3,2,1,0:T(8,128)(2,1)}, u32[]{:S(2)}) copy-start(bf16[2,1,320,1280]{3,2,1,0:T(8,128)(2,1)} %refs_3_.1) | copy-start | bytes 4915204
  2.9 32.4 %copy-start.1 = (s32[1,3,2]{1,2,0:T(2,128)S(1)}, s32[1,3,2]{1,2,0:T(2,128)}, u32[]{:S(2)}) copy-start(s32[1,3,2]{1,2,0:T(2,128)} %param.7) | copy-start | bytes 76
  3.0 32.4 %copy-start.2 = (s32[1,3]{1,0:T(1,128)S(1)}, s32[1,3]{1,0:T(1,128)}, u32[]{:S(2)}) copy-start(s32[1,3]{1,0:T(1,128)} %refs_1_.1) | copy-start | bytes 40
  5.6 3.7 %collective-permute-start.5 = (bf16[320,128]{1,0:T(8,128)(2,1)S(1)}, bf16[320,128]{1,0:T(8,128)(2,1)S(1)}, u32[]{:S(2)}, u32[]{:S(2)}) collective-permute-start(bf16[320,128]{1,0:T(8,128)(2,1)S(1)} %collective-permute-done.4), channel_id=1, source_target_pairs={{0,1},{1,0},{2,3},{3,2},{4,5},{5,4},{6,7},{7,6},{8,9},{9,8},{10,11... | collective-permute-start | bytes 245768 | tf_op jit(solution)/shard_map/ppermute | solution.py:204
  5.6 25.2 %collective-permute-start.10 = (bf16[2,320,640]{2,1,0:T(8,128)(2,1)S(1)}, bf16[2,320,640]{2,1,0:T(8,128)(2,1)S(1)}, u32[]{:S(2)}, u32[]{:S(2)}) collective-permute-start(bf16[2,320,640]{2,1,0:T(8,128)(2,1)S(1)} %get-tuple-element.16), channel_id=1, source_target_pairs={{0,2},{1,3},{2,0},{3,1},{4,6},{5,7},{6,4},{7,5},{8,10},{9,11},{10,... | collective-permute-start | bytes 2457608 | tf_op jit(solution)/shard_map/ppermute | solution.py:207
  7.7 27.1 %copy-start.3 = (bf16[640,128]{1,0:T(8,128)(2,1)}, bf16[640,128]{1,0:T(8,128)(2,1)S(1)}, u32[]{:S(2)}) copy-start(bf16[640,128]{1,0:T(8,128)(2,1)S(1)} %maximum_select_fusion.refs_7_) | copy-start | bytes 491524
  7.7 5.4 %collective-permute-start.1 = (bf16[640,128]{1,0:T(8,128)(2,1)S(1)}, bf16[640,128]{1,0:T(8,128)(2,1)S(1)}, u32[]{:S(2)}, u32[]{:S(2)}) collective-permute-start(bf16[640,128]{1,0:T(8,128)(2,1)S(1)} %maximum_select_fusion.refs_7_), channel_id=1, source_target_pairs={{0,8},{1,5},{2,10},{3,7},{8,16},{9,1},{10,18},{11,3},{16,24},{17,9... | collective-permute-start | bytes 491528 | tf_op jit(solution)/shard_map/ppermute | solution.py:216
  9.3 25.4 %copy-start.4 = (bf16[640,128]{1,0:T(8,128)(2,1)}, bf16[640,128]{1,0:T(8,128)(2,1)S(1)}, u32[]{:S(2)}) copy-start(bf16[640,128]{1,0:T(8,128)(2,1)S(1)} %maximum_select_fusion.1.refs_8_) | copy-start | bytes 491524
  9.4 5.4 %collective-permute-start.6 = (bf16[640,128]{1,0:T(8,128)(2,1)S(1)}, bf16[640,128]{1,0:T(8,128)(2,1)S(1)}, u32[]{:S(2)}, u32[]{:S(2)}) collective-permute-start(bf16[640,128]{1,0:T(8,128)(2,1)S(1)} %maximum_select_fusion.1.refs_8_), channel_id=1, source_target_pairs={{0,8},{1,5},{2,10},{3,7},{8,16},{9,1},{10,18},{11,3},{16,24},{17,9... | collective-permute-start | bytes 491528 | tf_op jit(solution)/shard_map/ppermute | solution.py:216
  13.0 21.7 %copy-start.5 = (bf16[640,128]{1,0:T(8,128)(2,1)}, bf16[640,128]{1,0:T(8,128)(2,1)S(1)}, u32[]{:S(2)}) copy-start(bf16[640,128]{1,0:T(8,128)(2,1)S(1)} %collective-permute-done.1.refs_9_) | copy-start | bytes 491524
  13.0 5.3 %collective-permute-start.2 = (bf16[640,128]{1,0:T(8,128)(2,1)S(1)}, bf16[640,128]{1,0:T(8,128)(2,1)S(1)}, u32[]{:S(2)}, u32[]{:S(2)}) collective-permute-start(bf16[640,128]{1,0:T(8,128)(2,1)S(1)} %collective-permute-done.1.refs_9_), channel_id=1, source_target_pairs={{0,8},{1,5},{2,10},{3,7},{8,16},{9,1},{10,18},{11,3},{16,24},{17,9... | collective-permute-start | bytes 491528 | tf_op jit(solution)/shard_map/ppermute | solution.py:216
  14.8 20.0 %copy-start.6 = (bf16[640,128]{1,0:T(8,128)(2,1)}, bf16[640,128]{1,0:T(8,128)(2,1)S(1)}, u32[]{:S(2)}) copy-start(bf16[640,128]{1,0:T(8,128)(2,1)S(1)} %collective-permute-done.6.refs_10_) | copy-start | bytes 491524
  14.8 5.3 %collective-permute-start.11 = (bf16[640,128]{1,0:T(8,128)(2,1)S(1)}, bf16[640,128]{1,0:T(8,128)(2,1)S(1)}, u32[]{:S(2)}, u32[]{:S(2)}) collective-permute-start(bf16[640,128]{1,0:T(8,128)(2,1)S(1)} %collective-permute-done.6.refs_10_), channel_id=1, source_target_pairs={{0,8},{1,5},{2,10},{3,7},{8,16},{9,1},{10,18},{11,3},{16,24},{17,9... | collective-permute-start | bytes 491528 | tf_op jit(solution)/shard_map/ppermute | solution.py:216
  16.4 5.3 %collective-permute-start.7 = (bf16[640,128]{1,0:T(8,128)(2,1)S(1)}, bf16[640,128]{1,0:T(8,128)(2,1)S(1)}, u32[]{:S(2)}, u32[]{:S(2)}) collective-permute-start(bf16[640,128]{1,0:T(8,128)(2,1)S(1)} %collective-permute-done.6.refs_10_), channel_id=1, source_target_pairs={{0,1},{1,0},{2,3},{3,2},{4,5},{5,4},{6,7},{7,6},{8,9},{9,8},{10,11... | collective-permute-start | bytes 491528 | tf_op jit(solution)/shard_map/ppermute | solution.py:204
  18.4 16.4 %copy-start.7 = (bf16[640,128]{1,0:T(8,128)(2,1)}, bf16[640,128]{1,0:T(8,128)(2,1)S(1)}, u32[]{:S(2)}) copy-start(bf16[640,128]{1,0:T(8,128)(2,1)S(1)} %collective-permute-done.2.refs_11_) | copy-start | bytes 491524
  18.4 5.3 %collective-permute-start.3 = (bf16[640,128]{1,0:T(8,128)(2,1)S(1)}, bf16[640,128]{1,0:T(8,128)(2,1)S(1)}, u32[]{:S(2)}, u32[]{:S(2)}) collective-permute-start(bf16[640,128]{1,0:T(8,128)(2,1)S(1)} %collective-permute-done.2.refs_11_), channel_id=1, source_target_pairs={{0,8},{1,5},{2,10},{3,7},{8,16},{9,1},{10,18},{11,3},{16,24},{17,9... | collective-permute-start | bytes 491528 | tf_op jit(solution)/shard_map/ppermute | solution.py:216
  19.9 5.3 %collective-permute-start.13 = (bf16[640,128]{1,0:T(8,128)(2,1)S(1)}, bf16[640,128]{1,0:T(8,128)(2,1)S(1)}, u32[]{:S(2)}, u32[]{:S(2)}) collective-permute-start(bf16[640,128]{1,0:T(8,128)(2,1)S(1)} %collective-permute-done.1.refs_9_), channel_id=1, source_target_pairs={{0,1},{1,0},{2,3},{3,2},{4,5},{5,4},{6,7},{7,6},{8,9},{9,8},{10,11... | collective-permute-start | bytes 491528 | tf_op jit(solution)/shard_map/ppermute | solution.py:204
  20.1 14.7 %copy-start.8 = (bf16[640,128]{1,0:T(8,128)(2,1)}, bf16[640,128]{1,0:T(8,128)(2,1)S(1)}, u32[]{:S(2)}) copy-start(bf16[640,128]{1,0:T(8,128)(2,1)S(1)} %collective-permute-done.11.refs_12_) | copy-start | bytes 491524
  20.1 5.3 %collective-permute-start.12 = (bf16[640,128]{1,0:T(8,128)(2,1)S(1)}, bf16[640,128]{1,0:T(8,128)(2,1)S(1)}, u32[]{:S(2)}, u32[]{:S(2)}) collective-permute-start(bf16[640,128]{1,0:T(8,128)(2,1)S(1)} %collective-permute-done.11.refs_12_), channel_id=1, source_target_pairs={{0,8},{1,5},{2,10},{3,7},{8,16},{9,1},{10,18},{11,3},{16,24},{17,9... | collective-permute-start | bytes 491528 | tf_op jit(solution)/shard_map/ppermute | solution.py:216
  21.7 13.1 %copy-start.9 = (bf16[640,128]{1,0:T(8,128)(2,1)}, bf16[640,128]{1,0:T(8,128)(2,1)S(1)}, u32[]{:S(2)}) copy-start(bf16[640,128]{1,0:T(8,128)(2,1)S(1)} %collective-permute-done.7.refs_16_) | copy-start | bytes 491524
  23.7 11.1 %copy-start.10 = (bf16[640,128]{1,0:T(8,128)(2,1)}, bf16[640,128]{1,0:T(8,128)(2,1)S(1)}, u32[]{:S(2)}) copy-start(bf16[640,128]{1,0:T(8,128)(2,1)S(1)} %collective-permute-done.3.refs_13_) | copy-start | bytes 491524
  23.7 5.3 %collective-permute-start.8 = (bf16[640,128]{1,0:T(8,128)(2,1)S(1)}, bf16[640,128]{1,0:T(8,128)(2,1)S(1)}, u32[]{:S(2)}, u32[]{:S(2)}) collective-permute-start(bf16[640,128]{1,0:T(8,128)(2,1)S(1)} %collective-permute-done.3.refs_13_), channel_id=1, source_target_pairs={{0,8},{1,5},{2,10},{3,7},{8,16},{9,1},{10,18},{11,3},{16,24},{17,9... | collective-permute-start | bytes 491528 | tf_op jit(solution)/shard_map/ppermute | solution.py:216
  25.3 9.6 %copy-start.11 = (bf16[640,128]{1,0:T(8,128)(2,1)}, bf16[640,128]{1,0:T(8,128)(2,1)S(1)}, u32[]{:S(2)}) copy-start(bf16[640,128]{1,0:T(8,128)(2,1)S(1)} %collective-permute-done.13.refs_15_) | copy-start | bytes 491524
  25.4 5.3 %collective-permute-start.14 = (bf16[640,128]{1,0:T(8,128)(2,1)S(1)}, bf16[640,128]{1,0:T(8,128)(2,1)S(1)}, u32[]{:S(2)}, u32[]{:S(2)}) collective-permute-start(bf16[640,128]{1,0:T(8,128)(2,1)S(1)} %collective-permute-done.12.refs_14_), channel_id=1, source_target_pairs={{0,8},{1,5},{2,10},{3,7},{8,16},{9,1},{10,18},{11,3},{16,24},{17,9... | collective-permute-start | bytes 491528 | tf_op jit(solution)/shard_map/ppermute | solution.py:216
  29.0 5.7 %collective-permute-start.9 = (bf16[2,320,640]{2,1,0:T(8,128)(2,1)S(1)}, bf16[2,320,640]{2,1,0:T(8,128)(2,1)S(1)}, u32[]{:S(2)}, u32[]{:S(2)}) collective-permute-start(bf16[2,320,640]{2,1,0:T(8,128)(2,1)S(1)} %get-tuple-element.15), channel_id=1, source_target_pairs={{0,1},{1,0},{2,3},{3,2},{4,5},{5,4},{6,7},{7,6},{8,9},{9,8},{10,11... | collective-permute-start | bytes 2457608 | tf_op jit(solution)/shard_map/ppermute | solution.py:204
  30.8 4.0 %collective-permute-start.15 = (bf16[2,320,640]{2,1,0:T(8,128)(2,1)S(1)}, bf16[2,320,640]{2,1,0:T(8,128)(2,1)S(1)}, u32[]{:S(2)}, u32[]{:S(2)}) collective-permute-start(bf16[2,320,640]{2,1,0:T(8,128)(2,1)S(1)} %collective-permute-done.10.refs_5_), channel_id=1, source_target_pairs={{0,1},{1,0},{2,3},{3,2},{4,5},{5,4},{6,7},{7,6},{8,9},{9,8},{10,11... | collective-permute-start | bytes 2457608 | tf_op jit(solution)/shard_map/ppermute | solution.py:204
  30.8 2.6 %collective-permute-start.16 = (bf16[640,128]{1,0:T(8,128)(2,1)S(1)}, bf16[640,128]{1,0:T(8,128)(2,1)S(1)}, u32[]{:S(2)}, u32[]{:S(2)}) collective-permute-start(bf16[640,128]{1,0:T(8,128)(2,1)S(1)} %collective-permute-done.2.refs_11_), channel_id=1, source_target_pairs={{0,1},{1,0},{2,3},{3,2},{4,5},{5,4},{6,7},{7,6},{8,9},{9,8},{10,11... | collective-permute-start | bytes 491528 | tf_op jit(solution)/shard_map/ppermute | solution.py:204
  31.3 2.8 %collective-permute-start.17 = (bf16[640,128]{1,0:T(8,128)(2,1)S(1)}, bf16[640,128]{1,0:T(8,128)(2,1)S(1)}, u32[]{:S(2)}, u32[]{:S(2)}) collective-permute-start(bf16[640,128]{1,0:T(8,128)(2,1)S(1)} %collective-permute-done.11.refs_12_), channel_id=1, source_target_pairs={{0,1},{1,0},{2,3},{3,2},{4,5},{5,4},{6,7},{7,6},{8,9},{9,8},{10,11... | collective-permute-start | bytes 491528 | tf_op jit(solution)/shard_map/ppermute | solution.py:204
  31.3 2.8 %collective-permute-start.18 = (bf16[640,128]{1,0:T(8,128)(2,1)S(1)}, bf16[640,128]{1,0:T(8,128)(2,1)S(1)}, u32[]{:S(2)}, u32[]{:S(2)}) collective-permute-start(bf16[640,128]{1,0:T(8,128)(2,1)S(1)} %collective-permute-done.3.refs_13_), channel_id=1, source_target_pairs={{0,1},{1,0},{2,3},{3,2},{4,5},{5,4},{6,7},{7,6},{8,9},{9,8},{10,11... | collective-permute-start | bytes 491528 | tf_op jit(solution)/shard_map/ppermute | solution.py:204
  33.3 1.4 %collective-permute-start.19 = (bf16[640,128]{1,0:T(8,128)(2,1)S(1)}, bf16[640,128]{1,0:T(8,128)(2,1)S(1)}, u32[]{:S(2)}, u32[]{:S(2)}) collective-permute-start(bf16[640,128]{1,0:T(8,128)(2,1)S(1)} %collective-permute-done.12.refs_14_), channel_id=1, source_target_pairs={{0,1},{1,0},{2,3},{3,2},{4,5},{5,4},{6,7},{7,6},{8,9},{9,8},{10,11... | collective-permute-start | bytes 491528 | tf_op jit(solution)/shard_map/ppermute | solution.py:204
  (8 other events, 27.6 us)

commit v3 on v2

--- a/solution.py
+++ b/solution.py
@@ -84,7 +84,7 @@
     ring, refs = refs[: 2 * steps], refs[2 * steps :]
     swap, refs = refs[: 2 * steps], refs[2 * steps :]
     last, refs = refs[:2], refs[2:]
-    out, eff, full, w_sem, orb_sem = refs
+    out, eff, full, orb_sem = refs
     slots, rows, width = out.shape[1:]
     points = full.shape[2]
     chip = 2 * rows
@@ -122,8 +122,6 @@
         ).wait()
 
     fetch(0)
-    eff_copy = pltpu.make_async_copy(w_own.at[:, 0], eff.at[0], w_sem)
-    eff_copy.start()
     for slot in range(1, slots):
         fetch(slot)
     any_turned = False
@@ -140,46 +138,48 @@
             skip = core * (wide - rows)
             for block, lanes, at in (
                 (w_own.at[:, 0], pl.ds(start, wide), core * rows),
-                (w_core, slice(first, first + wide), (1 - core) * rows),
+                (w_core, slice(0, wide), (1 - core) * rows),
                 (w_far, slice(first, first + wide), chip + core * rows),
                 (w_far_core, slice(first, first + wide), chip + (1 - core) * rows),
             ):
-                eff[1, 0, :, at : at + rows] = block[0, :, lanes].T[skip : skip + rows]
-                eff[1, 1, :, at : at + rows] = -block[1, :, lanes].T[skip : skip + rows]
-
-    eff_copy.wait()
+                eff[0, :, at : at + rows] = block[0, :, lanes].T[skip : skip + rows]
+                eff[1, :, at : at + rows] = -block[1, :, lanes].T[skip : skip + rows]
+
+    def apply(slot, w_real, w_imag, mine):
+        local = full[1, slot, pl.ds(pl.multiple_of(mine * rows, rows), rows)]
+        left = jnp.concatenate([local, rotated(local)], axis=0)
+        step = 128
+        result = jnp.zeros((rows, width), jnp.float32)
+        for at in range(0, points, step):
+            dens = lax.dot_general(
+                left,
+                full[1, slot, at : at + step],
+                (((1,), (1,)), ((), ())),
+                preferred_element_type=jnp.float32,
+            )
+            dens_real, dens_imag = dens[:rows], dens[rows:]
+            eff_real = w_real[:, at : at + step].astype(jnp.float32)
+            eff_imag = w_imag[:, at : at + step].astype(jnp.float32)
+            kern_real = (eff_real * dens_real - eff_imag * dens_imag).astype(jnp.bfloat16)
+            kern_imag = (eff_real * dens_imag + eff_imag * dens_real).astype(jnp.bfloat16)
+            target = full[0, slot, at : at + step]
+            result += jnp.dot(kern_real, target, preferred_element_type=jnp.float32)
+            result += jnp.dot(kern_imag, -rotated(target), preferred_element_type=jnp.float32)
+        out[0, slot] = result
 
     def compute(slot, carry):
         arrive(1, slot)
         arrive(0, slot)
         live = slot < counts[0]
-
-        @pl.when(live)
+        turned = flags[0, slot] == 1
+
+        @pl.when(jnp.logical_and(live, jnp.logical_not(turned)))
         def _():
-            flag = flags[0, slot]
-            mine = pl.multiple_of(jnp.where(flag == 1, c, 2 * x + c) * rows, rows)
-            local = full[1, slot, pl.ds(mine, rows)]
-            left = jnp.concatenate([local, rotated(local)], axis=0)
-            step = 128
-            result = jnp.zeros((rows, width), jnp.float32)
-            for at in range(0, points, step):
-                dens = lax.dot_general(
-                    left,
-                    full[1, slot, at : at + step],
-                    (((1,), (1,)), ((), ())),
-                    preferred_element_type=jnp.float32,
-                )
-                dens_real, dens_imag = dens[:rows], dens[rows:]
-                eff_real = eff[flag, 0, :, at : at + step].astype(jnp.float32)
-                eff_imag = eff[flag, 1, :, at : at + step].astype(jnp.float32)
-                kern_real = (eff_real * dens_real - eff_imag * dens_imag).astype(jnp.bfloat16)
-                kern_imag = (eff_real * dens_imag + eff_imag * dens_real).astype(jnp.bfloat16)
-                target = full[0, slot, at : at + step]
-                result += jnp.dot(kern_real, target, preferred_element_type=jnp.float32)
-                result += jnp.dot(
-                    kern_imag, -rotated(target), preferred_element_type=jnp.float32
-                )
-            out[0, slot] = result
+            apply(slot, w_own.at[0, 0], w_own.at[1, 0], 2 * x + c)
+
+        @pl.when(jnp.logical_and(live, turned))
+        def _():
+            apply(slot, eff.at[0], eff.at[1], c)
 
         @pl.when(jnp.logical_not(live))
         def _():
@@ -234,21 +234,25 @@
     steps = total // 2 - 1
     first, second = [near[0]], [near[1]]
     swap_first, swap_second = [], []
+    wide = rows + 64
+    w_mine = lax.dynamic_slice_in_dim(w_block, x * chip + (1 - c) * (chip - wide), wide, axis=2)
     for k in range(steps + 1):
+        if k == 1:
+            w_core = other_core(after(w_mine, first[1]))
         if k >= 2:
             swap_first.append(other_core(first[k - 1]))
             swap_second.append(other_core(second[k - 1]))
-        first.append(along_ring(after(first[-1], swap_second[0]) if k == 3 else first[-1]))
-        second.append(along_ring(after(second[-1], swap_first[0]) if k == 3 else second[-1]))
+        ahead = [*second[k - 1 : k], *(swap_second[:1] if k == 3 else [])] if k else []
+        behind = [first[k], *([w_core, *swap_first[:1]] if k == 3 else [])] if k else []
+        first.append(along_ring(after(first[k], *ahead)))
+        second.append(along_ring(after(second[k], *behind)))
     ring = [wave[k] for k in range(1, steps + 1) for wave in (first, second)]
     last = [first[steps + 1], second[steps + 1]]
     for k in range(len(swap_first) + 1, steps + 1):
         swap_first.append(other_core(after(first[k], last[0])))
-        swap_second.append(other_core(after(second[k], last[1])))
+        swap_second.append(other_core(after(second[k], *last)))
     swap = [wave[k] for k in range(steps) for wave in (swap_first, swap_second)]
-    w_far_core = other_core(after(w_far, last[1]))
-    w_mine = lax.dynamic_slice_in_dim(w_block, x * chip, chip, axis=2)
-    w_core = other_core(after(w_mine, last[0]))
+    w_far_core = other_core(after(w_far, *last))
 
     in_hbm = pl.BlockSpec(memory_space=pltpu.HBM)
     in_vmem = pl.BlockSpec(memory_space=pltpu.VMEM)
@@ -264,9 +268,8 @@
         in_specs=[scalars] * 3 + [in_vmem] * 4 + [in_hbm] * len(pieces),
         out_specs=in_vmem,
         scratch_shapes=[
-            pltpu.VMEM((2, 2, rows, points), jnp.bfloat16),
+            pltpu.VMEM((2, rows, points), jnp.bfloat16),
             pltpu.VMEM((2, slots, points, width), jnp.bfloat16),
-            pltpu.SemaphoreType.DMA,
             pltpu.SemaphoreType.DMA((2, slots)),
         ],
         compiler_params=pltpu.CompilerParams(vmem_limit_bytes=24 * 2**20),

time: 41.9 us -> 41.3 us (0.986)
  waiting for transfers between devices: 13.4 us -> 12 us
  starting transfers between devices: 18.8 us -> 19.9 us
    ppermute x8, starting transfers between devices: 12.7 us -> 14.3 us  [along_ring(): return lax.ppermute(value, ('pb', 'row'), moves)]
    ppermute x8, waiting for transfers between devices: 10.3 us -> 9 us  [along_ring(): return lax.ppermute(value, ('pb', 'row'), moves)]
    ppermute x10, waiting for transfers between devices: 2.13 us -> 1.53 us  [other_core(): return lax.ppermute(value, 'row', [(r, r ^ 1) for r in range(row_total)])]
    ppermute x2, starting transfers between devices: 4.94 us -> 4.43 us  [other_chip(): lax.ppermute(value, 'row', [(r, r ^ CORES) for r in range(row_total)])]
    ppermute x2, waiting for transfers between devices: 0.96 us -> 1.47 us  [other_chip(): lax.ppermute(value, 'row', [(r, r ^ CORES) for r in range(row_total)])]
    dynamic_slice x1, local copies, waits for them, and re-layouts: 1.66 us -> 1.24 us  [paired_shards(): w_away = lax.dynamic_slice_in_dim(w_block, (1 - x) * chip, chip, axis=2)]
  transfers between devices with their start and end apart: 20 -> 20, of which waited for: 11 -> 13; matrix products, arithmetic and copies ran while one was open for 4% -> 3% of each run, Pallas kernels for 0% -> 0%
where the time goes in v3:
time: 41.3 us; the launch traced here: 41.2 us
  starting transfers between devices  19.9 us (48%)
  waiting for transfers between devices  12 us (29%)
  Pallas kernels  6.46 us (16%)
  local copies, waits for them, and re-layouts  1.89 us (5%)
  between operations  0.84 us (2%)
    ppermute x8, starting transfers between devices, along_ring(): return lax.ppermute(value, ('pb', 'row'), moves)  14.3 us
    ppermute x8, waiting for transfers between devices, along_ring(): return lax.ppermute(value, ('pb', 'row'), moves)  9 us
    pallas_call x1, Pallas kernels, paired_shards(): pl.pallas_call(functools.partial(exchange_kernel, steps, total), out_shap...  6.46 us
    ppermute x2, starting transfers between devices, other_chip(): lax.ppermute(value, 'row', [(r, r ^ CORES) for r in range(row_total)])  4.43 us
    ppermute x10, waiting for transfers between devices, other_core(): return lax.ppermute(value, 'row', [(r, r ^ 1) for r in range(row_total)])  1.53 us
    ppermute x2, waiting for transfers between devices, other_chip(): lax.ppermute(value, 'row', [(r, r ^ CORES) for r in range(row_total)])  1.47 us
    dynamic_slice x1, local copies, waits for them, and re-layouts, paired_shards(): w_away = lax.dynamic_slice_in_dim(w_block, (1 - x) * chip, chip, axis=2)  1.24 us
    ppermute x10, starting transfers between devices, other_core(): return lax.ppermute(value, 'row', [(r, r ^ 1) for r in range(row_total)])  1.13 us
  transfers between devices with their start and end apart: 20, of which 13 were waited for; matrix products, arithmetic and copies ran while one was open for 3% of the time, Pallas kernels for 0%

profile of v3, /device:TPU:0, one launch (start us, length us, event | category | flops | bytes accessed | tf_op | source)
XLA Modules:
  0.0 41.2 jit_solution(15044376610320201201)
XLA Ops:
  0.0 2.9 %collective-permute-start.3 = (bf16[320,128]{1,0:T(8,128)(2,1)}, bf16[320,128]{1,0:T(8,128)(2,1)S(1)}, u32[]{:S(2)}, u32[]{:S(2)}) collective-permute-start(bf16[320,128]{1,0:T(8,128)(2,1)} %bitcast.7), channel_id=1, source_target_pairs={{0,2},{1,3},{2,0},{3,1},{4,6},{5,7},{6,4},{7,5},{8,10},{9,11},{10,... | collective-permute-start | bytes 245768 | tf_op jit(solution)/shard_map/ppermute | solution.py:207
  3.0 1.2 %dynamic-slice_bitcast_fusion = bf16[2,320,640]{2,1,0:T(8,128)(2,1)S(1)} fusion(bf16[2,1,320,1280]{3,2,1,0:T(8,128)(2,1)} %refs_3_.1, s32[]{:T(128)S(6)} %select_n.34), kind=kLoop, calls=%fused_computation | loop fusion | bytes 1638404 | tf_op jit(solution)/shard_map/dynamic_slice | solution.py:231
  4.2 1.5 %collective-permute-done.3 = bf16[320,128]{1,0:T(8,128)(2,1)S(1)} collective-permute-done((bf16[320,128]{1,0:T(8,128)(2,1)}, bf16[320,128]{1,0:T(8,128)(2,1)S(1)}, u32[]{:S(2)}, u32[]{:S(2)}) %collective-permute-start.3) | collective-permute-done | bytes 81952 | tf_op jit(solution)/shard_map/ppermute | solution.py:207
  5.7 2.1 %collective-permute-start.1 = (bf16[640,128]{1,0:T(8,128)(2,1)S(1)}, bf16[640,128]{1,0:T(8,128)(2,1)S(1)}, u32[]{:S(2)}, u32[]{:S(2)}) collective-permute-start(bf16[640,128]{1,0:T(8,128)(2,1)S(1)} %maximum_select_fusion.refs_7_), channel_id=1, source_target_pairs={{0,8},{1,5},{2,10},{3,7},{8,16},{9,1},{10,18},{11,3},{16,24},{17,9... | collective-permute-start | bytes 491528 | tf_op jit(solution)/shard_map/ppermute | solution.py:216
  7.8 1.5 %collective-permute-start.4 = (bf16[2,320,640]{2,1,0:T(8,128)(2,1)S(1)}, bf16[2,320,640]{2,1,0:T(8,128)(2,1)S(1)}, u32[]{:S(2)}, u32[]{:S(2)}) collective-permute-start(bf16[2,320,640]{2,1,0:T(8,128)(2,1)S(1)} %dynamic-slice_bitcast_fusion), channel_id=1, source_target_pairs={{0,2},{1,3},{2,0},{3,1},{4,6},{5,7},{6,4},{7,5},{8,10},{9,11},{10,... | collective-permute-start | bytes 2457608 | tf_op jit(solution)/shard_map/ppermute | solution.py:207
  9.4 1.6 %collective-permute-start.7 = (bf16[640,128]{1,0:T(8,128)(2,1)S(1)}, bf16[640,128]{1,0:T(8,128)(2,1)S(1)}, u32[]{:S(2)}, u32[]{:S(2)}) collective-permute-start(bf16[640,128]{1,0:T(8,128)(2,1)S(1)} %maximum_select_fusion.1.refs_8_), channel_id=1, source_target_pairs={{0,8},{1,5},{2,10},{3,7},{8,16},{9,1},{10,18},{11,3},{16,24},{17,9... | collective-permute-start | bytes 491528 | tf_op jit(solution)/shard_map/ppermute | solution.py:216
  11.0 0.1 collective-permute-done.1.refs_9_
  11.1 2.0 %collective-permute-start.6 = (bf16[640,128]{1,0:T(8,128)(2,1)S(1)}, bf16[640,128]{1,0:T(8,128)(2,1)S(1)}, u32[]{:S(2)}, u32[]{:S(2)}) collective-permute-start(bf16[640,128]{1,0:T(8,128)(2,1)S(1)} %collective-permute-done.1.refs_9_), channel_id=1, source_target_pairs={{0,8},{1,5},{2,10},{3,7},{8,16},{9,1},{10,18},{11,3},{16,24},{17,9... | collective-permute-start | bytes 491528 | tf_op jit(solution)/shard_map/ppermute | solution.py:216
  13.1 1.6 %collective-permute-done.7.refs_10_ = bf16[640,128]{1,0:T(8,128)(2,1)S(1)} collective-permute-done((bf16[640,128]{1,0:T(8,128)(2,1)S(1)}, bf16[640,128]{1,0:T(8,128)(2,1)S(1)}, u32[]{:S(2)}, u32[]{:S(2)}) %collective-permute-start.7) | collective-permute-done | bytes 163872 | tf_op jit(solution)/shard_map/ppermute | solution.py:216
  14.7 1.6 %collective-permute-start.9 = (bf16[640,128]{1,0:T(8,128)(2,1)S(1)}, bf16[640,128]{1,0:T(8,128)(2,1)S(1)}, u32[]{:S(2)}, u32[]{:S(2)}) collective-permute-start(bf16[640,128]{1,0:T(8,128)(2,1)S(1)} %collective-permute-done.7.refs_10_), channel_id=1, source_target_pairs={{0,8},{1,5},{2,10},{3,7},{8,16},{9,1},{10,18},{11,3},{16,24},{17,9... | collective-permute-start | bytes 491528 | tf_op jit(solution)/shard_map/ppermute | solution.py:216
  16.3 0.2 collective-permute-done.6.refs_11_
  16.5 1.9 %collective-permute-start.8 = (bf16[640,128]{1,0:T(8,128)(2,1)S(1)}, bf16[640,128]{1,0:T(8,128)(2,1)S(1)}, u32[]{:S(2)}, u32[]{:S(2)}) collective-permute-start(bf16[640,128]{1,0:T(8,128)(2,1)S(1)} %collective-permute-done.6.refs_11_), channel_id=1, source_target_pairs={{0,8},{1,5},{2,10},{3,7},{8,16},{9,1},{10,18},{11,3},{16,24},{17,9... | collective-permute-start | bytes 491528 | tf_op jit(solution)/shard_map/ppermute | solution.py:216
  18.5 1.6 %collective-permute-done.9.refs_12_ = bf16[640,128]{1,0:T(8,128)(2,1)S(1)} collective-permute-done((bf16[640,128]{1,0:T(8,128)(2,1)S(1)}, bf16[640,128]{1,0:T(8,128)(2,1)S(1)}, u32[]{:S(2)}, u32[]{:S(2)}) %collective-permute-start.9) | collective-permute-done | bytes 163872 | tf_op jit(solution)/shard_map/ppermute | solution.py:216
  20.1 1.6 %collective-permute-start.12 = (bf16[640,128]{1,0:T(8,128)(2,1)S(1)}, bf16[640,128]{1,0:T(8,128)(2,1)S(1)}, u32[]{:S(2)}, u32[]{:S(2)}) collective-permute-start(bf16[640,128]{1,0:T(8,128)(2,1)S(1)} %collective-permute-done.9.refs_12_), channel_id=1, source_target_pairs={{0,8},{1,5},{2,10},{3,7},{8,16},{9,1},{10,18},{11,3},{16,24},{17,9... | collective-permute-start | bytes 491528 | tf_op jit(solution)/shard_map/ppermute | solution.py:216
  21.7 0.1 collective-permute-done.8.refs_13_
  21.8 1.9 %collective-permute-start.11 = (bf16[640,128]{1,0:T(8,128)(2,1)S(1)}, bf16[640,128]{1,0:T(8,128)(2,1)S(1)}, u32[]{:S(2)}, u32[]{:S(2)}) collective-permute-start(bf16[640,128]{1,0:T(8,128)(2,1)S(1)} %collective-permute-done.8.refs_13_), channel_id=1, source_target_pairs={{0,8},{1,5},{2,10},{3,7},{8,16},{9,1},{10,18},{11,3},{16,24},{17,9... | collective-permute-start | bytes 491528 | tf_op jit(solution)/shard_map/ppermute | solution.py:216
  23.8 1.7 %collective-permute-done.12.refs_14_ = bf16[640,128]{1,0:T(8,128)(2,1)S(1)} collective-permute-done((bf16[640,128]{1,0:T(8,128)(2,1)S(1)}, bf16[640,128]{1,0:T(8,128)(2,1)S(1)}, u32[]{:S(2)}, u32[]{:S(2)}) %collective-permute-start.12) | collective-permute-done | bytes 163872 | tf_op jit(solution)/shard_map/ppermute | solution.py:216
  25.5 1.6 %collective-permute-start.14 = (bf16[640,128]{1,0:T(8,128)(2,1)S(1)}, bf16[640,128]{1,0:T(8,128)(2,1)S(1)}, u32[]{:S(2)}, u32[]{:S(2)}) collective-permute-start(bf16[640,128]{1,0:T(8,128)(2,1)S(1)} %collective-permute-done.12.refs_14_), channel_id=1, source_target_pairs={{0,8},{1,5},{2,10},{3,7},{8,16},{9,1},{10,18},{11,3},{16,24},{17,9... | collective-permute-start | bytes 491528 | tf_op jit(solution)/shard_map/ppermute | solution.py:216
  27.0 0.2 collective-permute-done.11.refs_21_
  27.2 3.6 %collective-permute-done.14.refs_22_ = bf16[640,128]{1,0:T(8,128)(2,1)S(1)} collective-permute-done((bf16[640,128]{1,0:T(8,128)(2,1)S(1)}, bf16[640,128]{1,0:T(8,128)(2,1)S(1)}, u32[]{:S(2)}, u32[]{:S(2)}) %collective-permute-start.14) | collective-permute-done | bytes 163872 | tf_op jit(solution)/shard_map/ppermute | solution.py:216
  30.8 0.5 %collective-permute-start.16 = (bf16[640,128]{1,0:T(8,128)(2,1)S(1)}, bf16[640,128]{1,0:T(8,128)(2,1)S(1)}, u32[]{:S(2)}, u32[]{:S(2)}) collective-permute-start(bf16[640,128]{1,0:T(8,128)(2,1)S(1)} %collective-permute-done.6.refs_11_), channel_id=1, source_target_pairs={{0,1},{1,0},{2,3},{3,2},{4,5},{5,4},{6,7},{7,6},{8,9},{9,8},{10,11... | collective-permute-start | bytes 491528 | tf_op jit(solution)/shard_map/ppermute | solution.py:204
  31.3 0.1 collective-permute-start.17
  31.4 0.4 %collective-permute-start.18 = (bf16[640,128]{1,0:T(8,128)(2,1)S(1)}, bf16[640,128]{1,0:T(8,128)(2,1)S(1)}, u32[]{:S(2)}, u32[]{:S(2)}) collective-permute-start(bf16[640,128]{1,0:T(8,128)(2,1)S(1)} %collective-permute-done.8.refs_13_), channel_id=1, source_target_pairs={{0,1},{1,0},{2,3},{3,2},{4,5},{5,4},{6,7},{7,6},{8,9},{9,8},{10,11... | collective-permute-start | bytes 491528 | tf_op jit(solution)/shard_map/ppermute | solution.py:204
  31.8 0.1 collective-permute-start.19
  32.5 0.8 %collective-permute-done.16.refs_17_ = bf16[640,128]{1,0:T(8,128)(2,1)S(1)} collective-permute-done((bf16[640,128]{1,0:T(8,128)(2,1)S(1)}, bf16[640,128]{1,0:T(8,128)(2,1)S(1)}, u32[]{:S(2)}, u32[]{:S(2)}) %collective-permute-start.16) | collective-permute-done | bytes 163872 | tf_op jit(solution)/shard_map/ppermute | solution.py:204
  33.3 0.2 collective-permute-done.17.refs_18_
  33.6 0.2 collective-permute-done.18.refs_19_
  33.8 0.2 collective-permute-done.19.refs_20_
  34.2 0.1 copy-done.16
  34.2 0.2 copy-done.17
  34.5 0.2 copy-done.18
  34.7 6.5 %shard_map.55 = f32[1,3,320,128]{3,2,1,0:T(8,128)} custom-call(s32[1,2,3]{2,1,0:T(2,128)S(1)} %bitcast.6, s32[1,3]{1,0:T(1,128)S(1)} %copy-done.2, s32[1]{0:T(128)S(6)} %copy.6.refs_2_, bf16[2,1,320,1280]{3,2,1,0:T(8,128)(2,1)S(1)} %copy-done, bf16[2,320,384]{2,1,0:T(8,128)(2,1)S(1)} %collective-permute-done.2.refs_4_, ...), custom_call_target="tpu_custom_call" | custom-call | flops 1258291200 | bytes 8388608 | tf_op jit(solution)/shard_map/pallas_call | solution.py:265
  (53 shorter events, 0.3 us)
Async XLA Ops:
  0.0 11.0 %copy-start = (bf16[2,1,320,1280]{3,2,1,0:T(8,128)(2,1)S(1)}, bf16[2,1,320,1280]{3,2,1,0:T(8,128)(2,1)}, u32[]{:S(2)}) copy-start(bf16[2,1,320,1280]{3,2,1,0:T(8,128)(2,1)} %refs_3_.1) | copy-start | bytes 4915204
  0.0 5.7 %collective-permute-start.3 = (bf16[320,128]{1,0:T(8,128)(2,1)}, bf16[320,128]{1,0:T(8,128)(2,1)S(1)}, u32[]{:S(2)}, u32[]{:S(2)}) collective-permute-start(bf16[320,128]{1,0:T(8,128)(2,1)} %bitcast.7), channel_id=1, source_target_pairs={{0,2},{1,3},{2,0},{3,1},{4,6},{5,7},{6,4},{7,5},{8,10},{9,11},{10,... | collective-permute-start | bytes 245768 | tf_op jit(solution)/shard_map/ppermute | solution.py:207
  2.9 2.7 %collective-permute-start = (bf16[320,128]{1,0:T(8,128)(2,1)}, bf16[320,128]{1,0:T(8,128)(2,1)S(1)}, u32[]{:S(2)}, u32[]{:S(2)}) collective-permute-start(bf16[320,128]{1,0:T(8,128)(2,1)} %bitcast.8), channel_id=1, source_target_pairs={{0,1},{1,0},{2,3},{3,2},{4,5},{5,4},{6,7},{7,6},{8,9},{9,8},{10,11... | collective-permute-start | bytes 245768 | tf_op jit(solution)/shard_map/ppermute | solution.py:204
  2.9 31.8 %copy-start.1 = (s32[1,3,2]{1,2,0:T(2,128)S(1)}, s32[1,3,2]{1,2,0:T(2,128)}, u32[]{:S(2)}) copy-start(s32[1,3,2]{1,2,0:T(2,128)} %param.7) | copy-start | bytes 76
  2.9 31.8 %copy-start.2 = (s32[1,3]{1,0:T(1,128)S(1)}, s32[1,3]{1,0:T(1,128)}, u32[]{:S(2)}) copy-start(s32[1,3]{1,0:T(1,128)} %refs_1_.1) | copy-start | bytes 40
  5.7 3.6 %collective-permute-start.5 = (bf16[320,128]{1,0:T(8,128)(2,1)S(1)}, bf16[320,128]{1,0:T(8,128)(2,1)S(1)}, u32[]{:S(2)}, u32[]{:S(2)}) collective-permute-start(bf16[320,128]{1,0:T(8,128)(2,1)S(1)} %collective-permute-done.3), channel_id=1, source_target_pairs={{0,1},{1,0},{2,3},{3,2},{4,5},{5,4},{6,7},{7,6},{8,9},{9,8},{10,11... | collective-permute-start | bytes 245768 | tf_op jit(solution)/shard_map/ppermute | solution.py:204
  5.7 28.3 %copy-start.3 = (bf16[640,128]{1,0:T(8,128)(2,1)}, bf16[640,128]{1,0:T(8,128)(2,1)S(1)}, u32[]{:S(2)}) copy-start(bf16[640,128]{1,0:T(8,128)(2,1)S(1)} %maximum_select_fusion.refs_7_) | copy-start | bytes 491524
  5.7 5.4 %collective-permute-start.1 = (bf16[640,128]{1,0:T(8,128)(2,1)S(1)}, bf16[640,128]{1,0:T(8,128)(2,1)S(1)}, u32[]{:S(2)}, u32[]{:S(2)}) collective-permute-start(bf16[640,128]{1,0:T(8,128)(2,1)S(1)} %maximum_select_fusion.refs_7_), channel_id=1, source_target_pairs={{0,8},{1,5},{2,10},{3,7},{8,16},{9,1},{10,18},{11,3},{16,24},{17,9... | collective-permute-start | bytes 491528 | tf_op jit(solution)/shard_map/ppermute | solution.py:216
  7.8 23.0 %collective-permute-start.4 = (bf16[2,320,640]{2,1,0:T(8,128)(2,1)S(1)}, bf16[2,320,640]{2,1,0:T(8,128)(2,1)S(1)}, u32[]{:S(2)}, u32[]{:S(2)}) collective-permute-start(bf16[2,320,640]{2,1,0:T(8,128)(2,1)S(1)} %dynamic-slice_bitcast_fusion), channel_id=1, source_target_pairs={{0,2},{1,3},{2,0},{3,1},{4,6},{5,7},{6,4},{7,5},{8,10},{9,11},{10,... | collective-permute-start | bytes 2457608 | tf_op jit(solution)/shard_map/ppermute | solution.py:207
  9.4 24.7 %copy-start.4 = (bf16[640,128]{1,0:T(8,128)(2,1)}, bf16[640,128]{1,0:T(8,128)(2,1)S(1)}, u32[]{:S(2)}) copy-start(bf16[640,128]{1,0:T(8,128)(2,1)S(1)} %maximum_select_fusion.1.refs_8_) | copy-start | bytes 491524
  9.4 5.4 %collective-permute-start.7 = (bf16[640,128]{1,0:T(8,128)(2,1)S(1)}, bf16[640,128]{1,0:T(8,128)(2,1)S(1)}, u32[]{:S(2)}, u32[]{:S(2)}) collective-permute-start(bf16[640,128]{1,0:T(8,128)(2,1)S(1)} %maximum_select_fusion.1.refs_8_), channel_id=1, source_target_pairs={{0,8},{1,5},{2,10},{3,7},{8,16},{9,1},{10,18},{11,3},{16,24},{17,9... | collective-permute-start | bytes 491528 | tf_op jit(solution)/shard_map/ppermute | solution.py:216
  11.1 23.0 %copy-start.5 = (bf16[640,128]{1,0:T(8,128)(2,1)}, bf16[640,128]{1,0:T(8,128)(2,1)S(1)}, u32[]{:S(2)}) copy-start(bf16[640,128]{1,0:T(8,128)(2,1)S(1)} %collective-permute-done.1.refs_9_) | copy-start | bytes 491524
  11.1 14.3 %collective-permute-start.2 = (bf16[2,320,384]{2,1,0:T(8,128)(2,1)S(1)}, bf16[2,320,384]{2,1,0:T(8,128)(2,1)S(1)}, u32[]{:S(2)}, u32[]{:S(2)}) collective-permute-start(bf16[2,320,384]{2,1,0:T(8,128)(2,1)S(1)} %dynamic-slice_bitcast_fusion.1), channel_id=1, source_target_pairs={{0,1},{1,0},{2,3},{3,2},{4,5},{5,4},{6,7},{7,6},{8,9},{9,8},{10,11... | collective-permute-start | bytes 1474568 | tf_op jit(solution)/shard_map/ppermute | solution.py:204
  11.1 5.4 %collective-permute-start.6 = (bf16[640,128]{1,0:T(8,128)(2,1)S(1)}, bf16[640,128]{1,0:T(8,128)(2,1)S(1)}, u32[]{:S(2)}, u32[]{:S(2)}) collective-permute-start(bf16[640,128]{1,0:T(8,128)(2,1)S(1)} %collective-permute-done.1.refs_9_), channel_id=1, source_target_pairs={{0,8},{1,5},{2,10},{3,7},{8,16},{9,1},{10,18},{11,3},{16,24},{17,9... | collective-permute-start | bytes 491528 | tf_op jit(solution)/shard_map/ppermute | solution.py:216
  14.7 19.3 %copy-start.6 = (bf16[640,128]{1,0:T(8,128)(2,1)}, bf16[640,128]{1,0:T(8,128)(2,1)S(1)}, u32[]{:S(2)}) copy-start(bf16[640,128]{1,0:T(8,128)(2,1)S(1)} %collective-permute-done.7.refs_10_) | copy-start | bytes 491524
  14.7 5.3 %collective-permute-start.9 = (bf16[640,128]{1,0:T(8,128)(2,1)S(1)}, bf16[640,128]{1,0:T(8,128)(2,1)S(1)}, u32[]{:S(2)}, u32[]{:S(2)}) collective-permute-start(bf16[640,128]{1,0:T(8,128)(2,1)S(1)} %collective-permute-done.7.refs_10_), channel_id=1, source_target_pairs={{0,8},{1,5},{2,10},{3,7},{8,16},{9,1},{10,18},{11,3},{16,24},{17,9... | collective-permute-start | bytes 491528 | tf_op jit(solution)/shard_map/ppermute | solution.py:216
  16.3 3.8 %collective-permute-start.10 = (bf16[640,128]{1,0:T(8,128)(2,1)S(1)}, bf16[640,128]{1,0:T(8,128)(2,1)S(1)}, u32[]{:S(2)}, u32[]{:S(2)}) collective-permute-start(bf16[640,128]{1,0:T(8,128)(2,1)S(1)} %collective-permute-done.7.refs_10_), channel_id=1, source_target_pairs={{0,1},{1,0},{2,3},{3,2},{4,5},{5,4},{6,7},{7,6},{8,9},{9,8},{10,11... | collective-permute-start | bytes 491528 | tf_op jit(solution)/shard_map/ppermute | solution.py:204
  16.5 17.6 %copy-start.7 = (bf16[640,128]{1,0:T(8,128)(2,1)}, bf16[640,128]{1,0:T(8,128)(2,1)S(1)}, u32[]{:S(2)}) copy-start(bf16[640,128]{1,0:T(8,128)(2,1)S(1)} %collective-permute-done.6.refs_11_) | copy-start | bytes 491524
  16.5 5.3 %collective-permute-start.8 = (bf16[640,128]{1,0:T(8,128)(2,1)S(1)}, bf16[640,128]{1,0:T(8,128)(2,1)S(1)}, u32[]{:S(2)}, u32[]{:S(2)}) collective-permute-start(bf16[640,128]{1,0:T(8,128)(2,1)S(1)} %collective-permute-done.6.refs_11_), channel_id=1, source_target_pairs={{0,8},{1,5},{2,10},{3,7},{8,16},{9,1},{10,18},{11,3},{16,24},{17,9... | collective-permute-start | bytes 491528 | tf_op jit(solution)/shard_map/ppermute | solution.py:216
  20.1 14.0 %copy-start.8 = (bf16[640,128]{1,0:T(8,128)(2,1)}, bf16[640,128]{1,0:T(8,128)(2,1)S(1)}, u32[]{:S(2)}) copy-start(bf16[640,128]{1,0:T(8,128)(2,1)S(1)} %collective-permute-done.9.refs_12_) | copy-start | bytes 491524
  20.1 3.7 %collective-permute-start.13 = (bf16[640,128]{1,0:T(8,128)(2,1)S(1)}, bf16[640,128]{1,0:T(8,128)(2,1)S(1)}, u32[]{:S(2)}, u32[]{:S(2)}) collective-permute-start(bf16[640,128]{1,0:T(8,128)(2,1)S(1)} %collective-permute-done.1.refs_9_), channel_id=1, source_target_pairs={{0,1},{1,0},{2,3},{3,2},{4,5},{5,4},{6,7},{7,6},{8,9},{9,8},{10,11... | collective-permute-start | bytes 491528 | tf_op jit(solution)/shard_map/ppermute | solution.py:204
  20.1 14.0 %copy-start.9 = (bf16[640,128]{1,0:T(8,128)(2,1)}, bf16[640,128]{1,0:T(8,128)(2,1)S(1)}, u32[]{:S(2)}) copy-start(bf16[640,128]{1,0:T(8,128)(2,1)S(1)} %collective-permute-done.10.refs_16_) | copy-start | bytes 491524
  20.1 5.4 %collective-permute-start.12 = (bf16[640,128]{1,0:T(8,128)(2,1)S(1)}, bf16[640,128]{1,0:T(8,128)(2,1)S(1)}, u32[]{:S(2)}, u32[]{:S(2)}) collective-permute-start(bf16[640,128]{1,0:T(8,128)(2,1)S(1)} %collective-permute-done.9.refs_12_), channel_id=1, source_target_pairs={{0,8},{1,5},{2,10},{3,7},{8,16},{9,1},{10,18},{11,3},{16,24},{17,9... | collective-permute-start | bytes 491528 | tf_op jit(solution)/shard_map/ppermute | solution.py:216
  21.8 12.3 %copy-start.10 = (bf16[640,128]{1,0:T(8,128)(2,1)}, bf16[640,128]{1,0:T(8,128)(2,1)S(1)}, u32[]{:S(2)}) copy-start(bf16[640,128]{1,0:T(8,128)(2,1)S(1)} %collective-permute-done.8.refs_13_) | copy-start | bytes 491524
  21.8 5.4 %collective-permute-start.11 = (bf16[640,128]{1,0:T(8,128)(2,1)S(1)}, bf16[640,128]{1,0:T(8,128)(2,1)S(1)}, u32[]{:S(2)}, u32[]{:S(2)}) collective-permute-start(bf16[640,128]{1,0:T(8,128)(2,1)S(1)} %collective-permute-done.8.refs_13_), channel_id=1, source_target_pairs={{0,8},{1,5},{2,10},{3,7},{8,16},{9,1},{10,18},{11,3},{16,24},{17,9... | collective-permute-start | bytes 491528 | tf_op jit(solution)/shard_map/ppermute | solution.py:216
  23.8 10.4 %copy-start.11 = (bf16[640,128]{1,0:T(8,128)(2,1)}, bf16[640,128]{1,0:T(8,128)(2,1)S(1)}, u32[]{:S(2)}) copy-start(bf16[640,128]{1,0:T(8,128)(2,1)S(1)} %collective-permute-done.13.refs_15_) | copy-start | bytes 491524
  25.5 5.3 %collective-permute-start.14 = (bf16[640,128]{1,0:T(8,128)(2,1)S(1)}, bf16[640,128]{1,0:T(8,128)(2,1)S(1)}, u32[]{:S(2)}, u32[]{:S(2)}) collective-permute-start(bf16[640,128]{1,0:T(8,128)(2,1)S(1)} %collective-permute-done.12.refs_14_), channel_id=1, source_target_pairs={{0,8},{1,5},{2,10},{3,7},{8,16},{9,1},{10,18},{11,3},{16,24},{17,9... | collective-permute-start | bytes 491528 | tf_op jit(solution)/shard_map/ppermute | solution.py:216
  30.8 3.3 %collective-permute-start.15 = (bf16[2,320,640]{2,1,0:T(8,128)(2,1)S(1)}, bf16[2,320,640]{2,1,0:T(8,128)(2,1)S(1)}, u32[]{:S(2)}, u32[]{:S(2)}) collective-permute-start(bf16[2,320,640]{2,1,0:T(8,128)(2,1)S(1)} %collective-permute-done.4.refs_5_), channel_id=1, source_target_pairs={{0,1},{1,0},{2,3},{3,2},{4,5},{5,4},{6,7},{7,6},{8,9},{9,8},{10,11... | collective-permute-start | bytes 2457608 | tf_op jit(solution)/shard_map/ppermute | solution.py:204
  30.8 2.6 %collective-permute-start.16 = (bf16[640,128]{1,0:T(8,128)(2,1)S(1)}, bf16[640,128]{1,0:T(8,128)(2,1)S(1)}, u32[]{:S(2)}, u32[]{:S(2)}) collective-permute-start(bf16[640,128]{1,0:T(8,128)(2,1)S(1)} %collective-permute-done.6.refs_11_), channel_id=1, source_target_pairs={{0,1},{1,0},{2,3},{3,2},{4,5},{5,4},{6,7},{7,6},{8,9},{9,8},{10,11... | collective-permute-start | bytes 491528 | tf_op jit(solution)/shard_map/ppermute | solution.py:204
  31.3 2.3 %collective-permute-start.17 = (bf16[640,128]{1,0:T(8,128)(2,1)S(1)}, bf16[640,128]{1,0:T(8,128)(2,1)S(1)}, u32[]{:S(2)}, u32[]{:S(2)}) collective-permute-start(bf16[640,128]{1,0:T(8,128)(2,1)S(1)} %collective-permute-done.9.refs_12_), channel_id=1, source_target_pairs={{0,1},{1,0},{2,3},{3,2},{4,5},{5,4},{6,7},{7,6},{8,9},{9,8},{10,11... | collective-permute-start | bytes 491528 | tf_op jit(solution)/shard_map/ppermute | solution.py:204
  31.4 2.5 %collective-permute-start.18 = (bf16[640,128]{1,0:T(8,128)(2,1)S(1)}, bf16[640,128]{1,0:T(8,128)(2,1)S(1)}, u32[]{:S(2)}, u32[]{:S(2)}) collective-permute-start(bf16[640,128]{1,0:T(8,128)(2,1)S(1)} %collective-permute-done.8.refs_13_), channel_id=1, source_target_pairs={{0,1},{1,0},{2,3},{3,2},{4,5},{5,4},{6,7},{7,6},{8,9},{9,8},{10,11... | collective-permute-start | bytes 491528 | tf_op jit(solution)/shard_map/ppermute | solution.py:204
  31.8 2.2 %collective-permute-start.19 = (bf16[640,128]{1,0:T(8,128)(2,1)S(1)}, bf16[640,128]{1,0:T(8,128)(2,1)S(1)}, u32[]{:S(2)}, u32[]{:S(2)}) collective-permute-start(bf16[640,128]{1,0:T(8,128)(2,1)S(1)} %collective-permute-done.12.refs_14_), channel_id=1, source_target_pairs={{0,1},{1,0},{2,3},{3,2},{4,5},{5,4},{6,7},{7,6},{8,9},{9,8},{10,11... | collective-permute-start | bytes 491528 | tf_op jit(solution)/shard_map/ppermute | solution.py:204
  (8 other events, 27.5 us)

commit v4 on v3

--- a/solution.py
+++ b/solution.py
@@ -101,19 +101,21 @@
             gap = lax.rem(spot - me + total, total)
             dst, sem = full.at[which, slot], orb_sem.at[which, slot]
 
-            def bring(waves, dst=dst, sem=sem):
+            def bring(waves, core=c, dst=dst, sem=sem):
                 for wave in range(2):
-                    at = jnp.where(turned, wave, jnp.where(wave == 0, x, 1 - x)) * chip
-                    pltpu.make_async_copy(
-                        waves[wave], dst.at[pl.ds(pl.multiple_of(at, chip), chip)], sem
-                    ).start()
+                    block = jnp.where(turned, wave, jnp.where(wave == 0, x, 1 - x))
+                    for part, unit in ((0, core), (1, 1 - core)):
+                        at = pl.multiple_of((CORES * block + unit) * rows, rows)
+                        pltpu.make_async_copy(
+                            waves[wave].at[pl.ds(part * rows, rows)], dst.at[pl.ds(at, rows)], sem
+                        ).start()
 
             pl.when(gap == 0)(functools.partial(bring, near))
             for k in range(1, steps + 1):
                 own = gap == jnp.where(c == 0, total - k, k)
                 other = gap == jnp.where(c == 0, k, total - k)
                 pl.when(own)(functools.partial(bring, ring[2 * k - 2 : 2 * k]))
-                pl.when(other)(functools.partial(bring, swap[2 * k - 2 : 2 * k]))
+                pl.when(other)(functools.partial(bring, swap[2 * k - 2 : 2 * k], 1 - c))
             pl.when(gap == steps + 1)(functools.partial(bring, last))
 
     def arrive(which, slot):
@@ -215,11 +217,6 @@
                 moves.append((order[place] * row_total + r, target * row_total + r))
         return lax.ppermute(value, ("pb", "row"), moves)
 
-    def in_order(mine, other):
-        return jnp.where(
-            c == 0, jnp.concatenate([mine, other]), jnp.concatenate([other, mine])
-        )
-
     def after(value, *earlier):
         return lax.optimization_barrier((value, *earlier))[0]
 
@@ -227,10 +224,10 @@
     w_block = interaction[:, 0]
     far = other_chip(own)
     near_other = other_core(own)
-    near = [in_order(own, near_other)]
+    near = [jnp.concatenate([own, near_other])]
     w_away = lax.dynamic_slice_in_dim(w_block, (1 - x) * chip, chip, axis=2)
     w_far = other_chip(after(w_away, far))
-    near.append(in_order(far, other_core(after(far, w_away))))
+    near.append(jnp.concatenate([far, other_core(after(far, w_away))]))
     steps = total // 2 - 1
     first, second = [near[0]], [near[1]]
     swap_first, swap_second = [], []
@@ -239,7 +236,7 @@
     for k in range(steps + 1):
         if k == 1:
             w_core = other_core(after(w_mine, first[1]))
-        if k >= 2:
+        if k == 2:
             swap_first.append(other_core(first[k - 1]))
             swap_second.append(other_core(second[k - 1]))
         ahead = [*second[k - 1 : k], *(swap_second[:1] if k == 3 else [])] if k else []
@@ -248,9 +245,10 @@
         second.append(along_ring(after(second[k], *behind)))
     ring = [wave[k] for k in range(1, steps + 1) for wave in (first, second)]
     last = [first[steps + 1], second[steps + 1]]
-    for k in range(len(swap_first) + 1, steps + 1):
-        swap_first.append(other_core(after(first[k], last[0])))
-        swap_second.append(other_core(after(second[k], *last)))
+    swap_first.append(other_core(after(first[steps - 1], last[0])))
+    swap_second.append(other_core(after(second[steps - 1], *last)))
+    swap_first.append(other_core(after(first[steps], last[0])))
+    swap_second.append(other_core(after(second[steps], *last)))
     swap = [wave[k] for k in range(steps) for wave in (swap_first, swap_second)]
     w_far_core = other_core(after(w_far, *last))
 

time: 41.3 us -> 39.6 us (0.959)
  starting transfers between devices: 19.9 us -> 18.3 us
    ppermute x8, starting transfers between devices: 14.3 us -> 12.8 us  [along_ring(): return lax.ppermute(value, ('pb', 'row'), moves)]
    ppermute x2, waiting for transfers between devices: 1.47 us -> 0.01 us  [other_chip(): lax.ppermute(value, 'row', [(r, r ^ CORES) for r in range(row_total)])]
    ppermute x8, waiting for transfers between devices: 9 us -> 10.2 us  [along_ring(): return lax.ppermute(value, ('pb', 'row'), moves)]
where the time goes in v4:
time: 39.6 us; the launch traced here: 39.3 us
  starting transfers between devices  18.3 us (46%)
  waiting for transfers between devices  11.9 us (30%)
  Pallas kernels  6.34 us (16%)
  local copies, waits for them, and re-layouts  1.91 us (5%)
  between operations  0.83 us (2%)
    ppermute x8, starting transfers between devices, along_ring(): return lax.ppermute(value, ('pb', 'row'), moves)  12.8 us
    ppermute x8, waiting for transfers between devices, along_ring(): return lax.ppermute(value, ('pb', 'row'), moves)  10.2 us
    pallas_call x1, Pallas kernels, paired_shards(): pl.pallas_call(functools.partial(exchange_kernel, steps, total), out_shap...  6.34 us
    ppermute x2, starting transfers between devices, other_chip(): lax.ppermute(value, 'row', [(r, r ^ CORES) for r in range(row_total)])  4.44 us
    ppermute x10, waiting for transfers between devices, other_core(): return lax.ppermute(value, 'row', [(r, r ^ 1) for r in range(row_total)])  1.77 us
    dynamic_slice x1, local copies, waits for them, and re-layouts, paired_shards(): w_away = lax.dynamic_slice_in_dim(w_block, (1 - x) * chip, chip, axis=2)  1.24 us
    ppermute x10, starting transfers between devices, other_core(): return lax.ppermute(value, 'row', [(r, r ^ 1) for r in range(row_total)])  1.1 us
  transfers between devices with their start and end apart: 20, of which 13 were waited for; matrix products, arithmetic and copies ran while one was open for 3% of the time, Pallas kernels for 0%

profile of v4, /device:TPU:0, one launch (start us, length us, event | category | flops | bytes accessed | tf_op | source)
XLA Modules:
  0.0 39.3 jit_solution(14508849738476943517)
XLA Ops:
  0.0 2.9 %collective-permute-start.3 = (bf16[320,128]{1,0:T(8,128)(2,1)}, bf16[320,128]{1,0:T(8,128)(2,1)S(1)}, u32[]{:S(2)}, u32[]{:S(2)}) collective-permute-start(bf16[320,128]{1,0:T(8,128)(2,1)} %bitcast.7), channel_id=1, source_target_pairs={{0,2},{1,3},{2,0},{3,1},{4,6},{5,7},{6,4},{7,5},{8,10},{9,11},{10,... | collective-permute-start | bytes 245768 | tf_op jit(solution)/shard_map/ppermute | solution.py:209
  3.0 1.2 %dynamic-slice_bitcast_fusion = bf16[2,320,640]{2,1,0:T(8,128)(2,1)S(1)} fusion(bf16[2,1,320,1280]{3,2,1,0:T(8,128)(2,1)} %refs_3_.1, s32[]{:T(128)S(6)} %select_n.20), kind=kLoop, calls=%fused_computation | loop fusion | bytes 1638404 | tf_op jit(solution)/shard_map/dynamic_slice | solution.py:228
  4.2 0.2 collective-permute-done
  4.5 1.6 %collective-permute-start.1 = (bf16[640,128]{1,0:T(8,128)(2,1)S(1)}, bf16[640,128]{1,0:T(8,128)(2,1)S(1)}, u32[]{:S(2)}, u32[]{:S(2)}) collective-permute-start(bf16[640,128]{1,0:T(8,128)(2,1)S(1)} %pad_maximum_fusion.refs_7_), channel_id=1, source_target_pairs={{0,8},{1,5},{2,10},{3,7},{8,16},{9,1},{10,18},{11,3},{16,24},{17,9... | collective-permute-start | bytes 491528 | tf_op jit(solution)/shard_map/ppermute | solution.py:218
  6.1 1.5 %collective-permute-start.4 = (bf16[2,320,640]{2,1,0:T(8,128)(2,1)S(1)}, bf16[2,320,640]{2,1,0:T(8,128)(2,1)S(1)}, u32[]{:S(2)}, u32[]{:S(2)}) collective-permute-start(bf16[2,320,640]{2,1,0:T(8,128)(2,1)S(1)} %dynamic-slice_bitcast_fusion), channel_id=1, source_target_pairs={{0,2},{1,3},{2,0},{3,1},{4,6},{5,7},{6,4},{7,5},{8,10},{9,11},{10,... | collective-permute-start | bytes 2457608 | tf_op jit(solution)/shard_map/ppermute | solution.py:209
  7.6 1.6 %collective-permute-start.7 = (bf16[640,128]{1,0:T(8,128)(2,1)S(1)}, bf16[640,128]{1,0:T(8,128)(2,1)S(1)}, u32[]{:S(2)}, u32[]{:S(2)}) collective-permute-start(bf16[640,128]{1,0:T(8,128)(2,1)S(1)} %constant_dynamic-update-slice_fusion.refs_8_), channel_id=1, source_target_pairs={{0,8},{1,5},{2,10},{3,7},{8,16},{9,1},{10,18},{11,3},{16,24},{17,9... | collective-permute-start | bytes 491528 | tf_op jit(solution)/shard_map/ppermute | solution.py:218
  9.3 0.5 %collective-permute-done.1.refs_9_ = bf16[640,128]{1,0:T(8,128)(2,1)S(1)} collective-permute-done((bf16[640,128]{1,0:T(8,128)(2,1)S(1)}, bf16[640,128]{1,0:T(8,128)(2,1)S(1)}, u32[]{:S(2)}, u32[]{:S(2)}) %collective-permute-start.1) | collective-permute-done | bytes 163872 | tf_op jit(solution)/shard_map/ppermute | solution.py:218
  9.8 1.6 %collective-permute-start.6 = (bf16[640,128]{1,0:T(8,128)(2,1)S(1)}, bf16[640,128]{1,0:T(8,128)(2,1)S(1)}, u32[]{:S(2)}, u32[]{:S(2)}) collective-permute-start(bf16[640,128]{1,0:T(8,128)(2,1)S(1)} %collective-permute-done.1.refs_9_), channel_id=1, source_target_pairs={{0,8},{1,5},{2,10},{3,7},{8,16},{9,1},{10,18},{11,3},{16,24},{17,9... | collective-permute-start | bytes 491528 | tf_op jit(solution)/shard_map/ppermute | solution.py:218
  11.4 1.6 %collective-permute-done.7.refs_10_ = bf16[640,128]{1,0:T(8,128)(2,1)S(1)} collective-permute-done((bf16[640,128]{1,0:T(8,128)(2,1)S(1)}, bf16[640,128]{1,0:T(8,128)(2,1)S(1)}, u32[]{:S(2)}, u32[]{:S(2)}) %collective-permute-start.7) | collective-permute-done | bytes 163872 | tf_op jit(solution)/shard_map/ppermute | solution.py:218
  13.0 1.6 %collective-permute-start.9 = (bf16[640,128]{1,0:T(8,128)(2,1)S(1)}, bf16[640,128]{1,0:T(8,128)(2,1)S(1)}, u32[]{:S(2)}, u32[]{:S(2)}) collective-permute-start(bf16[640,128]{1,0:T(8,128)(2,1)S(1)} %collective-permute-done.7.refs_10_), channel_id=1, source_target_pairs={{0,8},{1,5},{2,10},{3,7},{8,16},{9,1},{10,18},{11,3},{16,24},{17,9... | collective-permute-start | bytes 491528 | tf_op jit(solution)/shard_map/ppermute | solution.py:218
  14.6 0.6 %collective-permute-done.6.refs_11_ = bf16[640,128]{1,0:T(8,128)(2,1)S(1)} collective-permute-done((bf16[640,128]{1,0:T(8,128)(2,1)S(1)}, bf16[640,128]{1,0:T(8,128)(2,1)S(1)}, u32[]{:S(2)}, u32[]{:S(2)}) %collective-permute-start.6) | collective-permute-done | bytes 163872 | tf_op jit(solution)/shard_map/ppermute | solution.py:218
  15.2 1.6 %collective-permute-start.8 = (bf16[640,128]{1,0:T(8,128)(2,1)S(1)}, bf16[640,128]{1,0:T(8,128)(2,1)S(1)}, u32[]{:S(2)}, u32[]{:S(2)}) collective-permute-start(bf16[640,128]{1,0:T(8,128)(2,1)S(1)} %collective-permute-done.6.refs_11_), channel_id=1, source_target_pairs={{0,8},{1,5},{2,10},{3,7},{8,16},{9,1},{10,18},{11,3},{16,24},{17,9... | collective-permute-start | bytes 491528 | tf_op jit(solution)/shard_map/ppermute | solution.py:218
  16.7 1.6 %collective-permute-done.9.refs_12_ = bf16[640,128]{1,0:T(8,128)(2,1)S(1)} collective-permute-done((bf16[640,128]{1,0:T(8,128)(2,1)S(1)}, bf16[640,128]{1,0:T(8,128)(2,1)S(1)}, u32[]{:S(2)}, u32[]{:S(2)}) %collective-permute-start.9) | collective-permute-done | bytes 163872 | tf_op jit(solution)/shard_map/ppermute | solution.py:218
  18.4 1.6 %collective-permute-start.12 = (bf16[640,128]{1,0:T(8,128)(2,1)S(1)}, bf16[640,128]{1,0:T(8,128)(2,1)S(1)}, u32[]{:S(2)}, u32[]{:S(2)}) collective-permute-start(bf16[640,128]{1,0:T(8,128)(2,1)S(1)} %collective-permute-done.9.refs_12_), channel_id=1, source_target_pairs={{0,8},{1,5},{2,10},{3,7},{8,16},{9,1},{10,18},{11,3},{16,24},{17,9... | collective-permute-start | bytes 491528 | tf_op jit(solution)/shard_map/ppermute | solution.py:218
  20.0 0.5 %collective-permute-done.8.refs_13_ = bf16[640,128]{1,0:T(8,128)(2,1)S(1)} collective-permute-done((bf16[640,128]{1,0:T(8,128)(2,1)S(1)}, bf16[640,128]{1,0:T(8,128)(2,1)S(1)}, u32[]{:S(2)}, u32[]{:S(2)}) %collective-permute-start.8) | collective-permute-done | bytes 163872 | tf_op jit(solution)/shard_map/ppermute | solution.py:218
  20.5 1.6 %collective-permute-start.11 = (bf16[640,128]{1,0:T(8,128)(2,1)S(1)}, bf16[640,128]{1,0:T(8,128)(2,1)S(1)}, u32[]{:S(2)}, u32[]{:S(2)}) collective-permute-start(bf16[640,128]{1,0:T(8,128)(2,1)S(1)} %collective-permute-done.8.refs_13_), channel_id=1, source_target_pairs={{0,8},{1,5},{2,10},{3,7},{8,16},{9,1},{10,18},{11,3},{16,24},{17,9... | collective-permute-start | bytes 491528 | tf_op jit(solution)/shard_map/ppermute | solution.py:218
  22.1 1.7 %collective-permute-done.12.refs_14_ = bf16[640,128]{1,0:T(8,128)(2,1)S(1)} collective-permute-done((bf16[640,128]{1,0:T(8,128)(2,1)S(1)}, bf16[640,128]{1,0:T(8,128)(2,1)S(1)}, u32[]{:S(2)}, u32[]{:S(2)}) %collective-permute-start.12) | collective-permute-done | bytes 163872 | tf_op jit(solution)/shard_map/ppermute | solution.py:218
  23.7 1.6 %collective-permute-start.14 = (bf16[640,128]{1,0:T(8,128)(2,1)S(1)}, bf16[640,128]{1,0:T(8,128)(2,1)S(1)}, u32[]{:S(2)}, u32[]{:S(2)}) collective-permute-start(bf16[640,128]{1,0:T(8,128)(2,1)S(1)} %collective-permute-done.12.refs_14_), channel_id=1, source_target_pairs={{0,8},{1,5},{2,10},{3,7},{8,16},{9,1},{10,18},{11,3},{16,24},{17,9... | collective-permute-start | bytes 491528 | tf_op jit(solution)/shard_map/ppermute | solution.py:218
  25.3 0.5 %collective-permute-done.11.refs_21_ = bf16[640,128]{1,0:T(8,128)(2,1)S(1)} collective-permute-done((bf16[640,128]{1,0:T(8,128)(2,1)S(1)}, bf16[640,128]{1,0:T(8,128)(2,1)S(1)}, u32[]{:S(2)}, u32[]{:S(2)}) %collective-permute-start.11) | collective-permute-done | bytes 163872 | tf_op jit(solution)/shard_map/ppermute | solution.py:218
  25.8 3.3 %collective-permute-done.14.refs_22_ = bf16[640,128]{1,0:T(8,128)(2,1)S(1)} collective-permute-done((bf16[640,128]{1,0:T(8,128)(2,1)S(1)}, bf16[640,128]{1,0:T(8,128)(2,1)S(1)}, u32[]{:S(2)}, u32[]{:S(2)}) %collective-permute-start.14) | collective-permute-done | bytes 163872 | tf_op jit(solution)/shard_map/ppermute | solution.py:218
  29.1 0.5 %collective-permute-start.16 = (bf16[640,128]{1,0:T(8,128)(2,1)S(1)}, bf16[640,128]{1,0:T(8,128)(2,1)S(1)}, u32[]{:S(2)}, u32[]{:S(2)}) collective-permute-start(bf16[640,128]{1,0:T(8,128)(2,1)S(1)} %collective-permute-done.6.refs_11_), channel_id=1, source_target_pairs={{0,1},{1,0},{2,3},{3,2},{4,5},{5,4},{6,7},{7,6},{8,9},{9,8},{10,11... | collective-permute-start | bytes 491528 | tf_op jit(solution)/shard_map/ppermute | solution.py:206
  29.6 0.1 collective-permute-start.18
  29.6 0.4 %collective-permute-start.17 = (bf16[640,128]{1,0:T(8,128)(2,1)S(1)}, bf16[640,128]{1,0:T(8,128)(2,1)S(1)}, u32[]{:S(2)}, u32[]{:S(2)}) collective-permute-start(bf16[640,128]{1,0:T(8,128)(2,1)S(1)} %collective-permute-done.9.refs_12_), channel_id=1, source_target_pairs={{0,1},{1,0},{2,3},{3,2},{4,5},{5,4},{6,7},{7,6},{8,9},{9,8},{10,11... | collective-permute-start | bytes 491528 | tf_op jit(solution)/shard_map/ppermute | solution.py:206
  30.1 0.1 collective-permute-start.19
  30.8 0.8 %collective-permute-done.16.refs_17_ = bf16[640,128]{1,0:T(8,128)(2,1)S(1)} collective-permute-done((bf16[640,128]{1,0:T(8,128)(2,1)S(1)}, bf16[640,128]{1,0:T(8,128)(2,1)S(1)}, u32[]{:S(2)}, u32[]{:S(2)}) %collective-permute-start.16) | collective-permute-done | bytes 163872 | tf_op jit(solution)/shard_map/ppermute | solution.py:206
  31.6 0.2 collective-permute-done.18.refs_19_
  31.9 0.2 collective-permute-done.17.refs_18_
  32.1 0.2 collective-permute-done.19.refs_20_
  32.5 0.1 copy-done.16
  32.5 0.2 copy-done.17
  32.8 0.2 copy-done.18
  33.0 6.3 %shard_map.55 = f32[1,3,320,128]{3,2,1,0:T(8,128)} custom-call(s32[1,2,3]{2,1,0:T(2,128)S(1)} %bitcast.6, s32[1,3]{1,0:T(1,128)S(1)} %copy-done.2, s32[1]{0:T(128)S(6)} %copy.7.refs_2_, bf16[2,1,320,1280]{3,2,1,0:T(8,128)(2,1)S(1)} %copy-done, bf16[2,320,384]{2,1,0:T(8,128)(2,1)S(1)} %collective-permute-done.2.refs_4_, ...), custom_call_target="tpu_custom_call" | custom-call | flops 1258291200 | bytes 8388608 | tf_op jit(solution)/shard_map/pallas_call | solution.py:263
  (54 shorter events, 0.2 us)
Async XLA Ops:
  0.0 9.3 %copy-start = (bf16[2,1,320,1280]{3,2,1,0:T(8,128)(2,1)S(1)}, bf16[2,1,320,1280]{3,2,1,0:T(8,128)(2,1)}, u32[]{:S(2)}) copy-start(bf16[2,1,320,1280]{3,2,1,0:T(8,128)(2,1)} %refs_3_.1) | copy-start | bytes 4915204
  0.0 6.1 %collective-permute-start.3 = (bf16[320,128]{1,0:T(8,128)(2,1)}, bf16[320,128]{1,0:T(8,128)(2,1)S(1)}, u32[]{:S(2)}, u32[]{:S(2)}) collective-permute-start(bf16[320,128]{1,0:T(8,128)(2,1)} %bitcast.7), channel_id=1, source_target_pairs={{0,2},{1,3},{2,0},{3,1},{4,6},{5,7},{6,4},{7,5},{8,10},{9,11},{10,... | collective-permute-start | bytes 245768 | tf_op jit(solution)/shard_map/ppermute | solution.py:209
  2.9 1.5 %collective-permute-start = (bf16[320,128]{1,0:T(8,128)(2,1)}, bf16[320,128]{1,0:T(8,128)(2,1)S(1)}, u32[]{:S(2)}, u32[]{:S(2)}) collective-permute-start(bf16[320,128]{1,0:T(8,128)(2,1)} %bitcast.8), channel_id=1, source_target_pairs={{0,1},{1,0},{2,3},{3,2},{4,5},{5,4},{6,7},{7,6},{8,9},{9,8},{10,11... | collective-permute-start | bytes 245768 | tf_op jit(solution)/shard_map/ppermute | solution.py:206
  2.9 30.0 %copy-start.1 = (s32[1,3,2]{1,2,0:T(2,128)S(1)}, s32[1,3,2]{1,2,0:T(2,128)}, u32[]{:S(2)}) copy-start(s32[1,3,2]{1,2,0:T(2,128)} %param.7) | copy-start | bytes 76
  2.9 30.0 %copy-start.2 = (s32[1,3]{1,0:T(1,128)S(1)}, s32[1,3]{1,0:T(1,128)}, u32[]{:S(2)}) copy-start(s32[1,3]{1,0:T(1,128)} %refs_1_.1) | copy-start | bytes 40
  4.5 27.9 %copy-start.3 = (bf16[640,128]{1,0:T(8,128)(2,1)}, bf16[640,128]{1,0:T(8,128)(2,1)S(1)}, u32[]{:S(2)}) copy-start(bf16[640,128]{1,0:T(8,128)(2,1)S(1)} %pad_maximum_fusion.refs_7_) | copy-start | bytes 491524
  4.5 5.4 %collective-permute-start.1 = (bf16[640,128]{1,0:T(8,128)(2,1)S(1)}, bf16[640,128]{1,0:T(8,128)(2,1)S(1)}, u32[]{:S(2)}, u32[]{:S(2)}) collective-permute-start(bf16[640,128]{1,0:T(8,128)(2,1)S(1)} %pad_maximum_fusion.refs_7_), channel_id=1, source_target_pairs={{0,8},{1,5},{2,10},{3,7},{8,16},{9,1},{10,18},{11,3},{16,24},{17,9... | collective-permute-start | bytes 491528 | tf_op jit(solution)/shard_map/ppermute | solution.py:218
  6.1 1.5 %collective-permute-start.5 = (bf16[320,128]{1,0:T(8,128)(2,1)S(1)}, bf16[320,128]{1,0:T(8,128)(2,1)S(1)}, u32[]{:S(2)}, u32[]{:S(2)}) collective-permute-start(bf16[320,128]{1,0:T(8,128)(2,1)S(1)} %collective-permute-done.3), channel_id=1, source_target_pairs={{0,1},{1,0},{2,3},{3,2},{4,5},{5,4},{6,7},{7,6},{8,9},{9,8},{10,11... | collective-permute-start | bytes 245768 | tf_op jit(solution)/shard_map/ppermute | solution.py:206
  6.1 23.0 %collective-permute-start.4 = (bf16[2,320,640]{2,1,0:T(8,128)(2,1)S(1)}, bf16[2,320,640]{2,1,0:T(8,128)(2,1)S(1)}, u32[]{:S(2)}, u32[]{:S(2)}) collective-permute-start(bf16[2,320,640]{2,1,0:T(8,128)(2,1)S(1)} %dynamic-slice_bitcast_fusion), channel_id=1, source_target_pairs={{0,2},{1,3},{2,0},{3,1},{4,6},{5,7},{6,4},{7,5},{8,10},{9,11},{10,... | collective-permute-start | bytes 2457608 | tf_op jit(solution)/shard_map/ppermute | solution.py:209
  7.6 24.7 %copy-start.4 = (bf16[640,128]{1,0:T(8,128)(2,1)}, bf16[640,128]{1,0:T(8,128)(2,1)S(1)}, u32[]{:S(2)}) copy-start(bf16[640,128]{1,0:T(8,128)(2,1)S(1)} %constant_dynamic-update-slice_fusion.refs_8_) | copy-start | bytes 491524
  7.6 5.4 %collective-permute-start.7 = (bf16[640,128]{1,0:T(8,128)(2,1)S(1)}, bf16[640,128]{1,0:T(8,128)(2,1)S(1)}, u32[]{:S(2)}, u32[]{:S(2)}) collective-permute-start(bf16[640,128]{1,0:T(8,128)(2,1)S(1)} %constant_dynamic-update-slice_fusion.refs_8_), channel_id=1, source_target_pairs={{0,8},{1,5},{2,10},{3,7},{8,16},{9,1},{10,18},{11,3},{16,24},{17,9... | collective-permute-start | bytes 491528 | tf_op jit(solution)/shard_map/ppermute | solution.py:218
  9.8 22.5 %copy-start.5 = (bf16[640,128]{1,0:T(8,128)(2,1)}, bf16[640,128]{1,0:T(8,128)(2,1)S(1)}, u32[]{:S(2)}) copy-start(bf16[640,128]{1,0:T(8,128)(2,1)S(1)} %collective-permute-done.1.refs_9_) | copy-start | bytes 491524
  9.8 13.9 %collective-permute-start.2 = (bf16[2,320,384]{2,1,0:T(8,128)(2,1)S(1)}, bf16[2,320,384]{2,1,0:T(8,128)(2,1)S(1)}, u32[]{:S(2)}, u32[]{:S(2)}) collective-permute-start(bf16[2,320,384]{2,1,0:T(8,128)(2,1)S(1)} %dynamic-slice_bitcast_fusion.1), channel_id=1, source_target_pairs={{0,1},{1,0},{2,3},{3,2},{4,5},{5,4},{6,7},{7,6},{8,9},{9,8},{10,11... | collective-permute-start | bytes 1474568 | tf_op jit(solution)/shard_map/ppermute | solution.py:206
  9.8 5.3 %collective-permute-start.6 = (bf16[640,128]{1,0:T(8,128)(2,1)S(1)}, bf16[640,128]{1,0:T(8,128)(2,1)S(1)}, u32[]{:S(2)}, u32[]{:S(2)}) collective-permute-start(bf16[640,128]{1,0:T(8,128)(2,1)S(1)} %collective-permute-done.1.refs_9_), channel_id=1, source_target_pairs={{0,8},{1,5},{2,10},{3,7},{8,16},{9,1},{10,18},{11,3},{16,24},{17,9... | collective-permute-start | bytes 491528 | tf_op jit(solution)/shard_map/ppermute | solution.py:218
  13.0 19.3 %copy-start.6 = (bf16[640,128]{1,0:T(8,128)(2,1)}, bf16[640,128]{1,0:T(8,128)(2,1)S(1)}, u32[]{:S(2)}) copy-start(bf16[640,128]{1,0:T(8,128)(2,1)S(1)} %collective-permute-done.7.refs_10_) | copy-start | bytes 491524
  13.0 5.3 %collective-permute-start.9 = (bf16[640,128]{1,0:T(8,128)(2,1)S(1)}, bf16[640,128]{1,0:T(8,128)(2,1)S(1)}, u32[]{:S(2)}, u32[]{:S(2)}) collective-permute-start(bf16[640,128]{1,0:T(8,128)(2,1)S(1)} %collective-permute-done.7.refs_10_), channel_id=1, source_target_pairs={{0,8},{1,5},{2,10},{3,7},{8,16},{9,1},{10,18},{11,3},{16,24},{17,9... | collective-permute-start | bytes 491528 | tf_op jit(solution)/shard_map/ppermute | solution.py:218
  14.6 3.8 %collective-permute-start.10 = (bf16[640,128]{1,0:T(8,128)(2,1)S(1)}, bf16[640,128]{1,0:T(8,128)(2,1)S(1)}, u32[]{:S(2)}, u32[]{:S(2)}) collective-permute-start(bf16[640,128]{1,0:T(8,128)(2,1)S(1)} %collective-permute-done.7.refs_10_), channel_id=1, source_target_pairs={{0,1},{1,0},{2,3},{3,2},{4,5},{5,4},{6,7},{7,6},{8,9},{9,8},{10,11... | collective-permute-start | bytes 491528 | tf_op jit(solution)/shard_map/ppermute | solution.py:206
  15.2 17.2 %copy-start.7 = (bf16[640,128]{1,0:T(8,128)(2,1)}, bf16[640,128]{1,0:T(8,128)(2,1)S(1)}, u32[]{:S(2)}) copy-start(bf16[640,128]{1,0:T(8,128)(2,1)S(1)} %collective-permute-done.6.refs_11_) | copy-start | bytes 491524
  15.2 5.3 %collective-permute-start.8 = (bf16[640,128]{1,0:T(8,128)(2,1)S(1)}, bf16[640,128]{1,0:T(8,128)(2,1)S(1)}, u32[]{:S(2)}, u32[]{:S(2)}) collective-permute-start(bf16[640,128]{1,0:T(8,128)(2,1)S(1)} %collective-permute-done.6.refs_11_), channel_id=1, source_target_pairs={{0,8},{1,5},{2,10},{3,7},{8,16},{9,1},{10,18},{11,3},{16,24},{17,9... | collective-permute-start | bytes 491528 | tf_op jit(solution)/shard_map/ppermute | solution.py:218
  18.3 14.0 %copy-start.8 = (bf16[640,128]{1,0:T(8,128)(2,1)}, bf16[640,128]{1,0:T(8,128)(2,1)S(1)}, u32[]{:S(2)}) copy-start(bf16[640,128]{1,0:T(8,128)(2,1)S(1)} %collective-permute-done.9.refs_12_) | copy-start | bytes 491524
  18.3 3.7 %collective-permute-start.13 = (bf16[640,128]{1,0:T(8,128)(2,1)S(1)}, bf16[640,128]{1,0:T(8,128)(2,1)S(1)}, u32[]{:S(2)}, u32[]{:S(2)}) collective-permute-start(bf16[640,128]{1,0:T(8,128)(2,1)S(1)} %collective-permute-done.1.refs_9_), channel_id=1, source_target_pairs={{0,1},{1,0},{2,3},{3,2},{4,5},{5,4},{6,7},{7,6},{8,9},{9,8},{10,11... | collective-permute-start | bytes 491528 | tf_op jit(solution)/shard_map/ppermute | solution.py:206
  18.3 14.0 %copy-start.9 = (bf16[640,128]{1,0:T(8,128)(2,1)}, bf16[640,128]{1,0:T(8,128)(2,1)S(1)}, u32[]{:S(2)}) copy-start(bf16[640,128]{1,0:T(8,128)(2,1)S(1)} %collective-permute-done.10.refs_16_) | copy-start | bytes 491524
  18.4 5.4 %collective-permute-start.12 = (bf16[640,128]{1,0:T(8,128)(2,1)S(1)}, bf16[640,128]{1,0:T(8,128)(2,1)S(1)}, u32[]{:S(2)}, u32[]{:S(2)}) collective-permute-start(bf16[640,128]{1,0:T(8,128)(2,1)S(1)} %collective-permute-done.9.refs_12_), channel_id=1, source_target_pairs={{0,8},{1,5},{2,10},{3,7},{8,16},{9,1},{10,18},{11,3},{16,24},{17,9... | collective-permute-start | bytes 491528 | tf_op jit(solution)/shard_map/ppermute | solution.py:218
  20.5 11.9 %copy-start.10 = (bf16[640,128]{1,0:T(8,128)(2,1)}, bf16[640,128]{1,0:T(8,128)(2,1)S(1)}, u32[]{:S(2)}) copy-start(bf16[640,128]{1,0:T(8,128)(2,1)S(1)} %collective-permute-done.8.refs_13_) | copy-start | bytes 491524
  20.5 5.3 %collective-permute-start.11 = (bf16[640,128]{1,0:T(8,128)(2,1)S(1)}, bf16[640,128]{1,0:T(8,128)(2,1)S(1)}, u32[]{:S(2)}, u32[]{:S(2)}) collective-permute-start(bf16[640,128]{1,0:T(8,128)(2,1)S(1)} %collective-permute-done.8.refs_13_), channel_id=1, source_target_pairs={{0,8},{1,5},{2,10},{3,7},{8,16},{9,1},{10,18},{11,3},{16,24},{17,9... | collective-permute-start | bytes 491528 | tf_op jit(solution)/shard_map/ppermute | solution.py:218
  22.1 10.4 %copy-start.11 = (bf16[640,128]{1,0:T(8,128)(2,1)}, bf16[640,128]{1,0:T(8,128)(2,1)S(1)}, u32[]{:S(2)}) copy-start(bf16[640,128]{1,0:T(8,128)(2,1)S(1)} %collective-permute-done.13.refs_15_) | copy-start | bytes 491524
  23.7 5.3 %collective-permute-start.14 = (bf16[640,128]{1,0:T(8,128)(2,1)S(1)}, bf16[640,128]{1,0:T(8,128)(2,1)S(1)}, u32[]{:S(2)}, u32[]{:S(2)}) collective-permute-start(bf16[640,128]{1,0:T(8,128)(2,1)S(1)} %collective-permute-done.12.refs_14_), channel_id=1, source_target_pairs={{0,8},{1,5},{2,10},{3,7},{8,16},{9,1},{10,18},{11,3},{16,24},{17,9... | collective-permute-start | bytes 491528 | tf_op jit(solution)/shard_map/ppermute | solution.py:218
  29.1 3.3 %collective-permute-start.15 = (bf16[2,320,640]{2,1,0:T(8,128)(2,1)S(1)}, bf16[2,320,640]{2,1,0:T(8,128)(2,1)S(1)}, u32[]{:S(2)}, u32[]{:S(2)}) collective-permute-start(bf16[2,320,640]{2,1,0:T(8,128)(2,1)S(1)} %collective-permute-done.4.refs_5_), channel_id=1, source_target_pairs={{0,1},{1,0},{2,3},{3,2},{4,5},{5,4},{6,7},{7,6},{8,9},{9,8},{10,11... | collective-permute-start | bytes 2457608 | tf_op jit(solution)/shard_map/ppermute | solution.py:206
  29.1 2.6 %collective-permute-start.16 = (bf16[640,128]{1,0:T(8,128)(2,1)S(1)}, bf16[640,128]{1,0:T(8,128)(2,1)S(1)}, u32[]{:S(2)}, u32[]{:S(2)}) collective-permute-start(bf16[640,128]{1,0:T(8,128)(2,1)S(1)} %collective-permute-done.6.refs_11_), channel_id=1, source_target_pairs={{0,1},{1,0},{2,3},{3,2},{4,5},{5,4},{6,7},{7,6},{8,9},{9,8},{10,11... | collective-permute-start | bytes 491528 | tf_op jit(solution)/shard_map/ppermute | solution.py:206
  29.6 2.3 %collective-permute-start.18 = (bf16[640,128]{1,0:T(8,128)(2,1)S(1)}, bf16[640,128]{1,0:T(8,128)(2,1)S(1)}, u32[]{:S(2)}, u32[]{:S(2)}) collective-permute-start(bf16[640,128]{1,0:T(8,128)(2,1)S(1)} %collective-permute-done.8.refs_13_), channel_id=1, source_target_pairs={{0,1},{1,0},{2,3},{3,2},{4,5},{5,4},{6,7},{7,6},{8,9},{9,8},{10,11... | collective-permute-start | bytes 491528 | tf_op jit(solution)/shard_map/ppermute | solution.py:206
  29.6 2.5 %collective-permute-start.17 = (bf16[640,128]{1,0:T(8,128)(2,1)S(1)}, bf16[640,128]{1,0:T(8,128)(2,1)S(1)}, u32[]{:S(2)}, u32[]{:S(2)}) collective-permute-start(bf16[640,128]{1,0:T(8,128)(2,1)S(1)} %collective-permute-done.9.refs_12_), channel_id=1, source_target_pairs={{0,1},{1,0},{2,3},{3,2},{4,5},{5,4},{6,7},{7,6},{8,9},{9,8},{10,11... | collective-permute-start | bytes 491528 | tf_op jit(solution)/shard_map/ppermute | solution.py:206
  30.1 2.2 %collective-permute-start.19 = (bf16[640,128]{1,0:T(8,128)(2,1)S(1)}, bf16[640,128]{1,0:T(8,128)(2,1)S(1)}, u32[]{:S(2)}, u32[]{:S(2)}) collective-permute-start(bf16[640,128]{1,0:T(8,128)(2,1)S(1)} %collective-permute-done.12.refs_14_), channel_id=1, source_target_pairs={{0,1},{1,0},{2,3},{3,2},{4,5},{5,4},{6,7},{7,6},{8,9},{9,8},{10,11... | collective-permute-start | bytes 491528 | tf_op jit(solution)/shard_map/ppermute | solution.py:206
  (8 other events, 26.0 us)

commit v5 on v4

--- a/solution.py
+++ b/solution.py
@@ -84,8 +84,8 @@
     ring, refs = refs[: 2 * steps], refs[2 * steps :]
     swap, refs = refs[: 2 * steps], refs[2 * steps :]
     last, refs = refs[:2], refs[2:]
-    out, eff, full, orb_sem = refs
-    slots, rows, width = out.shape[1:]
+    out_hbm, out, eff, full, orb_sem, out_sem = refs
+    slots, rows, width = out.shape
     points = full.shape[2]
     chip = 2 * rows
     wide = rows + 64
@@ -167,7 +167,7 @@
             target = full[0, slot, at : at + step]
             result += jnp.dot(kern_real, target, preferred_element_type=jnp.float32)
             result += jnp.dot(kern_imag, -rotated(target), preferred_element_type=jnp.float32)
-        out[0, slot] = result
+        out[slot] = result
 
     def compute(slot, carry):
         arrive(1, slot)
@@ -185,11 +185,14 @@
 
         @pl.when(jnp.logical_not(live))
         def _():
-            out[0, slot] = jnp.zeros((rows, width), jnp.float32)
-
+            out[slot] = jnp.zeros((rows, width), jnp.float32)
+
+        pltpu.make_async_copy(out.at[slot], out_hbm.at[0, slot], out_sem.at[slot]).start()
         return carry
 
     lax.fori_loop(0, slots, compute, 0)
+    for slot in range(slots):
+        pltpu.make_async_copy(out.at[slot], out_hbm.at[0, slot], out_sem.at[slot]).wait()
 
 
 def paired_shards(total, orbitals, interaction, pair_list, flag_list, pair_counts):
@@ -264,11 +267,13 @@
         functools.partial(exchange_kernel, steps, total),
         out_shape=jax.ShapeDtypeStruct((1, slots, rows, width), jnp.float32),
         in_specs=[scalars] * 3 + [in_vmem] * 4 + [in_hbm] * len(pieces),
-        out_specs=in_vmem,
+        out_specs=in_hbm,
         scratch_shapes=[
+            pltpu.VMEM((slots, rows, width), jnp.float32),
             pltpu.VMEM((2, rows, points), jnp.bfloat16),
             pltpu.VMEM((2, slots, points, width), jnp.bfloat16),
             pltpu.SemaphoreType.DMA((2, slots)),
+            pltpu.SemaphoreType.DMA((slots,)),
         ],
         compiler_params=pltpu.CompilerParams(vmem_limit_bytes=24 * 2**20),
         cost_estimate=pl.CostEstimate(

time: 39.6 us -> 39.5 us (level)
  no operation moved by 1% of the time
where the time goes in v5:
time: 39.5 us; the launch traced here: 39.4 us
  starting transfers between devices  18.3 us (46%)
  waiting for transfers between devices  11.9 us (30%)
  Pallas kernels  6.36 us (16%)
  local copies, waits for them, and re-layouts  1.91 us (5%)
  between operations  0.83 us (2%)
    ppermute x8, starting transfers between devices, along_ring(): return lax.ppermute(value, ('pb', 'row'), moves)  12.8 us
    ppermute x8, waiting for transfers between devices, along_ring(): return lax.ppermute(value, ('pb', 'row'), moves)  10.2 us
    pallas_call x1, Pallas kernels, paired_shards(): pl.pallas_call(functools.partial(exchange_kernel, steps, total), out_shap...  6.36 us
    ppermute x2, starting transfers between devices, other_chip(): lax.ppermute(value, 'row', [(r, r ^ CORES) for r in range(row_total)])  4.44 us
    ppermute x10, waiting for transfers between devices, other_core(): return lax.ppermute(value, 'row', [(r, r ^ 1) for r in range(row_total)])  1.77 us
    dynamic_slice x1, local copies, waits for them, and re-layouts, paired_shards(): w_away = lax.dynamic_slice_in_dim(w_block, (1 - x) * chip, chip, axis=2)  1.24 us
    ppermute x10, starting transfers between devices, other_core(): return lax.ppermute(value, 'row', [(r, r ^ 1) for r in range(row_total)])  1.1 us
  transfers between devices with their start and end apart: 20, of which 13 were waited for; matrix products, arithmetic and copies ran while one was open for 3% of the time, Pallas kernels for 0%

profile of v5, /device:TPU:0, one launch (start us, length us, event | category | flops | bytes accessed | tf_op | source)
XLA Modules:
  0.0 39.4 jit_solution(10453415393528223871)
XLA Ops:
  0.0 2.9 %collective-permute-start.3 = (bf16[320,128]{1,0:T(8,128)(2,1)}, bf16[320,128]{1,0:T(8,128)(2,1)S(1)}, u32[]{:S(2)}, u32[]{:S(2)}) collective-permute-start(bf16[320,128]{1,0:T(8,128)(2,1)} %bitcast.7), channel_id=1, source_target_pairs={{0,2},{1,3},{2,0},{3,1},{4,6},{5,7},{6,4},{7,5},{8,10},{9,11},{10,... | collective-permute-start | bytes 245768 | tf_op jit(solution)/shard_map/ppermute | solution.py:212
  3.0 1.2 %dynamic-slice_bitcast_fusion = bf16[2,320,640]{2,1,0:T(8,128)(2,1)S(1)} fusion(bf16[2,1,320,1280]{3,2,1,0:T(8,128)(2,1)} %refs_3_.1, s32[]{:T(128)S(6)} %select_n.20), kind=kLoop, calls=%fused_computation | loop fusion | bytes 1638404 | tf_op jit(solution)/shard_map/dynamic_slice | solution.py:231
  4.2 0.2 collective-permute-done
  4.5 1.6 %collective-permute-start.1 = (bf16[640,128]{1,0:T(8,128)(2,1)S(1)}, bf16[640,128]{1,0:T(8,128)(2,1)S(1)}, u32[]{:S(2)}, u32[]{:S(2)}) collective-permute-start(bf16[640,128]{1,0:T(8,128)(2,1)S(1)} %pad_maximum_fusion.refs_7_), channel_id=1, source_target_pairs={{0,8},{1,5},{2,10},{3,7},{8,16},{9,1},{10,18},{11,3},{16,24},{17,9... | collective-permute-start | bytes 491528 | tf_op jit(solution)/shard_map/ppermute | solution.py:221
  6.1 1.5 %collective-permute-start.4 = (bf16[2,320,640]{2,1,0:T(8,128)(2,1)S(1)}, bf16[2,320,640]{2,1,0:T(8,128)(2,1)S(1)}, u32[]{:S(2)}, u32[]{:S(2)}) collective-permute-start(bf16[2,320,640]{2,1,0:T(8,128)(2,1)S(1)} %dynamic-slice_bitcast_fusion), channel_id=1, source_target_pairs={{0,2},{1,3},{2,0},{3,1},{4,6},{5,7},{6,4},{7,5},{8,10},{9,11},{10,... | collective-permute-start | bytes 2457608 | tf_op jit(solution)/shard_map/ppermute | solution.py:212
  7.6 1.6 %collective-permute-start.7 = (bf16[640,128]{1,0:T(8,128)(2,1)S(1)}, bf16[640,128]{1,0:T(8,128)(2,1)S(1)}, u32[]{:S(2)}, u32[]{:S(2)}) collective-permute-start(bf16[640,128]{1,0:T(8,128)(2,1)S(1)} %constant_dynamic-update-slice_fusion.refs_8_), channel_id=1, source_target_pairs={{0,8},{1,5},{2,10},{3,7},{8,16},{9,1},{10,18},{11,3},{16,24},{17,9... | collective-permute-start | bytes 491528 | tf_op jit(solution)/shard_map/ppermute | solution.py:221
  9.3 0.5 %collective-permute-done.1.refs_9_ = bf16[640,128]{1,0:T(8,128)(2,1)S(1)} collective-permute-done((bf16[640,128]{1,0:T(8,128)(2,1)S(1)}, bf16[640,128]{1,0:T(8,128)(2,1)S(1)}, u32[]{:S(2)}, u32[]{:S(2)}) %collective-permute-start.1) | collective-permute-done | bytes 163872 | tf_op jit(solution)/shard_map/ppermute | solution.py:221
  9.8 1.6 %collective-permute-start.6 = (bf16[640,128]{1,0:T(8,128)(2,1)S(1)}, bf16[640,128]{1,0:T(8,128)(2,1)S(1)}, u32[]{:S(2)}, u32[]{:S(2)}) collective-permute-start(bf16[640,128]{1,0:T(8,128)(2,1)S(1)} %collective-permute-done.1.refs_9_), channel_id=1, source_target_pairs={{0,8},{1,5},{2,10},{3,7},{8,16},{9,1},{10,18},{11,3},{16,24},{17,9... | collective-permute-start | bytes 491528 | tf_op jit(solution)/shard_map/ppermute | solution.py:221
  11.4 1.6 %collective-permute-done.7.refs_10_ = bf16[640,128]{1,0:T(8,128)(2,1)S(1)} collective-permute-done((bf16[640,128]{1,0:T(8,128)(2,1)S(1)}, bf16[640,128]{1,0:T(8,128)(2,1)S(1)}, u32[]{:S(2)}, u32[]{:S(2)}) %collective-permute-start.7) | collective-permute-done | bytes 163872 | tf_op jit(solution)/shard_map/ppermute | solution.py:221
  13.0 1.6 %collective-permute-start.9 = (bf16[640,128]{1,0:T(8,128)(2,1)S(1)}, bf16[640,128]{1,0:T(8,128)(2,1)S(1)}, u32[]{:S(2)}, u32[]{:S(2)}) collective-permute-start(bf16[640,128]{1,0:T(8,128)(2,1)S(1)} %collective-permute-done.7.refs_10_), channel_id=1, source_target_pairs={{0,8},{1,5},{2,10},{3,7},{8,16},{9,1},{10,18},{11,3},{16,24},{17,9... | collective-permute-start | bytes 491528 | tf_op jit(solution)/shard_map/ppermute | solution.py:221
  14.6 0.6 %collective-permute-done.6.refs_11_ = bf16[640,128]{1,0:T(8,128)(2,1)S(1)} collective-permute-done((bf16[640,128]{1,0:T(8,128)(2,1)S(1)}, bf16[640,128]{1,0:T(8,128)(2,1)S(1)}, u32[]{:S(2)}, u32[]{:S(2)}) %collective-permute-start.6) | collective-permute-done | bytes 163872 | tf_op jit(solution)/shard_map/ppermute | solution.py:221
  15.2 1.6 %collective-permute-start.8 = (bf16[640,128]{1,0:T(8,128)(2,1)S(1)}, bf16[640,128]{1,0:T(8,128)(2,1)S(1)}, u32[]{:S(2)}, u32[]{:S(2)}) collective-permute-start(bf16[640,128]{1,0:T(8,128)(2,1)S(1)} %collective-permute-done.6.refs_11_), channel_id=1, source_target_pairs={{0,8},{1,5},{2,10},{3,7},{8,16},{9,1},{10,18},{11,3},{16,24},{17,9... | collective-permute-start | bytes 491528 | tf_op jit(solution)/shard_map/ppermute | solution.py:221
  16.7 1.6 %collective-permute-done.9.refs_12_ = bf16[640,128]{1,0:T(8,128)(2,1)S(1)} collective-permute-done((bf16[640,128]{1,0:T(8,128)(2,1)S(1)}, bf16[640,128]{1,0:T(8,128)(2,1)S(1)}, u32[]{:S(2)}, u32[]{:S(2)}) %collective-permute-start.9) | collective-permute-done | bytes 163872 | tf_op jit(solution)/shard_map/ppermute | solution.py:221
  18.4 1.6 %collective-permute-start.12 = (bf16[640,128]{1,0:T(8,128)(2,1)S(1)}, bf16[640,128]{1,0:T(8,128)(2,1)S(1)}, u32[]{:S(2)}, u32[]{:S(2)}) collective-permute-start(bf16[640,128]{1,0:T(8,128)(2,1)S(1)} %collective-permute-done.9.refs_12_), channel_id=1, source_target_pairs={{0,8},{1,5},{2,10},{3,7},{8,16},{9,1},{10,18},{11,3},{16,24},{17,9... | collective-permute-start | bytes 491528 | tf_op jit(solution)/shard_map/ppermute | solution.py:221
  20.0 0.5 %collective-permute-done.8.refs_13_ = bf16[640,128]{1,0:T(8,128)(2,1)S(1)} collective-permute-done((bf16[640,128]{1,0:T(8,128)(2,1)S(1)}, bf16[640,128]{1,0:T(8,128)(2,1)S(1)}, u32[]{:S(2)}, u32[]{:S(2)}) %collective-permute-start.8) | collective-permute-done | bytes 163872 | tf_op jit(solution)/shard_map/ppermute | solution.py:221
  20.5 1.6 %collective-permute-start.11 = (bf16[640,128]{1,0:T(8,128)(2,1)S(1)}, bf16[640,128]{1,0:T(8,128)(2,1)S(1)}, u32[]{:S(2)}, u32[]{:S(2)}) collective-permute-start(bf16[640,128]{1,0:T(8,128)(2,1)S(1)} %collective-permute-done.8.refs_13_), channel_id=1, source_target_pairs={{0,8},{1,5},{2,10},{3,7},{8,16},{9,1},{10,18},{11,3},{16,24},{17,9... | collective-permute-start | bytes 491528 | tf_op jit(solution)/shard_map/ppermute | solution.py:221
  22.1 1.7 %collective-permute-done.12.refs_14_ = bf16[640,128]{1,0:T(8,128)(2,1)S(1)} collective-permute-done((bf16[640,128]{1,0:T(8,128)(2,1)S(1)}, bf16[640,128]{1,0:T(8,128)(2,1)S(1)}, u32[]{:S(2)}, u32[]{:S(2)}) %collective-permute-start.12) | collective-permute-done | bytes 163872 | tf_op jit(solution)/shard_map/ppermute | solution.py:221
  23.7 1.6 %collective-permute-start.14 = (bf16[640,128]{1,0:T(8,128)(2,1)S(1)}, bf16[640,128]{1,0:T(8,128)(2,1)S(1)}, u32[]{:S(2)}, u32[]{:S(2)}) collective-permute-start(bf16[640,128]{1,0:T(8,128)(2,1)S(1)} %collective-permute-done.12.refs_14_), channel_id=1, source_target_pairs={{0,8},{1,5},{2,10},{3,7},{8,16},{9,1},{10,18},{11,3},{16,24},{17,9... | collective-permute-start | bytes 491528 | tf_op jit(solution)/shard_map/ppermute | solution.py:221
  25.3 0.5 %collective-permute-done.11.refs_21_ = bf16[640,128]{1,0:T(8,128)(2,1)S(1)} collective-permute-done((bf16[640,128]{1,0:T(8,128)(2,1)S(1)}, bf16[640,128]{1,0:T(8,128)(2,1)S(1)}, u32[]{:S(2)}, u32[]{:S(2)}) %collective-permute-start.11) | collective-permute-done | bytes 163872 | tf_op jit(solution)/shard_map/ppermute | solution.py:221
  25.8 3.3 %collective-permute-done.14.refs_22_ = bf16[640,128]{1,0:T(8,128)(2,1)S(1)} collective-permute-done((bf16[640,128]{1,0:T(8,128)(2,1)S(1)}, bf16[640,128]{1,0:T(8,128)(2,1)S(1)}, u32[]{:S(2)}, u32[]{:S(2)}) %collective-permute-start.14) | collective-permute-done | bytes 163872 | tf_op jit(solution)/shard_map/ppermute | solution.py:221
  29.1 0.5 %collective-permute-start.16 = (bf16[640,128]{1,0:T(8,128)(2,1)S(1)}, bf16[640,128]{1,0:T(8,128)(2,1)S(1)}, u32[]{:S(2)}, u32[]{:S(2)}) collective-permute-start(bf16[640,128]{1,0:T(8,128)(2,1)S(1)} %collective-permute-done.6.refs_11_), channel_id=1, source_target_pairs={{0,1},{1,0},{2,3},{3,2},{4,5},{5,4},{6,7},{7,6},{8,9},{9,8},{10,11... | collective-permute-start | bytes 491528 | tf_op jit(solution)/shard_map/ppermute | solution.py:209
  29.6 0.1 collective-permute-start.18
  29.6 0.4 %collective-permute-start.17 = (bf16[640,128]{1,0:T(8,128)(2,1)S(1)}, bf16[640,128]{1,0:T(8,128)(2,1)S(1)}, u32[]{:S(2)}, u32[]{:S(2)}) collective-permute-start(bf16[640,128]{1,0:T(8,128)(2,1)S(1)} %collective-permute-done.9.refs_12_), channel_id=1, source_target_pairs={{0,1},{1,0},{2,3},{3,2},{4,5},{5,4},{6,7},{7,6},{8,9},{9,8},{10,11... | collective-permute-start | bytes 491528 | tf_op jit(solution)/shard_map/ppermute | solution.py:209
  30.1 0.1 collective-permute-start.19
  30.8 0.8 %collective-permute-done.16.refs_17_ = bf16[640,128]{1,0:T(8,128)(2,1)S(1)} collective-permute-done((bf16[640,128]{1,0:T(8,128)(2,1)S(1)}, bf16[640,128]{1,0:T(8,128)(2,1)S(1)}, u32[]{:S(2)}, u32[]{:S(2)}) %collective-permute-start.16) | collective-permute-done | bytes 163872 | tf_op jit(solution)/shard_map/ppermute | solution.py:209
  31.6 0.2 collective-permute-done.18.refs_19_
  31.9 0.2 collective-permute-done.17.refs_18_
  32.1 0.2 collective-permute-done.19.refs_20_
  32.5 0.1 copy-done.16
  32.5 0.2 copy-done.17
  32.8 0.2 copy-done.18
  33.0 6.4 %shard_map.55 = f32[1,3,320,128]{3,2,1,0:T(8,128)} custom-call(s32[1,2,3]{2,1,0:T(2,128)S(1)} %bitcast.6, s32[1,3]{1,0:T(1,128)S(1)} %copy-done.2, s32[1]{0:T(128)S(6)} %copy.7.refs_2_, bf16[2,1,320,1280]{3,2,1,0:T(8,128)(2,1)S(1)} %copy-done, bf16[2,320,384]{2,1,0:T(8,128)(2,1)S(1)} %collective-permute-done.2.refs_4_, ...), custom_call_target="tpu_custom_call" | custom-call | flops 1258291200 | bytes 8388608 | tf_op jit(solution)/shard_map/pallas_call | solution.py:266
  (54 shorter events, 0.2 us)
Async XLA Ops:
  0.0 9.3 %copy-start = (bf16[2,1,320,1280]{3,2,1,0:T(8,128)(2,1)S(1)}, bf16[2,1,320,1280]{3,2,1,0:T(8,128)(2,1)}, u32[]{:S(2)}) copy-start(bf16[2,1,320,1280]{3,2,1,0:T(8,128)(2,1)} %refs_3_.1) | copy-start | bytes 4915204
  0.0 6.1 %collective-permute-start.3 = (bf16[320,128]{1,0:T(8,128)(2,1)}, bf16[320,128]{1,0:T(8,128)(2,1)S(1)}, u32[]{:S(2)}, u32[]{:S(2)}) collective-permute-start(bf16[320,128]{1,0:T(8,128)(2,1)} %bitcast.7), channel_id=1, source_target_pairs={{0,2},{1,3},{2,0},{3,1},{4,6},{5,7},{6,4},{7,5},{8,10},{9,11},{10,... | collective-permute-start | bytes 245768 | tf_op jit(solution)/shard_map/ppermute | solution.py:212
  2.9 1.5 %collective-permute-start = (bf16[320,128]{1,0:T(8,128)(2,1)}, bf16[320,128]{1,0:T(8,128)(2,1)S(1)}, u32[]{:S(2)}, u32[]{:S(2)}) collective-permute-start(bf16[320,128]{1,0:T(8,128)(2,1)} %bitcast.8), channel_id=1, source_target_pairs={{0,1},{1,0},{2,3},{3,2},{4,5},{5,4},{6,7},{7,6},{8,9},{9,8},{10,11... | collective-permute-start | bytes 245768 | tf_op jit(solution)/shard_map/ppermute | solution.py:209
  2.9 30.0 %copy-start.1 = (s32[1,3,2]{1,2,0:T(2,128)S(1)}, s32[1,3,2]{1,2,0:T(2,128)}, u32[]{:S(2)}) copy-start(s32[1,3,2]{1,2,0:T(2,128)} %param.7) | copy-start | bytes 76
  2.9 30.0 %copy-start.2 = (s32[1,3]{1,0:T(1,128)S(1)}, s32[1,3]{1,0:T(1,128)}, u32[]{:S(2)}) copy-start(s32[1,3]{1,0:T(1,128)} %refs_1_.1) | copy-start | bytes 40
  4.5 27.9 %copy-start.3 = (bf16[640,128]{1,0:T(8,128)(2,1)}, bf16[640,128]{1,0:T(8,128)(2,1)S(1)}, u32[]{:S(2)}) copy-start(bf16[640,128]{1,0:T(8,128)(2,1)S(1)} %pad_maximum_fusion.refs_7_) | copy-start | bytes 491524
  4.5 5.4 %collective-permute-start.1 = (bf16[640,128]{1,0:T(8,128)(2,1)S(1)}, bf16[640,128]{1,0:T(8,128)(2,1)S(1)}, u32[]{:S(2)}, u32[]{:S(2)}) collective-permute-start(bf16[640,128]{1,0:T(8,128)(2,1)S(1)} %pad_maximum_fusion.refs_7_), channel_id=1, source_target_pairs={{0,8},{1,5},{2,10},{3,7},{8,16},{9,1},{10,18},{11,3},{16,24},{17,9... | collective-permute-start | bytes 491528 | tf_op jit(solution)/shard_map/ppermute | solution.py:221
  6.1 1.5 %collective-permute-start.5 = (bf16[320,128]{1,0:T(8,128)(2,1)S(1)}, bf16[320,128]{1,0:T(8,128)(2,1)S(1)}, u32[]{:S(2)}, u32[]{:S(2)}) collective-permute-start(bf16[320,128]{1,0:T(8,128)(2,1)S(1)} %collective-permute-done.3), channel_id=1, source_target_pairs={{0,1},{1,0},{2,3},{3,2},{4,5},{5,4},{6,7},{7,6},{8,9},{9,8},{10,11... | collective-permute-start | bytes 245768 | tf_op jit(solution)/shard_map/ppermute | solution.py:209
  6.1 23.0 %collective-permute-start.4 = (bf16[2,320,640]{2,1,0:T(8,128)(2,1)S(1)}, bf16[2,320,640]{2,1,0:T(8,128)(2,1)S(1)}, u32[]{:S(2)}, u32[]{:S(2)}) collective-permute-start(bf16[2,320,640]{2,1,0:T(8,128)(2,1)S(1)} %dynamic-slice_bitcast_fusion), channel_id=1, source_target_pairs={{0,2},{1,3},{2,0},{3,1},{4,6},{5,7},{6,4},{7,5},{8,10},{9,11},{10,... | collective-permute-start | bytes 2457608 | tf_op jit(solution)/shard_map/ppermute | solution.py:212
  7.6 24.7 %copy-start.4 = (bf16[640,128]{1,0:T(8,128)(2,1)}, bf16[640,128]{1,0:T(8,128)(2,1)S(1)}, u32[]{:S(2)}) copy-start(bf16[640,128]{1,0:T(8,128)(2,1)S(1)} %constant_dynamic-update-slice_fusion.refs_8_) | copy-start | bytes 491524
  7.6 5.4 %collective-permute-start.7 = (bf16[640,128]{1,0:T(8,128)(2,1)S(1)}, bf16[640,128]{1,0:T(8,128)(2,1)S(1)}, u32[]{:S(2)}, u32[]{:S(2)}) collective-permute-start(bf16[640,128]{1,0:T(8,128)(2,1)S(1)} %constant_dynamic-update-slice_fusion.refs_8_), channel_id=1, source_target_pairs={{0,8},{1,5},{2,10},{3,7},{8,16},{9,1},{10,18},{11,3},{16,24},{17,9... | collective-permute-start | bytes 491528 | tf_op jit(solution)/shard_map/ppermute | solution.py:221
  9.8 22.5 %copy-start.5 = (bf16[640,128]{1,0:T(8,128)(2,1)}, bf16[640,128]{1,0:T(8,128)(2,1)S(1)}, u32[]{:S(2)}) copy-start(bf16[640,128]{1,0:T(8,128)(2,1)S(1)} %collective-permute-done.1.refs_9_) | copy-start | bytes 491524
  9.8 13.9 %collective-permute-start.2 = (bf16[2,320,384]{2,1,0:T(8,128)(2,1)S(1)}, bf16[2,320,384]{2,1,0:T(8,128)(2,1)S(1)}, u32[]{:S(2)}, u32[]{:S(2)}) collective-permute-start(bf16[2,320,384]{2,1,0:T(8,128)(2,1)S(1)} %dynamic-slice_bitcast_fusion.1), channel_id=1, source_target_pairs={{0,1},{1,0},{2,3},{3,2},{4,5},{5,4},{6,7},{7,6},{8,9},{9,8},{10,11... | collective-permute-start | bytes 1474568 | tf_op jit(solution)/shard_map/ppermute | solution.py:209
  9.8 5.3 %collective-permute-start.6 = (bf16[640,128]{1,0:T(8,128)(2,1)S(1)}, bf16[640,128]{1,0:T(8,128)(2,1)S(1)}, u32[]{:S(2)}, u32[]{:S(2)}) collective-permute-start(bf16[640,128]{1,0:T(8,128)(2,1)S(1)} %collective-permute-done.1.refs_9_), channel_id=1, source_target_pairs={{0,8},{1,5},{2,10},{3,7},{8,16},{9,1},{10,18},{11,3},{16,24},{17,9... | collective-permute-start | bytes 491528 | tf_op jit(solution)/shard_map/ppermute | solution.py:221
  13.0 19.3 %copy-start.6 = (bf16[640,128]{1,0:T(8,128)(2,1)}, bf16[640,128]{1,0:T(8,128)(2,1)S(1)}, u32[]{:S(2)}) copy-start(bf16[640,128]{1,0:T(8,128)(2,1)S(1)} %collective-permute-done.7.refs_10_) | copy-start | bytes 491524
  13.0 5.3 %collective-permute-start.9 = (bf16[640,128]{1,0:T(8,128)(2,1)S(1)}, bf16[640,128]{1,0:T(8,128)(2,1)S(1)}, u32[]{:S(2)}, u32[]{:S(2)}) collective-permute-start(bf16[640,128]{1,0:T(8,128)(2,1)S(1)} %collective-permute-done.7.refs_10_), channel_id=1, source_target_pairs={{0,8},{1,5},{2,10},{3,7},{8,16},{9,1},{10,18},{11,3},{16,24},{17,9... | collective-permute-start | bytes 491528 | tf_op jit(solution)/shard_map/ppermute | solution.py:221
  14.6 3.8 %collective-permute-start.10 = (bf16[640,128]{1,0:T(8,128)(2,1)S(1)}, bf16[640,128]{1,0:T(8,128)(2,1)S(1)}, u32[]{:S(2)}, u32[]{:S(2)}) collective-permute-start(bf16[640,128]{1,0:T(8,128)(2,1)S(1)} %collective-permute-done.7.refs_10_), channel_id=1, source_target_pairs={{0,1},{1,0},{2,3},{3,2},{4,5},{5,4},{6,7},{7,6},{8,9},{9,8},{10,11... | collective-permute-start | bytes 491528 | tf_op jit(solution)/shard_map/ppermute | solution.py:209
  15.2 17.2 %copy-start.7 = (bf16[640,128]{1,0:T(8,128)(2,1)}, bf16[640,128]{1,0:T(8,128)(2,1)S(1)}, u32[]{:S(2)}) copy-start(bf16[640,128]{1,0:T(8,128)(2,1)S(1)} %collective-permute-done.6.refs_11_) | copy-start | bytes 491524
  15.2 5.3 %collective-permute-start.8 = (bf16[640,128]{1,0:T(8,128)(2,1)S(1)}, bf16[640,128]{1,0:T(8,128)(2,1)S(1)}, u32[]{:S(2)}, u32[]{:S(2)}) collective-permute-start(bf16[640,128]{1,0:T(8,128)(2,1)S(1)} %collective-permute-done.6.refs_11_), channel_id=1, source_target_pairs={{0,8},{1,5},{2,10},{3,7},{8,16},{9,1},{10,18},{11,3},{16,24},{17,9... | collective-permute-start | bytes 491528 | tf_op jit(solution)/shard_map/ppermute | solution.py:221
  18.3 14.0 %copy-start.8 = (bf16[640,128]{1,0:T(8,128)(2,1)}, bf16[640,128]{1,0:T(8,128)(2,1)S(1)}, u32[]{:S(2)}) copy-start(bf16[640,128]{1,0:T(8,128)(2,1)S(1)} %collective-permute-done.9.refs_12_) | copy-start | bytes 491524
  18.3 3.7 %collective-permute-start.13 = (bf16[640,128]{1,0:T(8,128)(2,1)S(1)}, bf16[640,128]{1,0:T(8,128)(2,1)S(1)}, u32[]{:S(2)}, u32[]{:S(2)}) collective-permute-start(bf16[640,128]{1,0:T(8,128)(2,1)S(1)} %collective-permute-done.1.refs_9_), channel_id=1, source_target_pairs={{0,1},{1,0},{2,3},{3,2},{4,5},{5,4},{6,7},{7,6},{8,9},{9,8},{10,11... | collective-permute-start | bytes 491528 | tf_op jit(solution)/shard_map/ppermute | solution.py:209
  18.3 14.0 %copy-start.9 = (bf16[640,128]{1,0:T(8,128)(2,1)}, bf16[640,128]{1,0:T(8,128)(2,1)S(1)}, u32[]{:S(2)}) copy-start(bf16[640,128]{1,0:T(8,128)(2,1)S(1)} %collective-permute-done.10.refs_16_) | copy-start | bytes 491524
  18.4 5.4 %collective-permute-start.12 = (bf16[640,128]{1,0:T(8,128)(2,1)S(1)}, bf16[640,128]{1,0:T(8,128)(2,1)S(1)}, u32[]{:S(2)}, u32[]{:S(2)}) collective-permute-start(bf16[640,128]{1,0:T(8,128)(2,1)S(1)} %collective-permute-done.9.refs_12_), channel_id=1, source_target_pairs={{0,8},{1,5},{2,10},{3,7},{8,16},{9,1},{10,18},{11,3},{16,24},{17,9... | collective-permute-start | bytes 491528 | tf_op jit(solution)/shard_map/ppermute | solution.py:221
  20.5 11.9 %copy-start.10 = (bf16[640,128]{1,0:T(8,128)(2,1)}, bf16[640,128]{1,0:T(8,128)(2,1)S(1)}, u32[]{:S(2)}) copy-start(bf16[640,128]{1,0:T(8,128)(2,1)S(1)} %collective-permute-done.8.refs_13_) | copy-start | bytes 491524
  20.5 5.3 %collective-permute-start.11 = (bf16[640,128]{1,0:T(8,128)(2,1)S(1)}, bf16[640,128]{1,0:T(8,128)(2,1)S(1)}, u32[]{:S(2)}, u32[]{:S(2)}) collective-permute-start(bf16[640,128]{1,0:T(8,128)(2,1)S(1)} %collective-permute-done.8.refs_13_), channel_id=1, source_target_pairs={{0,8},{1,5},{2,10},{3,7},{8,16},{9,1},{10,18},{11,3},{16,24},{17,9... | collective-permute-start | bytes 491528 | tf_op jit(solution)/shard_map/ppermute | solution.py:221
  22.1 10.4 %copy-start.11 = (bf16[640,128]{1,0:T(8,128)(2,1)}, bf16[640,128]{1,0:T(8,128)(2,1)S(1)}, u32[]{:S(2)}) copy-start(bf16[640,128]{1,0:T(8,128)(2,1)S(1)} %collective-permute-done.13.refs_15_) | copy-start | bytes 491524
  23.7 5.3 %collective-permute-start.14 = (bf16[640,128]{1,0:T(8,128)(2,1)S(1)}, bf16[640,128]{1,0:T(8,128)(2,1)S(1)}, u32[]{:S(2)}, u32[]{:S(2)}) collective-permute-start(bf16[640,128]{1,0:T(8,128)(2,1)S(1)} %collective-permute-done.12.refs_14_), channel_id=1, source_target_pairs={{0,8},{1,5},{2,10},{3,7},{8,16},{9,1},{10,18},{11,3},{16,24},{17,9... | collective-permute-start | bytes 491528 | tf_op jit(solution)/shard_map/ppermute | solution.py:221
  29.1 3.3 %collective-permute-start.15 = (bf16[2,320,640]{2,1,0:T(8,128)(2,1)S(1)}, bf16[2,320,640]{2,1,0:T(8,128)(2,1)S(1)}, u32[]{:S(2)}, u32[]{:S(2)}) collective-permute-start(bf16[2,320,640]{2,1,0:T(8,128)(2,1)S(1)} %collective-permute-done.4.refs_5_), channel_id=1, source_target_pairs={{0,1},{1,0},{2,3},{3,2},{4,5},{5,4},{6,7},{7,6},{8,9},{9,8},{10,11... | collective-permute-start | bytes 2457608 | tf_op jit(solution)/shard_map/ppermute | solution.py:209
  29.1 2.6 %collective-permute-start.16 = (bf16[640,128]{1,0:T(8,128)(2,1)S(1)}, bf16[640,128]{1,0:T(8,128)(2,1)S(1)}, u32[]{:S(2)}, u32[]{:S(2)}) collective-permute-start(bf16[640,128]{1,0:T(8,128)(2,1)S(1)} %collective-permute-done.6.refs_11_), channel_id=1, source_target_pairs={{0,1},{1,0},{2,3},{3,2},{4,5},{5,4},{6,7},{7,6},{8,9},{9,8},{10,11... | collective-permute-start | bytes 491528 | tf_op jit(solution)/shard_map/ppermute | solution.py:209
  29.6 2.3 %collective-permute-start.18 = (bf16[640,128]{1,0:T(8,128)(2,1)S(1)}, bf16[640,128]{1,0:T(8,128)(2,1)S(1)}, u32[]{:S(2)}, u32[]{:S(2)}) collective-permute-start(bf16[640,128]{1,0:T(8,128)(2,1)S(1)} %collective-permute-done.8.refs_13_), channel_id=1, source_target_pairs={{0,1},{1,0},{2,3},{3,2},{4,5},{5,4},{6,7},{7,6},{8,9},{9,8},{10,11... | collective-permute-start | bytes 491528 | tf_op jit(solution)/shard_map/ppermute | solution.py:209
  29.6 2.5 %collective-permute-start.17 = (bf16[640,128]{1,0:T(8,128)(2,1)S(1)}, bf16[640,128]{1,0:T(8,128)(2,1)S(1)}, u32[]{:S(2)}, u32[]{:S(2)}) collective-permute-start(bf16[640,128]{1,0:T(8,128)(2,1)S(1)} %collective-permute-done.9.refs_12_), channel_id=1, source_target_pairs={{0,1},{1,0},{2,3},{3,2},{4,5},{5,4},{6,7},{7,6},{8,9},{9,8},{10,11... | collective-permute-start | bytes 491528 | tf_op jit(solution)/shard_map/ppermute | solution.py:209
  30.1 2.2 %collective-permute-start.19 = (bf16[640,128]{1,0:T(8,128)(2,1)S(1)}, bf16[640,128]{1,0:T(8,128)(2,1)S(1)}, u32[]{:S(2)}, u32[]{:S(2)}) collective-permute-start(bf16[640,128]{1,0:T(8,128)(2,1)S(1)} %collective-permute-done.12.refs_14_), channel_id=1, source_target_pairs={{0,1},{1,0},{2,3},{3,2},{4,5},{5,4},{6,7},{7,6},{8,9},{9,8},{10,11... | collective-permute-start | bytes 491528 | tf_op jit(solution)/shard_map/ppermute | solution.py:209
  (8 other events, 26.0 us)

commit v6 on v5

--- a/solution.py
+++ b/solution.py
@@ -124,8 +124,6 @@
         ).wait()
 
     fetch(0)
-    for slot in range(1, slots):
-        fetch(slot)
     any_turned = False
     for slot in range(slots):
         any_turned = jnp.logical_or(
@@ -146,6 +144,9 @@
             ):
                 eff[0, :, at : at + rows] = block[0, :, lanes].T[skip : skip + rows]
                 eff[1, :, at : at + rows] = -block[1, :, lanes].T[skip : skip + rows]
+
+    for slot in range(1, slots):
+        fetch(slot)
 
     def apply(slot, w_real, w_imag, mine):
         local = full[1, slot, pl.ds(pl.multiple_of(mine * rows, rows), rows)]
@@ -249,7 +250,7 @@
     ring = [wave[k] for k in range(1, steps + 1) for wave in (first, second)]
     last = [first[steps + 1], second[steps + 1]]
     swap_first.append(other_core(after(first[steps - 1], last[0])))
-    swap_second.append(other_core(after(second[steps - 1], *last)))
+    swap_second.append(other_core(after(second[steps - 1], last[0])))
     swap_first.append(other_core(after(first[steps], last[0])))
     swap_second.append(other_core(after(second[steps], *last)))
     swap = [wave[k] for k in range(steps) for wave in (swap_first, swap_second)]

time: 39.5 us -> 39.5 us (level)
  no operation moved by 1% of the time
where the time goes in v6:
time: 39.5 us; the launch traced here: 39.4 us
  starting transfers between devices  18.3 us (46%)
  waiting for transfers between devices  11.9 us (30%)
  Pallas kernels  6.36 us (16%)
  local copies, waits for them, and re-layouts  1.91 us (5%)
  between operations  0.83 us (2%)
    ppermute x8, starting transfers between devices, along_ring(): return lax.ppermute(value, ('pb', 'row'), moves)  12.8 us
    ppermute x8, waiting for transfers between devices, along_ring(): return lax.ppermute(value, ('pb', 'row'), moves)  10.2 us
    pallas_call x1, Pallas kernels, paired_shards(): pl.pallas_call(functools.partial(exchange_kernel, steps, total), out_shap...  6.36 us
    ppermute x2, starting transfers between devices, other_chip(): lax.ppermute(value, 'row', [(r, r ^ CORES) for r in range(row_total)])  4.44 us
    ppermute x10, waiting for transfers between devices, other_core(): return lax.ppermute(value, 'row', [(r, r ^ 1) for r in range(row_total)])  1.77 us
    dynamic_slice x1, local copies, waits for them, and re-layouts, paired_shards(): w_away = lax.dynamic_slice_in_dim(w_block, (1 - x) * chip, chip, axis=2)  1.24 us
    ppermute x10, starting transfers between devices, other_core(): return lax.ppermute(value, 'row', [(r, r ^ 1) for r in range(row_total)])  1.1 us
  transfers between devices with their start and end apart: 20, of which 13 were waited for; matrix products, arithmetic and copies ran while one was open for 3% of the time, Pallas kernels for 0%

profile of v6, /device:TPU:0, one launch (start us, length us, event | category | flops | bytes accessed | tf_op | source)
XLA Modules:
  0.0 39.4 jit_solution(3592261063969236933)
XLA Ops:
  0.0 2.9 %collective-permute-start.3 = (bf16[320,128]{1,0:T(8,128)(2,1)}, bf16[320,128]{1,0:T(8,128)(2,1)S(1)}, u32[]{:S(2)}, u32[]{:S(2)}) collective-permute-start(bf16[320,128]{1,0:T(8,128)(2,1)} %bitcast.7), channel_id=1, source_target_pairs={{0,2},{1,3},{2,0},{3,1},{4,6},{5,7},{6,4},{7,5},{8,10},{9,11},{10,... | collective-permute-start | bytes 245768 | tf_op jit(solution)/shard_map/ppermute | solution.py:213
  3.0 1.2 %dynamic-slice_bitcast_fusion = bf16[2,320,640]{2,1,0:T(8,128)(2,1)S(1)} fusion(bf16[2,1,320,1280]{3,2,1,0:T(8,128)(2,1)} %refs_3_.1, s32[]{:T(128)S(6)} %select_n.20), kind=kLoop, calls=%fused_computation | loop fusion | bytes 1638404 | tf_op jit(solution)/shard_map/dynamic_slice | solution.py:232
  4.2 0.2 collective-permute-done
  4.5 1.6 %collective-permute-start.1 = (bf16[640,128]{1,0:T(8,128)(2,1)S(1)}, bf16[640,128]{1,0:T(8,128)(2,1)S(1)}, u32[]{:S(2)}, u32[]{:S(2)}) collective-permute-start(bf16[640,128]{1,0:T(8,128)(2,1)S(1)} %pad_maximum_fusion.refs_7_), channel_id=1, source_target_pairs={{0,8},{1,5},{2,10},{3,7},{8,16},{9,1},{10,18},{11,3},{16,24},{17,9... | collective-permute-start | bytes 491528 | tf_op jit(solution)/shard_map/ppermute | solution.py:222
  6.1 1.5 %collective-permute-start.4 = (bf16[2,320,640]{2,1,0:T(8,128)(2,1)S(1)}, bf16[2,320,640]{2,1,0:T(8,128)(2,1)S(1)}, u32[]{:S(2)}, u32[]{:S(2)}) collective-permute-start(bf16[2,320,640]{2,1,0:T(8,128)(2,1)S(1)} %dynamic-slice_bitcast_fusion), channel_id=1, source_target_pairs={{0,2},{1,3},{2,0},{3,1},{4,6},{5,7},{6,4},{7,5},{8,10},{9,11},{10,... | collective-permute-start | bytes 2457608 | tf_op jit(solution)/shard_map/ppermute | solution.py:213
  7.6 1.6 %collective-permute-start.7 = (bf16[640,128]{1,0:T(8,128)(2,1)S(1)}, bf16[640,128]{1,0:T(8,128)(2,1)S(1)}, u32[]{:S(2)}, u32[]{:S(2)}) collective-permute-start(bf16[640,128]{1,0:T(8,128)(2,1)S(1)} %constant_dynamic-update-slice_fusion.refs_8_), channel_id=1, source_target_pairs={{0,8},{1,5},{2,10},{3,7},{8,16},{9,1},{10,18},{11,3},{16,24},{17,9... | collective-permute-start | bytes 491528 | tf_op jit(solution)/shard_map/ppermute | solution.py:222
  9.3 0.5 %collective-permute-done.1.refs_9_ = bf16[640,128]{1,0:T(8,128)(2,1)S(1)} collective-permute-done((bf16[640,128]{1,0:T(8,128)(2,1)S(1)}, bf16[640,128]{1,0:T(8,128)(2,1)S(1)}, u32[]{:S(2)}, u32[]{:S(2)}) %collective-permute-start.1) | collective-permute-done | bytes 163872 | tf_op jit(solution)/shard_map/ppermute | solution.py:222
  9.8 1.6 %collective-permute-start.6 = (bf16[640,128]{1,0:T(8,128)(2,1)S(1)}, bf16[640,128]{1,0:T(8,128)(2,1)S(1)}, u32[]{:S(2)}, u32[]{:S(2)}) collective-permute-start(bf16[640,128]{1,0:T(8,128)(2,1)S(1)} %collective-permute-done.1.refs_9_), channel_id=1, source_target_pairs={{0,8},{1,5},{2,10},{3,7},{8,16},{9,1},{10,18},{11,3},{16,24},{17,9... | collective-permute-start | bytes 491528 | tf_op jit(solution)/shard_map/ppermute | solution.py:222
  11.4 1.6 %collective-permute-done.7.refs_10_ = bf16[640,128]{1,0:T(8,128)(2,1)S(1)} collective-permute-done((bf16[640,128]{1,0:T(8,128)(2,1)S(1)}, bf16[640,128]{1,0:T(8,128)(2,1)S(1)}, u32[]{:S(2)}, u32[]{:S(2)}) %collective-permute-start.7) | collective-permute-done | bytes 163872 | tf_op jit(solution)/shard_map/ppermute | solution.py:222
  13.0 1.6 %collective-permute-start.9 = (bf16[640,128]{1,0:T(8,128)(2,1)S(1)}, bf16[640,128]{1,0:T(8,128)(2,1)S(1)}, u32[]{:S(2)}, u32[]{:S(2)}) collective-permute-start(bf16[640,128]{1,0:T(8,128)(2,1)S(1)} %collective-permute-done.7.refs_10_), channel_id=1, source_target_pairs={{0,8},{1,5},{2,10},{3,7},{8,16},{9,1},{10,18},{11,3},{16,24},{17,9... | collective-permute-start | bytes 491528 | tf_op jit(solution)/shard_map/ppermute | solution.py:222
  14.6 0.6 %collective-permute-done.6.refs_11_ = bf16[640,128]{1,0:T(8,128)(2,1)S(1)} collective-permute-done((bf16[640,128]{1,0:T(8,128)(2,1)S(1)}, bf16[640,128]{1,0:T(8,128)(2,1)S(1)}, u32[]{:S(2)}, u32[]{:S(2)}) %collective-permute-start.6) | collective-permute-done | bytes 163872 | tf_op jit(solution)/shard_map/ppermute | solution.py:222
  15.2 1.6 %collective-permute-start.8 = (bf16[640,128]{1,0:T(8,128)(2,1)S(1)}, bf16[640,128]{1,0:T(8,128)(2,1)S(1)}, u32[]{:S(2)}, u32[]{:S(2)}) collective-permute-start(bf16[640,128]{1,0:T(8,128)(2,1)S(1)} %collective-permute-done.6.refs_11_), channel_id=1, source_target_pairs={{0,8},{1,5},{2,10},{3,7},{8,16},{9,1},{10,18},{11,3},{16,24},{17,9... | collective-permute-start | bytes 491528 | tf_op jit(solution)/shard_map/ppermute | solution.py:222
  16.7 1.6 %collective-permute-done.9.refs_12_ = bf16[640,128]{1,0:T(8,128)(2,1)S(1)} collective-permute-done((bf16[640,128]{1,0:T(8,128)(2,1)S(1)}, bf16[640,128]{1,0:T(8,128)(2,1)S(1)}, u32[]{:S(2)}, u32[]{:S(2)}) %collective-permute-start.9) | collective-permute-done | bytes 163872 | tf_op jit(solution)/shard_map/ppermute | solution.py:222
  18.4 1.6 %collective-permute-start.12 = (bf16[640,128]{1,0:T(8,128)(2,1)S(1)}, bf16[640,128]{1,0:T(8,128)(2,1)S(1)}, u32[]{:S(2)}, u32[]{:S(2)}) collective-permute-start(bf16[640,128]{1,0:T(8,128)(2,1)S(1)} %collective-permute-done.9.refs_12_), channel_id=1, source_target_pairs={{0,8},{1,5},{2,10},{3,7},{8,16},{9,1},{10,18},{11,3},{16,24},{17,9... | collective-permute-start | bytes 491528 | tf_op jit(solution)/shard_map/ppermute | solution.py:222
  20.0 0.5 %collective-permute-done.8.refs_13_ = bf16[640,128]{1,0:T(8,128)(2,1)S(1)} collective-permute-done((bf16[640,128]{1,0:T(8,128)(2,1)S(1)}, bf16[640,128]{1,0:T(8,128)(2,1)S(1)}, u32[]{:S(2)}, u32[]{:S(2)}) %collective-permute-start.8) | collective-permute-done | bytes 163872 | tf_op jit(solution)/shard_map/ppermute | solution.py:222
  20.5 1.6 %collective-permute-start.11 = (bf16[640,128]{1,0:T(8,128)(2,1)S(1)}, bf16[640,128]{1,0:T(8,128)(2,1)S(1)}, u32[]{:S(2)}, u32[]{:S(2)}) collective-permute-start(bf16[640,128]{1,0:T(8,128)(2,1)S(1)} %collective-permute-done.8.refs_13_), channel_id=1, source_target_pairs={{0,8},{1,5},{2,10},{3,7},{8,16},{9,1},{10,18},{11,3},{16,24},{17,9... | collective-permute-start | bytes 491528 | tf_op jit(solution)/shard_map/ppermute | solution.py:222
  22.1 1.7 %collective-permute-done.12.refs_14_ = bf16[640,128]{1,0:T(8,128)(2,1)S(1)} collective-permute-done((bf16[640,128]{1,0:T(8,128)(2,1)S(1)}, bf16[640,128]{1,0:T(8,128)(2,1)S(1)}, u32[]{:S(2)}, u32[]{:S(2)}) %collective-permute-start.12) | collective-permute-done | bytes 163872 | tf_op jit(solution)/shard_map/ppermute | solution.py:222
  23.7 1.6 %collective-permute-start.14 = (bf16[640,128]{1,0:T(8,128)(2,1)S(1)}, bf16[640,128]{1,0:T(8,128)(2,1)S(1)}, u32[]{:S(2)}, u32[]{:S(2)}) collective-permute-start(bf16[640,128]{1,0:T(8,128)(2,1)S(1)} %collective-permute-done.12.refs_14_), channel_id=1, source_target_pairs={{0,8},{1,5},{2,10},{3,7},{8,16},{9,1},{10,18},{11,3},{16,24},{17,9... | collective-permute-start | bytes 491528 | tf_op jit(solution)/shard_map/ppermute | solution.py:222
  25.3 0.5 %collective-permute-done.11.refs_21_ = bf16[640,128]{1,0:T(8,128)(2,1)S(1)} collective-permute-done((bf16[640,128]{1,0:T(8,128)(2,1)S(1)}, bf16[640,128]{1,0:T(8,128)(2,1)S(1)}, u32[]{:S(2)}, u32[]{:S(2)}) %collective-permute-start.11) | collective-permute-done | bytes 163872 | tf_op jit(solution)/shard_map/ppermute | solution.py:222
  25.8 3.3 %collective-permute-done.14.refs_22_ = bf16[640,128]{1,0:T(8,128)(2,1)S(1)} collective-permute-done((bf16[640,128]{1,0:T(8,128)(2,1)S(1)}, bf16[640,128]{1,0:T(8,128)(2,1)S(1)}, u32[]{:S(2)}, u32[]{:S(2)}) %collective-permute-start.14) | collective-permute-done | bytes 163872 | tf_op jit(solution)/shard_map/ppermute | solution.py:222
  29.1 0.5 %collective-permute-start.16 = (bf16[640,128]{1,0:T(8,128)(2,1)S(1)}, bf16[640,128]{1,0:T(8,128)(2,1)S(1)}, u32[]{:S(2)}, u32[]{:S(2)}) collective-permute-start(bf16[640,128]{1,0:T(8,128)(2,1)S(1)} %collective-permute-done.6.refs_11_), channel_id=1, source_target_pairs={{0,1},{1,0},{2,3},{3,2},{4,5},{5,4},{6,7},{7,6},{8,9},{9,8},{10,11... | collective-permute-start | bytes 491528 | tf_op jit(solution)/shard_map/ppermute | solution.py:210
  29.6 0.1 collective-permute-start.17
  29.6 0.4 %collective-permute-start.18 = (bf16[640,128]{1,0:T(8,128)(2,1)S(1)}, bf16[640,128]{1,0:T(8,128)(2,1)S(1)}, u32[]{:S(2)}, u32[]{:S(2)}) collective-permute-start(bf16[640,128]{1,0:T(8,128)(2,1)S(1)} %collective-permute-done.8.refs_13_), channel_id=1, source_target_pairs={{0,1},{1,0},{2,3},{3,2},{4,5},{5,4},{6,7},{7,6},{8,9},{9,8},{10,11... | collective-permute-start | bytes 491528 | tf_op jit(solution)/shard_map/ppermute | solution.py:210
  30.1 0.1 collective-permute-start.19
  30.8 0.8 %collective-permute-done.16.refs_17_ = bf16[640,128]{1,0:T(8,128)(2,1)S(1)} collective-permute-done((bf16[640,128]{1,0:T(8,128)(2,1)S(1)}, bf16[640,128]{1,0:T(8,128)(2,1)S(1)}, u32[]{:S(2)}, u32[]{:S(2)}) %collective-permute-start.16) | collective-permute-done | bytes 163872 | tf_op jit(solution)/shard_map/ppermute | solution.py:210
  31.6 0.2 collective-permute-done.17.refs_18_
  31.9 0.2 collective-permute-done.18.refs_19_
  32.1 0.2 collective-permute-done.19.refs_20_
  32.5 0.1 copy-done.16
  32.5 0.2 copy-done.17
  32.8 0.2 copy-done.18
  33.0 6.4 %shard_map.55 = f32[1,3,320,128]{3,2,1,0:T(8,128)} custom-call(s32[1,2,3]{2,1,0:T(2,128)S(1)} %bitcast.6, s32[1,3]{1,0:T(1,128)S(1)} %copy-done.2, s32[1]{0:T(128)S(6)} %copy.7.refs_2_, bf16[2,1,320,1280]{3,2,1,0:T(8,128)(2,1)S(1)} %copy-done, bf16[2,320,384]{2,1,0:T(8,128)(2,1)S(1)} %collective-permute-done.2.refs_4_, ...), custom_call_target="tpu_custom_call" | custom-call | flops 1258291200 | bytes 8388608 | tf_op jit(solution)/shard_map/pallas_call | solution.py:267
  (54 shorter events, 0.2 us)
Async XLA Ops:
  0.0 9.3 %copy-start = (bf16[2,1,320,1280]{3,2,1,0:T(8,128)(2,1)S(1)}, bf16[2,1,320,1280]{3,2,1,0:T(8,128)(2,1)}, u32[]{:S(2)}) copy-start(bf16[2,1,320,1280]{3,2,1,0:T(8,128)(2,1)} %refs_3_.1) | copy-start | bytes 4915204
  0.0 6.1 %collective-permute-start.3 = (bf16[320,128]{1,0:T(8,128)(2,1)}, bf16[320,128]{1,0:T(8,128)(2,1)S(1)}, u32[]{:S(2)}, u32[]{:S(2)}) collective-permute-start(bf16[320,128]{1,0:T(8,128)(2,1)} %bitcast.7), channel_id=1, source_target_pairs={{0,2},{1,3},{2,0},{3,1},{4,6},{5,7},{6,4},{7,5},{8,10},{9,11},{10,... | collective-permute-start | bytes 245768 | tf_op jit(solution)/shard_map/ppermute | solution.py:213
  2.9 1.5 %collective-permute-start = (bf16[320,128]{1,0:T(8,128)(2,1)}, bf16[320,128]{1,0:T(8,128)(2,1)S(1)}, u32[]{:S(2)}, u32[]{:S(2)}) collective-permute-start(bf16[320,128]{1,0:T(8,128)(2,1)} %bitcast.8), channel_id=1, source_target_pairs={{0,1},{1,0},{2,3},{3,2},{4,5},{5,4},{6,7},{7,6},{8,9},{9,8},{10,11... | collective-permute-start | bytes 245768 | tf_op jit(solution)/shard_map/ppermute | solution.py:210
  2.9 30.0 %copy-start.1 = (s32[1,3,2]{1,2,0:T(2,128)S(1)}, s32[1,3,2]{1,2,0:T(2,128)}, u32[]{:S(2)}) copy-start(s32[1,3,2]{1,2,0:T(2,128)} %param.7) | copy-start | bytes 76
  2.9 30.0 %copy-start.2 = (s32[1,3]{1,0:T(1,128)S(1)}, s32[1,3]{1,0:T(1,128)}, u32[]{:S(2)}) copy-start(s32[1,3]{1,0:T(1,128)} %refs_1_.1) | copy-start | bytes 40
  4.5 27.9 %copy-start.3 = (bf16[640,128]{1,0:T(8,128)(2,1)}, bf16[640,128]{1,0:T(8,128)(2,1)S(1)}, u32[]{:S(2)}) copy-start(bf16[640,128]{1,0:T(8,128)(2,1)S(1)} %pad_maximum_fusion.refs_7_) | copy-start | bytes 491524
  4.5 5.4 %collective-permute-start.1 = (bf16[640,128]{1,0:T(8,128)(2,1)S(1)}, bf16[640,128]{1,0:T(8,128)(2,1)S(1)}, u32[]{:S(2)}, u32[]{:S(2)}) collective-permute-start(bf16[640,128]{1,0:T(8,128)(2,1)S(1)} %pad_maximum_fusion.refs_7_), channel_id=1, source_target_pairs={{0,8},{1,5},{2,10},{3,7},{8,16},{9,1},{10,18},{11,3},{16,24},{17,9... | collective-permute-start | bytes 491528 | tf_op jit(solution)/shard_map/ppermute | solution.py:222
  6.1 1.5 %collective-permute-start.5 = (bf16[320,128]{1,0:T(8,128)(2,1)S(1)}, bf16[320,128]{1,0:T(8,128)(2,1)S(1)}, u32[]{:S(2)}, u32[]{:S(2)}) collective-permute-start(bf16[320,128]{1,0:T(8,128)(2,1)S(1)} %collective-permute-done.3), channel_id=1, source_target_pairs={{0,1},{1,0},{2,3},{3,2},{4,5},{5,4},{6,7},{7,6},{8,9},{9,8},{10,11... | collective-permute-start | bytes 245768 | tf_op jit(solution)/shard_map/ppermute | solution.py:210
  6.1 23.0 %collective-permute-start.4 = (bf16[2,320,640]{2,1,0:T(8,128)(2,1)S(1)}, bf16[2,320,640]{2,1,0:T(8,128)(2,1)S(1)}, u32[]{:S(2)}, u32[]{:S(2)}) collective-permute-start(bf16[2,320,640]{2,1,0:T(8,128)(2,1)S(1)} %dynamic-slice_bitcast_fusion), channel_id=1, source_target_pairs={{0,2},{1,3},{2,0},{3,1},{4,6},{5,7},{6,4},{7,5},{8,10},{9,11},{10,... | collective-permute-start | bytes 2457608 | tf_op jit(solution)/shard_map/ppermute | solution.py:213
  7.6 24.7 %copy-start.4 = (bf16[640,128]{1,0:T(8,128)(2,1)}, bf16[640,128]{1,0:T(8,128)(2,1)S(1)}, u32[]{:S(2)}) copy-start(bf16[640,128]{1,0:T(8,128)(2,1)S(1)} %constant_dynamic-update-slice_fusion.refs_8_) | copy-start | bytes 491524
  7.6 5.4 %collective-permute-start.7 = (bf16[640,128]{1,0:T(8,128)(2,1)S(1)}, bf16[640,128]{1,0:T(8,128)(2,1)S(1)}, u32[]{:S(2)}, u32[]{:S(2)}) collective-permute-start(bf16[640,128]{1,0:T(8,128)(2,1)S(1)} %constant_dynamic-update-slice_fusion.refs_8_), channel_id=1, source_target_pairs={{0,8},{1,5},{2,10},{3,7},{8,16},{9,1},{10,18},{11,3},{16,24},{17,9... | collective-permute-start | bytes 491528 | tf_op jit(solution)/shard_map/ppermute | solution.py:222
  9.8 22.5 %copy-start.5 = (bf16[640,128]{1,0:T(8,128)(2,1)}, bf16[640,128]{1,0:T(8,128)(2,1)S(1)}, u32[]{:S(2)}) copy-start(bf16[640,128]{1,0:T(8,128)(2,1)S(1)} %collective-permute-done.1.refs_9_) | copy-start | bytes 491524
  9.8 13.9 %collective-permute-start.2 = (bf16[2,320,384]{2,1,0:T(8,128)(2,1)S(1)}, bf16[2,320,384]{2,1,0:T(8,128)(2,1)S(1)}, u32[]{:S(2)}, u32[]{:S(2)}) collective-permute-start(bf16[2,320,384]{2,1,0:T(8,128)(2,1)S(1)} %dynamic-slice_bitcast_fusion.1), channel_id=1, source_target_pairs={{0,1},{1,0},{2,3},{3,2},{4,5},{5,4},{6,7},{7,6},{8,9},{9,8},{10,11... | collective-permute-start | bytes 1474568 | tf_op jit(solution)/shard_map/ppermute | solution.py:210
  9.8 5.3 %collective-permute-start.6 = (bf16[640,128]{1,0:T(8,128)(2,1)S(1)}, bf16[640,128]{1,0:T(8,128)(2,1)S(1)}, u32[]{:S(2)}, u32[]{:S(2)}) collective-permute-start(bf16[640,128]{1,0:T(8,128)(2,1)S(1)} %collective-permute-done.1.refs_9_), channel_id=1, source_target_pairs={{0,8},{1,5},{2,10},{3,7},{8,16},{9,1},{10,18},{11,3},{16,24},{17,9... | collective-permute-start | bytes 491528 | tf_op jit(solution)/shard_map/ppermute | solution.py:222
  13.0 19.3 %copy-start.6 = (bf16[640,128]{1,0:T(8,128)(2,1)}, bf16[640,128]{1,0:T(8,128)(2,1)S(1)}, u32[]{:S(2)}) copy-start(bf16[640,128]{1,0:T(8,128)(2,1)S(1)} %collective-permute-done.7.refs_10_) | copy-start | bytes 491524
  13.0 5.3 %collective-permute-start.9 = (bf16[640,128]{1,0:T(8,128)(2,1)S(1)}, bf16[640,128]{1,0:T(8,128)(2,1)S(1)}, u32[]{:S(2)}, u32[]{:S(2)}) collective-permute-start(bf16[640,128]{1,0:T(8,128)(2,1)S(1)} %collective-permute-done.7.refs_10_), channel_id=1, source_target_pairs={{0,8},{1,5},{2,10},{3,7},{8,16},{9,1},{10,18},{11,3},{16,24},{17,9... | collective-permute-start | bytes 491528 | tf_op jit(solution)/shard_map/ppermute | solution.py:222
  14.6 3.8 %collective-permute-start.10 = (bf16[640,128]{1,0:T(8,128)(2,1)S(1)}, bf16[640,128]{1,0:T(8,128)(2,1)S(1)}, u32[]{:S(2)}, u32[]{:S(2)}) collective-permute-start(bf16[640,128]{1,0:T(8,128)(2,1)S(1)} %collective-permute-done.7.refs_10_), channel_id=1, source_target_pairs={{0,1},{1,0},{2,3},{3,2},{4,5},{5,4},{6,7},{7,6},{8,9},{9,8},{10,11... | collective-permute-start | bytes 491528 | tf_op jit(solution)/shard_map/ppermute | solution.py:210
  15.2 17.2 %copy-start.7 = (bf16[640,128]{1,0:T(8,128)(2,1)}, bf16[640,128]{1,0:T(8,128)(2,1)S(1)}, u32[]{:S(2)}) copy-start(bf16[640,128]{1,0:T(8,128)(2,1)S(1)} %collective-permute-done.6.refs_11_) | copy-start | bytes 491524
  15.2 5.3 %collective-permute-start.8 = (bf16[640,128]{1,0:T(8,128)(2,1)S(1)}, bf16[640,128]{1,0:T(8,128)(2,1)S(1)}, u32[]{:S(2)}, u32[]{:S(2)}) collective-permute-start(bf16[640,128]{1,0:T(8,128)(2,1)S(1)} %collective-permute-done.6.refs_11_), channel_id=1, source_target_pairs={{0,8},{1,5},{2,10},{3,7},{8,16},{9,1},{10,18},{11,3},{16,24},{17,9... | collective-permute-start | bytes 491528 | tf_op jit(solution)/shard_map/ppermute | solution.py:222
  18.3 14.0 %copy-start.8 = (bf16[640,128]{1,0:T(8,128)(2,1)}, bf16[640,128]{1,0:T(8,128)(2,1)S(1)}, u32[]{:S(2)}) copy-start(bf16[640,128]{1,0:T(8,128)(2,1)S(1)} %collective-permute-done.9.refs_12_) | copy-start | bytes 491524
  18.3 3.7 %collective-permute-start.13 = (bf16[640,128]{1,0:T(8,128)(2,1)S(1)}, bf16[640,128]{1,0:T(8,128)(2,1)S(1)}, u32[]{:S(2)}, u32[]{:S(2)}) collective-permute-start(bf16[640,128]{1,0:T(8,128)(2,1)S(1)} %collective-permute-done.1.refs_9_), channel_id=1, source_target_pairs={{0,1},{1,0},{2,3},{3,2},{4,5},{5,4},{6,7},{7,6},{8,9},{9,8},{10,11... | collective-permute-start | bytes 491528 | tf_op jit(solution)/shard_map/ppermute | solution.py:210
  18.3 14.0 %copy-start.9 = (bf16[640,128]{1,0:T(8,128)(2,1)}, bf16[640,128]{1,0:T(8,128)(2,1)S(1)}, u32[]{:S(2)}) copy-start(bf16[640,128]{1,0:T(8,128)(2,1)S(1)} %collective-permute-done.10.refs_16_) | copy-start | bytes 491524
  18.4 5.4 %collective-permute-start.12 = (bf16[640,128]{1,0:T(8,128)(2,1)S(1)}, bf16[640,128]{1,0:T(8,128)(2,1)S(1)}, u32[]{:S(2)}, u32[]{:S(2)}) collective-permute-start(bf16[640,128]{1,0:T(8,128)(2,1)S(1)} %collective-permute-done.9.refs_12_), channel_id=1, source_target_pairs={{0,8},{1,5},{2,10},{3,7},{8,16},{9,1},{10,18},{11,3},{16,24},{17,9... | collective-permute-start | bytes 491528 | tf_op jit(solution)/shard_map/ppermute | solution.py:222
  20.5 11.9 %copy-start.10 = (bf16[640,128]{1,0:T(8,128)(2,1)}, bf16[640,128]{1,0:T(8,128)(2,1)S(1)}, u32[]{:S(2)}) copy-start(bf16[640,128]{1,0:T(8,128)(2,1)S(1)} %collective-permute-done.8.refs_13_) | copy-start | bytes 491524
  20.5 5.3 %collective-permute-start.11 = (bf16[640,128]{1,0:T(8,128)(2,1)S(1)}, bf16[640,128]{1,0:T(8,128)(2,1)S(1)}, u32[]{:S(2)}, u32[]{:S(2)}) collective-permute-start(bf16[640,128]{1,0:T(8,128)(2,1)S(1)} %collective-permute-done.8.refs_13_), channel_id=1, source_target_pairs={{0,8},{1,5},{2,10},{3,7},{8,16},{9,1},{10,18},{11,3},{16,24},{17,9... | collective-permute-start | bytes 491528 | tf_op jit(solution)/shard_map/ppermute | solution.py:222
  22.1 10.4 %copy-start.11 = (bf16[640,128]{1,0:T(8,128)(2,1)}, bf16[640,128]{1,0:T(8,128)(2,1)S(1)}, u32[]{:S(2)}) copy-start(bf16[640,128]{1,0:T(8,128)(2,1)S(1)} %collective-permute-done.13.refs_15_) | copy-start | bytes 491524
  23.7 5.3 %collective-permute-start.14 = (bf16[640,128]{1,0:T(8,128)(2,1)S(1)}, bf16[640,128]{1,0:T(8,128)(2,1)S(1)}, u32[]{:S(2)}, u32[]{:S(2)}) collective-permute-start(bf16[640,128]{1,0:T(8,128)(2,1)S(1)} %collective-permute-done.12.refs_14_), channel_id=1, source_target_pairs={{0,8},{1,5},{2,10},{3,7},{8,16},{9,1},{10,18},{11,3},{16,24},{17,9... | collective-permute-start | bytes 491528 | tf_op jit(solution)/shard_map/ppermute | solution.py:222
  29.1 3.3 %collective-permute-start.15 = (bf16[2,320,640]{2,1,0:T(8,128)(2,1)S(1)}, bf16[2,320,640]{2,1,0:T(8,128)(2,1)S(1)}, u32[]{:S(2)}, u32[]{:S(2)}) collective-permute-start(bf16[2,320,640]{2,1,0:T(8,128)(2,1)S(1)} %collective-permute-done.4.refs_5_), channel_id=1, source_target_pairs={{0,1},{1,0},{2,3},{3,2},{4,5},{5,4},{6,7},{7,6},{8,9},{9,8},{10,11... | collective-permute-start | bytes 2457608 | tf_op jit(solution)/shard_map/ppermute | solution.py:210
  29.1 2.6 %collective-permute-start.16 = (bf16[640,128]{1,0:T(8,128)(2,1)S(1)}, bf16[640,128]{1,0:T(8,128)(2,1)S(1)}, u32[]{:S(2)}, u32[]{:S(2)}) collective-permute-start(bf16[640,128]{1,0:T(8,128)(2,1)S(1)} %collective-permute-done.6.refs_11_), channel_id=1, source_target_pairs={{0,1},{1,0},{2,3},{3,2},{4,5},{5,4},{6,7},{7,6},{8,9},{9,8},{10,11... | collective-permute-start | bytes 491528 | tf_op jit(solution)/shard_map/ppermute | solution.py:210
  29.6 2.3 %collective-permute-start.17 = (bf16[640,128]{1,0:T(8,128)(2,1)S(1)}, bf16[640,128]{1,0:T(8,128)(2,1)S(1)}, u32[]{:S(2)}, u32[]{:S(2)}) collective-permute-start(bf16[640,128]{1,0:T(8,128)(2,1)S(1)} %collective-permute-done.9.refs_12_), channel_id=1, source_target_pairs={{0,1},{1,0},{2,3},{3,2},{4,5},{5,4},{6,7},{7,6},{8,9},{9,8},{10,11... | collective-permute-start | bytes 491528 | tf_op jit(solution)/shard_map/ppermute | solution.py:210
  29.6 2.5 %collective-permute-start.18 = (bf16[640,128]{1,0:T(8,128)(2,1)S(1)}, bf16[640,128]{1,0:T(8,128)(2,1)S(1)}, u32[]{:S(2)}, u32[]{:S(2)}) collective-permute-start(bf16[640,128]{1,0:T(8,128)(2,1)S(1)} %collective-permute-done.8.refs_13_), channel_id=1, source_target_pairs={{0,1},{1,0},{2,3},{3,2},{4,5},{5,4},{6,7},{7,6},{8,9},{9,8},{10,11... | collective-permute-start | bytes 491528 | tf_op jit(solution)/shard_map/ppermute | solution.py:210
  30.1 2.2 %collective-permute-start.19 = (bf16[640,128]{1,0:T(8,128)(2,1)S(1)}, bf16[640,128]{1,0:T(8,128)(2,1)S(1)}, u32[]{:S(2)}, u32[]{:S(2)}) collective-permute-start(bf16[640,128]{1,0:T(8,128)(2,1)S(1)} %collective-permute-done.12.refs_14_), channel_id=1, source_target_pairs={{0,1},{1,0},{2,3},{3,2},{4,5},{5,4},{6,7},{7,6},{8,9},{9,8},{10,11... | collective-permute-start | bytes 491528 | tf_op jit(solution)/shard_map/ppermute | solution.py:210
  (8 other events, 26.0 us)
